TPU v7x, 256 devices: a whole 4x4x8 slice. The times are simulated.
256 devices in a mesh: row: 32 (over y, x, core), col: 8 (over z).
Axes of the slice: x: 4, y: 4, z: 8, core: 2. Of those that a mesh axis runs over, the one named last changes fastest.
Arguments:
- alignment_matrix: bfloat16 [128, 2048, 256], P(None, ('row', 'col')), may hold values from -70 to 70, as said below
- standardize_factor: float32 [256], replicated, may hold values from 0.4 to 1.6
- standardize_shift: float32 [256], replicated, may hold values from -3 to 3
- first_map_matrix: bfloat16 [256, 32], replicated, may hold values from -0.375 to 0.375
- first_map_offset: float32 [32], replicated, may hold values from -3 to 3
- second_map_matrix: bfloat16 [256, 32], replicated, may hold values from -0.375 to 0.375
- second_map_offset: float32 [32], replicated, may hold values from -3 to 3
- couple_map_matrix: bfloat16 [1024, 128], replicated, may hold values from -1.5 to 1.5
- couple_map_offset: float32 [128], replicated, may hold values from -3 to 3
Outputs:
- pair_update: bfloat16 [2048, 2048, 128], P(('row', 'col'))
Inputs may be any that keep to these rules, and one draw needn't show every extreme that they name: `alignment_matrix`: MSA features.
All inputs are finite; a program needn't handle non-finite values.
Results may differ from a plain program's by a relative error of at most 0.0051.
Values may be sent and summed in bfloat16 or wider, within the bound.
No kernel may reach another device: no remote copies, remote signals or barrier semaphores. Data moves between devices by JAX's collectives and lax.ppermute only.
A program may use at most 128 MiB of HBM per device.

v0:
```python
import math

import jax
import jax.numpy as jnp
from jax import lax
from jax.sharding import PartitionSpec as P


def standardize_rows(alignment_matrix, standardize_factor, standardize_shift):
    element_list = alignment_matrix.astype(jnp.float32)
    mean = jnp.mean(element_list, axis=-1, keepdims=True)
    centered = element_list - mean
    variance = jnp.mean(centered * centered, axis=-1, keepdims=True)
    return (centered * lax.rsqrt(variance + 1e-05) * standardize_factor + standardize_shift).astype(
        jnp.bfloat16
    )


def project(standardized_alignment, weight, bias):
    return (
        jnp.einsum(
            "srm,mc->src", standardized_alignment, weight, preferred_element_type=jnp.float32
        )
        + bias
    ).astype(jnp.bfloat16)


def pair_block(left_rows, piece, couple_map_matrix, couple_map_offset):
    seqs = left_rows.shape[0]
    width = piece.shape[1]
    block = math.gcd(width, 128)
    count = width // block
    parts = jnp.moveaxis(piece.reshape(seqs, count, block, piece.shape[2]), 1, 0)

    def one_part(right_part):
        outer = (
            jnp.einsum("sic,sje->ijce", left_rows, right_part, preferred_element_type=jnp.float32)
            / seqs
        )
        outer = outer.astype(jnp.bfloat16)
        outer = outer.reshape(outer.shape[0], block, -1)
        return (
            jnp.einsum("ijk,kf->ijf", outer, couple_map_matrix, preferred_element_type=jnp.float32)
            + couple_map_offset
        ).astype(jnp.bfloat16)

    result = lax.map(one_part, parts)
    return jnp.moveaxis(result, 0, 1).reshape(left_rows.shape[1], width, couple_map_matrix.shape[1])


def per_device(
    alignment_matrix,
    standardize_factor,
    standardize_shift,
    first_map_matrix,
    first_map_offset,
    second_map_matrix,
    second_map_offset,
    couple_map_matrix,
    couple_map_offset,
):
    standardized_alignment = standardize_rows(
        alignment_matrix, standardize_factor, standardize_shift
    )
    left = project(standardized_alignment, first_map_matrix, first_map_offset)
    right = project(standardized_alignment, second_map_matrix, second_map_offset)
    return pair_block(
        left,
        lax.all_gather(right, ("row", "col"), axis=1, tiled=True),
        couple_map_matrix,
        couple_map_offset,
    )


def solution(mesh):
    return jax.shard_map(
        per_device,
        mesh=mesh,
        in_specs=(P(None, ("row", "col"), None), P(), P(), P(), P(), P(), P(), P(), P()),
        out_specs=P(("row", "col"), None, None),
        check_vma=False,
    )
```

profile of v0, /device:TPU:1, one launch (start us, length us, event | category | flops | bytes accessed | tf_op | source)
XLA Modules:
  0.0 254.5 jit_solution(6899660916147554961)
XLA Ops:
  9.4 1.5 fusion.17
  13.2 128.5 %all-gather.2.cloned.1.call-done = bf16[128,2048,32]{0,2,1:T(8,128)(2,1)} async-done(((bf16[128,8,32]{0,2,1:T(8,128)(2,1)}), bf16[128,2048,32]{0,2,1:T(8,128)(2,1)}) %all-gather.2.cloned.1.call-update) | async-done | bytes 16777232 | tf_op jit(solution)/shard_map/all_gather | solution.py:69
  141.7 25.0 %copy.29 = bf16[128,16,128,32]{2,0,3,1:T(8,128)(2,1)} copy(bf16[128,16,128,32]{0,3,2,1:T(8,128)(2,1)} %bitcast.46) | data formatting | bytes 33554432 | tf_op jit(solution)/shard_map/reshape | solution.py:33
  166.8 76.1 %while.10 = (s32[]{:T(128)}, bf16[16,8,128,128]{3,2,1,0:T(8,128)(2,1)}, bf16[16,128,128,32]{2,1,3,0:T(8,128)(2,1)}, bf16[128,8,32]{0,2,1:T(8,128)(2,1)S(1)}, bf1...) while((s32[]{:T(128)}, bf16[16,8,128,128]{3,2,1,0:T(8,128)(2,1)}, ...), condition=%wide.region_3.4_spmd, body=%wide.region_2.3_spmd.sunk | while | flops 539230208 | bytes 10027613 | solution.py:47
  166.8 1.9 fusion.32
  171.5 1.9 fusion.32
  174.8 1.5 fusion.33
  176.3 1.9 fusion.32
  179.5 1.5 fusion.33
  181.0 1.9 fusion.32
  184.3 1.5 fusion.33
  185.8 1.9 fusion.32
  189.1 1.5 fusion.33
  190.5 1.9 fusion.32
  193.8 1.5 fusion.33
  195.3 1.9 fusion.32
  200.0 1.9 fusion.32
  204.8 1.9 fusion.32
  208.1 1.5 fusion.33
  209.6 1.9 fusion.32
  212.8 1.5 fusion.33
  214.3 1.9 fusion.32
  217.6 1.5 fusion.33
  219.1 1.9 fusion.32
  223.8 1.9 fusion.32
  227.1 1.5 fusion.33
  228.6 1.9 fusion.32
  233.3 1.9 fusion.32
  236.6 1.5 fusion.33
  238.1 1.9 fusion.32
  241.4 1.5 fusion.33
  242.8 4.8 %copy.31 = bf16[8,16,128,128]{3,2,1,0:T(8,128)(2,1)} copy(bf16[8,16,128,128]{3,2,0,1:T(8,128)(2,1)} %bitcast.47) | data formatting | bytes 8388608 | tf_op jit(solution)/shard_map/transpose | solution.py:48
  (48 shorter events, 34.0 us)
Async XLA Ops:
  6.5 2.8 %copy-start = (bf16[256,32]{0,1:T(8,128)(2,1)S(1)}, bf16[256,32]{0,1:T(8,128)(2,1)}, u32[]{:S(2)}) copy-start(bf16[256,32]{0,1:T(8,128)(2,1)} %param.16) | copy-start | bytes 49156
  6.5 6.0 %copy-start.1 = (bf16[128,8,256]{2,1,0:T(8,128)(2,1)S(1)}, bf16[128,8,256]{2,1,0:T(8,128)(2,1)}, u32[]{:S(2)}) copy-start(bf16[128,8,256]{2,1,0:T(8,128)(2,1)} %param.11) | copy-start | bytes 1572868
  6.5 6.0 %copy-start.4 = (f32[256]{0:T(256)S(1)}, f32[256]{0:T(256)}, u32[]{:S(2)}) copy-start(f32[256]{0:T(256)} %param.13) | copy-start | bytes 3076
  6.5 6.0 %copy-start.5 = (f32[256]{0:T(256)S(1)}, f32[256]{0:T(256)}, u32[]{:S(2)}) copy-start(f32[256]{0:T(256)} %param.12) | copy-start | bytes 3076
  6.5 6.0 %copy-start.6 = (f32[32]{0:T(128)S(1)}, f32[32]{0:T(128)}, u32[]{:S(2)}) copy-start(f32[32]{0:T(128)} %param.15) | copy-start | bytes 388
  6.5 6.0 %copy-start.3 = (bf16[256,32]{0,1:T(8,128)(2,1)S(1)}, bf16[256,32]{0,1:T(8,128)(2,1)}, u32[]{:S(2)}) copy-start(bf16[256,32]{0,1:T(8,128)(2,1)} %param.14) | copy-start | bytes 49156
  6.6 135.2 %all-gather.2.cloned.1.call-start = ((), (), s32[]{:S(2)}) async-start(), calls=%async_computation | async-start | bytes 16842752 | tf_op jit(solution)/shard_map/all_gather | solution.py:69
  141.7 25.0 %copy-start.2 = (bf16[1024,128]{1,0:T(8,128)(2,1)S(1)}, bf16[1024,128]{1,0:T(8,128)(2,1)}, u32[]{:S(2)}) copy-start(bf16[1024,128]{1,0:T(8,128)(2,1)} %param.18) | copy-start | bytes 786436
  141.7 25.0 %copy-start.7 = (f32[128]{0:T(128)S(1)}, f32[128]{0:T(128)}, u32[]{:S(2)}) copy-start(f32[128]{0:T(128)} %param.19) | copy-start | bytes 1540
Sparse Core Ops, SparseCore 0:
  12.6 129.0 all-gather.1
where the time goes:
time: 256 us; the launch traced here: 254 us
  waiting for transfers between devices  129 us (50%)
  matrix products  56.1 us (22%)
  local copies, waits for them, and re-layouts  51.9 us (20%)
  between operations  13.5 us (5%)
  other arithmetic  4.12 us (2%)
    all_gather x1, waiting for transfers between devices, per_device(): lax.all_gather(right, ('row', 'col'), axis=1, tiled=True)  129 us
    dot_general x16, matrix products, one_part(): jnp.einsum('sic,sje->ijce', left_rows, right_part, preferred_element_type...  30.7 us
    reshape x1, local copies, waits for them, and re-layouts, pair_block(): piece.reshape(seqs, count, block, piece.shape[2])  25 us
    dot_general x16, matrix products, one_part(): jnp.einsum('ijk,kf->ijf', outer, couple_map_matrix, preferred_element_typ...  23.5 us
    convert_element_type x16, local copies, waits for them, and re-layouts, one_part(): outer = outer.astype(jnp.bfloat16)  21.7 us
  transfers between devices with their start and end apart: 1, of which 1 were waited for; matrix products, arithmetic and copies ran while one was open for 0% of the time, Pallas kernels for 0%

commit v1 on v0

v1 whole, which is shorter than its diff:
```python
import functools

import jax
import jax.numpy as jnp
from jax import lax
from jax.experimental import pallas as pl
from jax.experimental.pallas import tpu as pltpu
from jax.sharding import Mesh, PartitionSpec as P

SIZES = {"y": 4, "x": 4, "c": 2, "z": 8}
S, CM, CH, CZ, LOCAL, UNITS = 128, 256, 32, 128, 8, 128
PARTS = ((0, 12), (12, 22), (22, 32))
VMEM_LIMIT = 56 * 1024 * 1024


def project_kernel(msa_ref, gain_ref, shift_ref, w1_ref, b1_ref, w2_ref, b2_ref, ra_ref, rb_ref, rc_ref, lt_ref,
                   w_s, y_s, r_s):
    x = msa_ref[...].astype(jnp.float32).reshape(S * LOCAL, CM)
    mean = jnp.mean(x, axis=-1, keepdims=True)
    centered = x - mean
    variance = jnp.mean(centered * centered, axis=-1, keepdims=True)
    normed = (centered * lax.rsqrt(variance + 1e-05) * gain_ref[...] + shift_ref[...]).astype(jnp.bfloat16)
    w_s[:, 0:CH] = w1_ref[...]
    w_s[:, CH:2 * CH] = w2_ref[...]
    y = jnp.dot(normed, w_s[...], preferred_element_type=jnp.float32)
    bias = jnp.concatenate([b1_ref[...], b2_ref[...]], axis=1)
    y_s[:, 0:2 * CH] = (y + bias).astype(jnp.bfloat16).astype(jnp.float32)
    for j in range(LOCAL):
        t = y_s[pl.ds(j, S, stride=LOCAL), :].T
        lt_ref[j * CH:(j + 1) * CH, :] = t[0:CH].astype(jnp.bfloat16)
        r_s[j * CH:(j + 1) * CH, :] = t[CH:2 * CH]
    for (lo, hi), ref in zip(PARTS, (ra_ref, rb_ref, rc_ref)):
        for e in range(lo, hi):
            ref[:, (e - lo) * S:(e - lo + 1) * S] = r_s[pl.ds(e, LOCAL, stride=CH), :].astype(jnp.bfloat16)


def project(msa, gain, shift, w1, b1, w2, b2):
    widths = [(hi - lo) * S for lo, hi in PARTS]
    return pl.pallas_call(
        project_kernel,
        out_shape=[jax.ShapeDtypeStruct((LOCAL, k), jnp.bfloat16) for k in widths]
        + [jax.ShapeDtypeStruct((LOCAL * CH, S), jnp.bfloat16)],
        scratch_shapes=[
            pltpu.VMEM((CM, 2 * CH), jnp.bfloat16),
            pltpu.VMEM((S * LOCAL, S), jnp.float32),
            pltpu.VMEM((LOCAL * CH, S), jnp.float32),
        ],
        compiler_params=pltpu.CompilerParams(vmem_limit_bytes=VMEM_LIMIT),
        name="project",
    )(msa, gain.reshape(1, CM), shift.reshape(1, CM), w1, b1.reshape(1, CH), w2, b2.reshape(1, CH))


def couple_kernel(lt_ref, w_ref, t_ref):
    for i in range(2):
        t = lax.dot_general(lt_ref[i * CH:(i + 1) * CH, :], w_ref[...], (((0,), (0,)), ((), ())),
                            preferred_element_type=jnp.float32)
        t = (t * (1.0 / S)).astype(jnp.bfloat16)
        for e in range(CH):
            t_ref[0, e * S:(e + 1) * S, i * CZ:(i + 1) * CZ] = t[:, e * CZ:(e + 1) * CZ]


def couple(lt, w):
    return pl.pallas_call(
        couple_kernel,
        grid=(LOCAL // 2,),
        in_specs=[
            pl.BlockSpec((2 * CH, S), lambda n: (n, 0)),
            pl.BlockSpec((CH, CH * CZ), lambda n: (0, 0)),
        ],
        out_specs=pl.BlockSpec((1, CH * S, 2 * CZ), lambda n: (n, 0, 0)),
        out_shape=jax.ShapeDtypeStruct((LOCAL // 2, CH * S, 2 * CZ), jnp.bfloat16),
        compiler_params=pltpu.CompilerParams(vmem_limit_bytes=VMEM_LIMIT),
        cost_estimate=pl.CostEstimate(flops=2 * LOCAL * S * CH * CH * CZ, bytes_accessed=8 << 20, transcendentals=0),
        name="couple",
    )(lt, w)


def place4(own, core, t):
    rel = jnp.where((own + core) % 2 == 0, t - own, own - t) & 3
    return rel ^ (rel >> 1)


def place8(own, core, t):
    rel = jnp.where((own + core) % 2 == 0, t - own, own - t) & 7
    half, low = rel >> 1, rel & 1
    return jnp.where(half == 0, low, jnp.where(half == 1, 4 + low, jnp.where(half == 2, 7 - low, 3 - low)))


def pair_kernel(at_ref, ra_ref, rb_ref, rc_ref, t_ref, bias_ref, o_ref, sa, sb, sc):
    for (lo, hi), r_ref, s_ref in zip(PARTS, (ra_ref, rb_ref, rc_ref), (sa, sb, sc)):
        s_ref[...] = jnp.dot(r_ref[...], t_ref[0, lo * S:hi * S, :], preferred_element_type=jnp.float32)
    c, y, x, z = at_ref[0], at_ref[1], at_ref[2], at_ref[3]
    bias = jnp.concatenate([bias_ref[...], bias_ref[...]], axis=1)
    px = [place4(x, c, t) for t in range(4)]
    py = [place4(y, c, t) for t in range(4)]
    pz = [place8(z, c, t) for t in range(8)]

    def rows(ref, unit):
        return ref[pl.ds(pl.multiple_of(unit * LOCAL, LOCAL), LOCAL), :]

    for ty in range(4):
        for tx in range(4):
            for tz in range(8):
                value = (
                    rows(sa, (tz * 4 + py[ty]) * 4 + px[tx])
                    + rows(sb, (px[tx] * 8 + pz[tz]) * 4 + py[ty])
                    + rows(sc, (py[ty] * 4 + px[tx]) * 8 + pz[tz])
                    + bias
                ).astype(jnp.bfloat16)
                for i in range(2):
                    o_ref[i, ty * 4 + tx, 0, tz * LOCAL:(tz + 1) * LOCAL, :] = value[:, i * CZ:(i + 1) * CZ]


def pair(at, ra, rb, rc, t, bias, whole):
    widths = [(hi - lo) * S for lo, hi in PARTS]
    return pl.pallas_call(
        pair_kernel,
        grid_spec=pltpu.PrefetchScalarGridSpec(
            num_scalar_prefetch=1,
            grid=(LOCAL // 2,),
            in_specs=[pl.BlockSpec((UNITS * LOCAL, k), lambda n, at: (0, 0)) for k in widths]
            + [
                pl.BlockSpec((1, CH * S, 2 * CZ), lambda n, at: (n, 0, 0)),
                pl.BlockSpec((1, CZ), lambda n, at: (0, 0)),
            ],
            out_specs=pl.BlockSpec((2, 16, 1, 64, CZ), lambda n, at: (n, 0, at[0] if whole else 0, 0, 0)),
            scratch_shapes=[pltpu.VMEM((UNITS * LOCAL, 2 * CZ), jnp.float32)] * 3,
        ),
        out_shape=jax.ShapeDtypeStruct((LOCAL, 16, 2 if whole else 1, 64, CZ), jnp.bfloat16),
        compiler_params=pltpu.CompilerParams(vmem_limit_bytes=VMEM_LIMIT),
        cost_estimate=pl.CostEstimate(flops=2 * 1024 * 4096 * 1024, bytes_accessed=16 << 20, transcendentals=0),
        name="pair",
    )(at, ra, rb, rc, t, bias.reshape(1, CZ))


def exchange(v, axis, step):
    n, pairs = SIZES[axis], []
    for core in range(2):
        even_up = (step % 2 == 0) == (core == 0)
        for i in range(n):
            partner = (i + 1 if (i % 2 == 0) == even_up else i - 1) % n
            flat = (lambda k: core * n + k) if axis == "z" else (lambda k: k * 2 + core)
            pairs.append((flat(i), flat(partner)))
    return lax.ppermute(v, ("c", "z") if axis == "z" else (axis, "c"), pairs)


def gather(v, axis):
    first = exchange(v, axis, 0)
    held = [jnp.concatenate([v, first], axis=0)]
    for step in range(1, SIZES[axis] // 2):
        held.append(exchange(held[-1], axis, step))
    return jnp.concatenate(held, axis=0)


def gather_last(v, axis):
    first = exchange(v, axis, 0)
    second = exchange(v, axis, 1)
    third = exchange(first, axis, 1)
    return jnp.concatenate([v, first, second, third], axis=0)


def per_device(msa, gain, shift, w1, b1, w2, b2, couple_map, couple_offset):
    core = lax.axis_index("c")
    at = jnp.stack([core, lax.axis_index("y"), lax.axis_index("x"), lax.axis_index("z")]).astype(jnp.int32)
    ra, rb, rc, lt = project(msa, gain, shift, w1, b1, w2, b2)
    other = [(0, 1), (1, 0)]
    lt_other = lax.ppermute(lt, "c", other)
    w = couple_map.reshape(CH, CH * CZ)

    ra = gather(gather(ra, "x"), "y")
    rb = gather(gather(rb, "y"), "z")
    rc = gather(gather(rc, "z"), "x")
    ra = lax.all_gather(ra, "z", axis=0, tiled=True)
    rb = gather_last(rb, "x")
    rc = gather_last(rc, "y")

    theirs = pair(at, ra, rb, rc, couple(lt_other, w), couple_offset, False)
    got = lax.ppermute(theirs, "c", other)
    mine = pair(at, ra, rb, rc, couple(lt, w), couple_offset, True)
    out = lax.dynamic_update_slice(mine, got, (0, 0, 1 - core, 0, 0))
    return out.reshape(LOCAL, 16 * 2 * 64, CZ)


def solution(mesh):
    fine = Mesh(mesh.devices.reshape(4, 4, 2, 8), ("y", "x", "c", "z"))
    rows = ("y", "x", "c", "z")
    return jax.shard_map(
        per_device,
        mesh=fine,
        in_specs=(P(None, rows, None), P(), P(), P(), P(), P(), P(), P(), P()),
        out_specs=P(rows, None, None),
        check_vma=False,
    )
```

time: 256 us -> 177 us (0.69)
  waiting for transfers between devices: 129 us -> 52.9 us
  matrix products: 56.1 us -> 0 us
  Pallas kernels: 0 us -> 47.9 us
  starting transfers between devices: 0.04 us -> 36.9 us
  local copies, waits for them, and re-layouts: 51.9 us -> 20.1 us
    all_gather x1, waiting for transfers between devices: 129 us -> 0.01 us  [per_device(): ra = lax.all_gather(ra, 'z', axis=0, tiled=True)]
    dot_general x34 -> x0, matrix products: 56.1 us -> none  [the longest x16 30.7 us: one_part(): jnp.einsum('sic,sje->ijce', left_rows, right_part, preferred_element_type...]
    ppermute x0 -> x24, waiting for transfers between devices: none -> 52.9 us  [the longest x22 52.9 us: exchange(): return lax.ppermute(v, ('c', 'z') if axis == 'z' else (axis, 'c'), pairs)]
    pallas_call x0 -> x5, Pallas kernels: none -> 47.9 us  [the longest x2 33.2 us: pair(): pl.pallas_call(pair_kernel, grid_spec=pltpu.PrefetchScalarGridSpec(num_sc...]
    ppermute x0 -> x24, starting transfers between devices: none -> 36.9 us  [the longest x22 20.2 us: exchange(): return lax.ppermute(v, ('c', 'z') if axis == 'z' else (axis, 'c'), pairs)]
    reshape x1, local copies, waits for them, and re-layouts: 25 us -> 0.83 us  [per_device(): w = couple_map.reshape(CH, CH * CZ)]
    convert_element_type x16 -> x0, local copies, waits for them, and re-layouts: 21.7 us -> none  [one_part(): outer = outer.astype(jnp.bfloat16)]
    unnamed x16 -> x35, local copies, waits for them, and re-layouts: 0.03 us -> 14.8 us
  transfers between devices with their start and end apart: 1 -> 25, of which waited for: 1 -> 13; matrix products, arithmetic and copies ran while one was open for 0% -> 11% of each run, Pallas kernels for 0% -> 16%
where the time goes in v1:
time: 177 us; the launch traced here: 176 us
  waiting for transfers between devices  52.9 us (30%)
  Pallas kernels  47.9 us (27%)
  starting transfers between devices  36.9 us (21%)
  local copies, waits for them, and re-layouts  20.1 us (11%)
  between operations  13.6 us (8%)
  other arithmetic  5.1 us (3%)
    ppermute x22, waiting for transfers between devices, exchange(): return lax.ppermute(v, ('c', 'z') if axis == 'z' else (axis, 'c'), pairs)  52.9 us
    pallas_call x2, Pallas kernels, pair(): pl.pallas_call(pair_kernel, grid_spec=pltpu.PrefetchScalarGridSpec(num_sc...  33.2 us
    ppermute x22, starting transfers between devices, exchange(): return lax.ppermute(v, ('c', 'z') if axis == 'z' else (axis, 'c'), pairs)  20.2 us
    unnamed x35, local copies, waits for them, and re-layouts  14.8 us
    ppermute x1, starting transfers between devices, per_device(): lt_other = lax.ppermute(lt, 'c', other)  14.6 us
    pallas_call x2, Pallas kernels, couple(): pl.pallas_call(couple_kernel, grid=(LOCAL // 2,), in_specs=[pl.BlockSpec(...  12 us
  transfers between devices with their start and end apart: 25, of which 13 were waited for; matrix products, arithmetic and copies ran while one was open for 11% of the time, Pallas kernels for 16%

profile of v1, /device:TPU:1, one launch (start us, length us, event | category | flops | bytes accessed | tf_op | source)
XLA Modules:
  0.0 176.5 jit_solution(9043920344751127000)
XLA Ops:
  6.5 1.4 copy.10.w1_ref
  8.0 1.4 copy.11.w2_ref
  9.4 2.7 %project.1 = (bf16[8,1536]{1,0:T(8,128)(2,1)}, bf16[8,1280]{1,0:T(8,128)(2,1)}, bf16[8,1280]{1,0:T(8,128)(2,1)}, bf16[256,128]{1,0:T(8,128)(2,1)}) custom-call(bf16[128,8,256]{2,1,0:T(8,128)(2,1)} %msa_ref.1, f32[1,256]{1,0:T(1,128)} %bitcast.10, f32[1,256]{1,0:T(1,128)} %bitcast.11, bf16[256,32]{1,0:T(8,128)(2,1)} %copy.10.w1_ref, f32[1,32]{1,0:T(1,128)} %bitcast.12, ...), custom_call_target="tpu_custom_call" | custom-call | tf_op jit(solution)/shard_map/project/pallas_call | solution.py:39
  12.2 6.4 %collective-permute-start.13 = (bf16[8,1280]{1,0:T(8,128)(2,1)}, bf16[8,1280]{1,0:T(8,128)(2,1)S(1)}, u32[]{:S(2)}, u32[]{:S(2)}) collective-permute-start(bf16[8,1280]{1,0:T(8,128)(2,1)} %get-tuple-element.11), channel_id=1, source_target_pairs={{0,1},{1,0},{2,3},{3,2},{4,5},{5,4},{6,7},{7,6},{8,15},{9,10},{10,... | collective-permute-start | bytes 61448 | tf_op jit(solution)/shard_map/ppermute | solution.py:144
  18.6 2.7 %collective-permute-start.4 = (bf16[8,1280]{1,0:T(8,128)(2,1)}, bf16[8,1280]{1,0:T(8,128)(2,1)S(1)}, u32[]{:S(2)}, u32[]{:S(2)}) collective-permute-start(bf16[8,1280]{1,0:T(8,128)(2,1)} %get-tuple-element.10), channel_id=1, source_target_pairs={{0,64},{64,0},{128,192},{192,128},{8,200},{72,136},{136,72},{200,8... | collective-permute-start | bytes 61448 | tf_op jit(solution)/shard_map/ppermute | solution.py:144
  21.3 2.5 %collective-permute-start = (bf16[8,1536]{1,0:T(8,128)(2,1)}, bf16[8,1536]{1,0:T(8,128)(2,1)S(1)}, u32[]{:S(2)}, u32[]{:S(2)}) collective-permute-start(bf16[8,1536]{1,0:T(8,128)(2,1)} %get-tuple-element.9), channel_id=1, source_target_pairs={{0,16},{16,0},{32,48},{48,32},{8,56},{24,40},{40,24},{56,8},{1,17}... | collective-permute-start | bytes 73736 | tf_op jit(solution)/shard_map/ppermute | solution.py:144
  23.8 1.4 constant_dynamic-update-slice_fusion.11
  26.6 2.9 %collective-permute-done.1 = bf16[16,1536]{1,0:T(8,128)(2,1)S(1)} collective-permute-done((bf16[16,1536]{1,0:T(8,128)(2,1)S(1)}, bf16[16,1536]{1,0:T(8,128)(2,1)S(1)}, u32[]{:S(2)}, u32[]{:S(2)}) %collective-permute-start.1) | collective-permute-done | bytes 49184 | tf_op jit(solution)/shard_map/ppermute | solution.py:144
  30.3 4.7 %collective-permute-done.2 = bf16[32,1536]{1,0:T(8,128)(2,1)S(1)} collective-permute-done((bf16[32,1536]{1,0:T(8,128)(2,1)S(1)}, bf16[32,1536]{1,0:T(8,128)(2,1)S(1)}, u32[]{:S(2)}, u32[]{:S(2)}) %collective-permute-start.2) | collective-permute-done | bytes 98336 | tf_op jit(solution)/shard_map/ppermute | solution.py:144
  35.9 4.5 %collective-permute-done.3 = bf16[64,1536]{1,0:T(8,128)(2,1)S(1)} collective-permute-done((bf16[64,1536]{1,0:T(8,128)(2,1)S(1)}, bf16[64,1536]{1,0:T(8,128)(2,1)S(1)}, u32[]{:S(2)}, u32[]{:S(2)}) %collective-permute-start.3) | collective-permute-done | bytes 196640 | tf_op jit(solution)/shard_map/ppermute | solution.py:144
  43.8 1.6 collective-permute-done.5
  46.2 1.4 collective-permute-start.6
  47.7 1.2 collective-permute-start.15
  50.1 1.9 %collective-permute-done.15 = bf16[16,1280]{1,0:T(8,128)(2,1)S(1)} collective-permute-done((bf16[16,1280]{1,0:T(8,128)(2,1)S(1)}, bf16[16,1280]{1,0:T(8,128)(2,1)S(1)}, u32[]{:S(2)}, u32[]{:S(2)}) %collective-permute-start.15) | collective-permute-done | bytes 40992 | tf_op jit(solution)/shard_map/ppermute | solution.py:144
  52.7 2.2 %collective-permute-done.16 = bf16[16,1280]{1,0:T(8,128)(2,1)S(1)} collective-permute-done((bf16[16,1280]{1,0:T(8,128)(2,1)S(1)}, bf16[16,1280]{1,0:T(8,128)(2,1)S(1)}, u32[]{:S(2)}, u32[]{:S(2)}) %collective-permute-start.16) | collective-permute-done | bytes 40992 | tf_op jit(solution)/shard_map/ppermute | solution.py:144
  55.5 1.7 collective-permute-start.17
  58.0 3.3 %collective-permute-done.17 = bf16[64,1280]{1,0:T(8,128)(2,1)S(1)} collective-permute-done((bf16[64,1280]{1,0:T(8,128)(2,1)S(1)}, bf16[64,1280]{1,0:T(8,128)(2,1)S(1)}, u32[]{:S(2)}, u32[]{:S(2)}) %collective-permute-start.17) | collective-permute-done | bytes 163872 | tf_op jit(solution)/shard_map/ppermute | solution.py:144
  62.0 3.5 %collective-permute-done.7 = bf16[64,1280]{1,0:T(8,128)(2,1)S(1)} collective-permute-done((bf16[64,1280]{1,0:T(8,128)(2,1)S(1)}, bf16[64,1280]{1,0:T(8,128)(2,1)S(1)}, u32[]{:S(2)}, u32[]{:S(2)}) %collective-permute-start.7) | collective-permute-done | bytes 163872 | tf_op jit(solution)/shard_map/ppermute | solution.py:144
  65.5 1.2 collective-permute-start.8
  67.4 8.2 %collective-permute-done.8 = bf16[64,1280]{1,0:T(8,128)(2,1)S(1)} collective-permute-done((bf16[64,1280]{1,0:T(8,128)(2,1)S(1)}, bf16[64,1280]{1,0:T(8,128)(2,1)S(1)}, u32[]{:S(2)}, u32[]{:S(2)}) %collective-permute-start.8) | collective-permute-done | bytes 163872 | tf_op jit(solution)/shard_map/ppermute | solution.py:144
  76.4 7.7 %collective-permute-done.9 = bf16[64,1280]{1,0:T(8,128)(2,1)S(1)} collective-permute-done((bf16[64,1280]{1,0:T(8,128)(2,1)S(1)}, bf16[64,1280]{1,0:T(8,128)(2,1)S(1)}, u32[]{:S(2)}, u32[]{:S(2)}) %collective-permute-start.9) | collective-permute-done | bytes 163872 | tf_op jit(solution)/shard_map/ppermute | solution.py:144
  86.0 14.6 %collective-permute-start.22 = (bf16[256,128]{1,0:T(8,128)(2,1)S(1)}, bf16[256,128]{1,0:T(8,128)(2,1)S(1)}, u32[]{:S(2)}, u32[]{:S(2)}) collective-permute-start(bf16[256,128]{1,0:T(8,128)(2,1)S(1)} %copy-done.3), channel_id=1, source_target_pairs={{0,8},{8,0},{1,9},{9,1},{2,10},{10,2},{3,11},{11,3},{4,12},{12,4},... | collective-permute-start | bytes 196616 | tf_op jit(solution)/shard_map/ppermute | solution.py:167
  102.7 6.1 %couple.3.t_ref = bf16[4,4096,256]{2,1,0:T(8,128)(2,1)} custom-call(bf16[256,128]{1,0:T(8,128)(2,1)} %copy-done.4, bf16[32,4096]{1,0:T(8,128)(2,1)} %reshape.26.w_ref), custom_call_target="tpu_custom_call" | custom-call | flops 268435456 | bytes 8388608 | tf_op jit(solution)/shard_map/couple/pallas_call | solution.py:63
  108.8 1.1 collective-permute-start.20
  109.9 1.1 collective-permute-start.12
  112.2 6.3 %collective-permute-done.20 = bf16[256,1280]{1,0:T(8,128)(2,1)S(1)} collective-permute-done((bf16[256,1280]{1,0:T(8,128)(2,1)S(1)}, bf16[256,1280]{1,0:T(8,128)(2,1)S(1)}, u32[]{:S(2)}, u32[]{:S(2)}) %collective-permute-start.20) | collective-permute-done | bytes 655392 | tf_op jit(solution)/shard_map/ppermute | solution.py:144
  119.7 5.9 %collective-permute-done.21 = bf16[256,1280]{1,0:T(8,128)(2,1)S(1)} collective-permute-done((bf16[256,1280]{1,0:T(8,128)(2,1)S(1)}, bf16[256,1280]{1,0:T(8,128)(2,1)S(1)}, u32[]{:S(2)}, u32[]{:S(2)}) %collective-permute-start.21) | collective-permute-done | bytes 655392 | tf_op jit(solution)/shard_map/ppermute | solution.py:144
  126.4 16.7 %pair.3 = bf16[8,16,1,64,128]{4,3,2,1,0:T(8,128)(2,1)} custom-call(s32[4]{0:T(128)} %pad_add_fusion.at_ref, bf16[1024,1536]{1,0:T(8,128)(2,1)} %all-gather.2.cloned.1.call-done.ra_ref, bf16[1024,1280]{1,0:T(8,128)(2,1)} %copy-done.6, bf16[1024,1280]{1,0:T(8,128)(2,1)} %constant_dynamic-update-slice_fusion.40.rc_ref, bf16[4,4096,256]{2,1,0:T(8,128)(2,1)} %couple.3.t_ref, ...), custom_call_target="tpu_custom_call" | custom-call | flops 8589934592 | bytes 16777216 | tf_op jit(solution)/shard_map/pair/pallas_call | solution.py:116
  143.2 2.1 %collective-permute-start.23 = (bf16[8,16,1,64,128]{4,3,2,1,0:T(8,128)(2,1)}, bf16[8,16,1,64,128]{4,3,2,1,0:T(8,128)(2,1)S(1)}, u32[]{:S(2)}, u32[]{:S(2)}) collective-permute-start(bf16[8,16,1,64,128]{4,3,2,1,0:T(8,128)(2,1)} %pair.3), channel_id=1, source_target_pairs={{0,8},{8,0},{1,9},{9,1},{2,10},{10,2},{3,11},{11,3},{4,12},{12,4},... | collective-permute-start | bytes 6291464 | tf_op jit(solution)/shard_map/ppermute | solution.py:178
  145.2 5.9 %couple.2.t_ref = bf16[4,4096,256]{2,1,0:T(8,128)(2,1)} custom-call(bf16[256,128]{1,0:T(8,128)(2,1)} %get-tuple-element.12.lt_ref, bf16[32,4096]{1,0:T(8,128)(2,1)} %reshape.26.w_ref), custom_call_target="tpu_custom_call" | custom-call | flops 268435456 | bytes 8388608 | tf_op jit(solution)/shard_map/couple/pallas_call | solution.py:63
  151.2 16.5 %pair.2 = bf16[8,16,2,64,128]{4,3,2,1,0:T(8,128)(2,1)} custom-call(s32[4]{0:T(128)} %pad_add_fusion.at_ref, bf16[1024,1536]{1,0:T(8,128)(2,1)} %all-gather.2.cloned.1.call-done.ra_ref, bf16[1024,1280]{1,0:T(8,128)(2,1)} %copy-done.6, bf16[1024,1280]{1,0:T(8,128)(2,1)} %constant_dynamic-update-slice_fusion.40.rc_ref, bf16[4,4096,256]{2,1,0:T(8,128)(2,1)} %couple.2.t_ref, ...), custom_call_target="tpu_custom_call" | custom-call | flops 8589934592 | bytes 16777216 | tf_op jit(solution)/shard_map/pair/pallas_call | solution.py:116
  167.6 2.0 %constant_dynamic-update-slice_fusion.50 = bf16[8,16,2,64,128]{4,3,2,1,0:T(8,128)(2,1)} fusion(bf16[8,16,2,64,128]{4,3,2,1,0:T(8,128)(2,1)} %pair.2, bf16[8,16,1,64,128]{4,3,2,1,0:T(8,128)(2,1)S(1)} %collective-permute-done.23, s32[]{:T(128)S(6)} %select_n.3), kind=kLoop, calls=%fused_computation.58 | loop fusion | bytes 4194308 | tf_op jit(solution)/shard_map/dynamic_update_slice | solution.py:180
  (74 shorter events, 20.0 us)
Async XLA Ops:
  6.5 119.9 %all-gather.2.cloned.1.call-start = ((), (), s32[]{:S(2)}) async-start(), calls=%async_computation | async-start | bytes 3538944 | tf_op jit(solution)/shard_map/all_gather | solution.py:173
  12.2 45.0 %copy-start.1 = (bf16[8,1280]{1,0:T(8,128)(2,1)S(1)}, bf16[8,1280]{1,0:T(8,128)(2,1)}, u32[]{:S(2)}) copy-start(bf16[8,1280]{1,0:T(8,128)(2,1)} %get-tuple-element.10) | copy-start | bytes 61444
  12.2 29.0 %collective-permute-start.13 = (bf16[8,1280]{1,0:T(8,128)(2,1)}, bf16[8,1280]{1,0:T(8,128)(2,1)S(1)}, u32[]{:S(2)}, u32[]{:S(2)}) collective-permute-start(bf16[8,1280]{1,0:T(8,128)(2,1)} %get-tuple-element.11), channel_id=1, source_target_pairs={{0,1},{1,0},{2,3},{3,2},{4,5},{5,4},{6,7},{7,6},{8,15},{9,10},{10,... | collective-permute-start | bytes 61448 | tf_op jit(solution)/shard_map/ppermute | solution.py:144
  18.6 23.3 %collective-permute-start.4 = (bf16[8,1280]{1,0:T(8,128)(2,1)}, bf16[8,1280]{1,0:T(8,128)(2,1)S(1)}, u32[]{:S(2)}, u32[]{:S(2)}) collective-permute-start(bf16[8,1280]{1,0:T(8,128)(2,1)} %get-tuple-element.10), channel_id=1, source_target_pairs={{0,64},{64,0},{128,192},{192,128},{8,200},{72,136},{136,72},{200,8... | collective-permute-start | bytes 61448 | tf_op jit(solution)/shard_map/ppermute | solution.py:144
  21.3 4.6 %collective-permute-start = (bf16[8,1536]{1,0:T(8,128)(2,1)}, bf16[8,1536]{1,0:T(8,128)(2,1)S(1)}, u32[]{:S(2)}, u32[]{:S(2)}) collective-permute-start(bf16[8,1536]{1,0:T(8,128)(2,1)} %get-tuple-element.9), channel_id=1, source_target_pairs={{0,16},{16,0},{32,48},{48,32},{8,56},{24,40},{40,24},{56,8},{1,17}... | collective-permute-start | bytes 73736 | tf_op jit(solution)/shard_map/ppermute | solution.py:144
  26.6 2.9 %collective-permute-start.1 = (bf16[16,1536]{1,0:T(8,128)(2,1)S(1)}, bf16[16,1536]{1,0:T(8,128)(2,1)S(1)}, u32[]{:S(2)}, u32[]{:S(2)}) collective-permute-start(bf16[16,1536]{1,0:T(8,128)(2,1)S(1)} %pad_maximum_fusion.4), channel_id=1, source_target_pairs={{0,48},{16,32},{32,16},{48,0},{8,24},{24,8},{40,56},{56,40},{1,49}... | collective-permute-start | bytes 147464 | tf_op jit(solution)/shard_map/ppermute | solution.py:144
  30.3 4.7 %collective-permute-start.2 = (bf16[32,1536]{1,0:T(8,128)(2,1)S(1)}, bf16[32,1536]{1,0:T(8,128)(2,1)S(1)}, u32[]{:S(2)}, u32[]{:S(2)}) collective-permute-start(bf16[32,1536]{1,0:T(8,128)(2,1)S(1)} %pad_maximum_fusion.2), channel_id=1, source_target_pairs={{0,64},{64,0},{128,192},{192,128},{8,200},{72,136},{136,72},{200,8... | collective-permute-start | bytes 294920 | tf_op jit(solution)/shard_map/ppermute | solution.py:144
  35.7 4.6 %collective-permute-start.3 = (bf16[64,1536]{1,0:T(8,128)(2,1)S(1)}, bf16[64,1536]{1,0:T(8,128)(2,1)S(1)}, u32[]{:S(2)}, u32[]{:S(2)}) collective-permute-start(bf16[64,1536]{1,0:T(8,128)(2,1)S(1)} %pad_maximum_fusion), channel_id=1, source_target_pairs={{0,192},{64,128},{128,64},{192,0},{8,72},{72,8},{136,200},{200,136... | collective-permute-start | bytes 589832 | tf_op jit(solution)/shard_map/ppermute | solution.py:144
  40.4 0.7 copy-start
  40.4 45.6 %copy-start.3 = (bf16[256,128]{1,0:T(8,128)(2,1)S(1)}, bf16[256,128]{1,0:T(8,128)(2,1)}, u32[]{:S(2)}) copy-start(bf16[256,128]{1,0:T(8,128)(2,1)} %get-tuple-element.12.lt_ref) | copy-start | bytes 196612
  40.4 60.2 %copy-start.2 = (bf16[1024,128]{1,0:T(8,128)(2,1)S(1)}, bf16[1024,128]{1,0:T(8,128)(2,1)}, u32[]{:S(2)}) copy-start(bf16[1024,128]{1,0:T(8,128)(2,1)} %param.16) | copy-start | bytes 786436
  41.9 5.8 %collective-permute-start.14 = (bf16[16,1280]{1,0:T(8,128)(2,1)S(1)}, bf16[16,1280]{1,0:T(8,128)(2,1)S(1)}, u32[]{:S(2)}, u32[]{:S(2)}) collective-permute-start(bf16[16,1280]{1,0:T(8,128)(2,1)S(1)} %pad_maximum_fusion.6), channel_id=1, source_target_pairs={{0,7},{1,2},{2,1},{3,4},{4,3},{5,6},{6,5},{7,0},{8,9},{9,8},{10,11... | collective-permute-start | bytes 122888 | tf_op jit(solution)/shard_map/ppermute | solution.py:144
  42.6 2.9 %collective-permute-start.5 = (bf16[16,1280]{1,0:T(8,128)(2,1)S(1)}, bf16[16,1280]{1,0:T(8,128)(2,1)S(1)}, u32[]{:S(2)}, u32[]{:S(2)}) collective-permute-start(bf16[16,1280]{1,0:T(8,128)(2,1)S(1)} %pad_maximum_fusion.5), channel_id=1, source_target_pairs={{0,192},{64,128},{128,64},{192,0},{8,72},{72,8},{136,200},{200,136... | collective-permute-start | bytes 122888 | tf_op jit(solution)/shard_map/ppermute | solution.py:144
  46.2 11.0 %collective-permute-start.6 = (bf16[32,1280]{1,0:T(8,128)(2,1)S(1)}, bf16[32,1280]{1,0:T(8,128)(2,1)S(1)}, u32[]{:S(2)}, u32[]{:S(2)}) collective-permute-start(bf16[32,1280]{1,0:T(8,128)(2,1)S(1)} %pad_maximum_fusion.3), channel_id=1, source_target_pairs={{0,1},{1,0},{2,3},{3,2},{4,5},{5,4},{6,7},{7,6},{8,15},{9,10},{10,... | collective-permute-start | bytes 245768 | tf_op jit(solution)/shard_map/ppermute | solution.py:144
  47.7 4.4 %collective-permute-start.15 = (bf16[16,1280]{1,0:T(8,128)(2,1)S(1)}, bf16[16,1280]{1,0:T(8,128)(2,1)S(1)}, u32[]{:S(2)}, u32[]{:S(2)}) collective-permute-start(bf16[16,1280]{1,0:T(8,128)(2,1)S(1)} %collective-permute-done.14), channel_id=1, source_target_pairs={{0,1},{1,0},{2,3},{3,2},{4,5},{5,4},{6,7},{7,6},{8,15},{9,10},{10,... | collective-permute-start | bytes 122888 | tf_op jit(solution)/shard_map/ppermute | solution.py:144
  52.0 2.9 %collective-permute-start.16 = (bf16[16,1280]{1,0:T(8,128)(2,1)S(1)}, bf16[16,1280]{1,0:T(8,128)(2,1)S(1)}, u32[]{:S(2)}, u32[]{:S(2)}) collective-permute-start(bf16[16,1280]{1,0:T(8,128)(2,1)S(1)} %collective-permute-done.15), channel_id=1, source_target_pairs={{0,7},{1,2},{2,1},{3,4},{4,3},{5,6},{6,5},{7,0},{8,9},{9,8},{10,11... | collective-permute-start | bytes 122888 | tf_op jit(solution)/shard_map/ppermute | solution.py:144
  55.5 5.8 %collective-permute-start.17 = (bf16[64,1280]{1,0:T(8,128)(2,1)S(1)}, bf16[64,1280]{1,0:T(8,128)(2,1)S(1)}, u32[]{:S(2)}, u32[]{:S(2)}) collective-permute-start(bf16[64,1280]{1,0:T(8,128)(2,1)S(1)} %get-tuple-element.29), channel_id=1, source_target_pairs={{0,16},{16,0},{32,48},{48,32},{8,56},{24,40},{40,24},{56,8},{1,17}... | collective-permute-start | bytes 491528 | tf_op jit(solution)/shard_map/ppermute | solution.py:144
  57.2 8.3 %collective-permute-start.7 = (bf16[64,1280]{1,0:T(8,128)(2,1)S(1)}, bf16[64,1280]{1,0:T(8,128)(2,1)S(1)}, u32[]{:S(2)}, u32[]{:S(2)}) collective-permute-start(bf16[64,1280]{1,0:T(8,128)(2,1)S(1)} %pad_maximum_fusion.1), channel_id=1, source_target_pairs={{0,7},{1,2},{2,1},{3,4},{4,3},{5,6},{6,5},{7,0},{8,9},{9,8},{10,11... | collective-permute-start | bytes 491528 | tf_op jit(solution)/shard_map/ppermute | solution.py:144
  62.0 22.8 %collective-permute-start.18 = (bf16[128,1280]{1,0:T(8,128)(2,1)S(1)}, bf16[128,1280]{1,0:T(8,128)(2,1)S(1)}, u32[]{:S(2)}, u32[]{:S(2)}) collective-permute-start(bf16[128,1280]{1,0:T(8,128)(2,1)S(1)} %get-tuple-element.17), channel_id=1, source_target_pairs={{0,48},{16,32},{32,16},{48,0},{8,24},{24,8},{40,56},{56,40},{1,49}... | collective-permute-start | bytes 983048 | tf_op jit(solution)/shard_map/ppermute | solution.py:144
  65.5 10.1 %collective-permute-start.8 = (bf16[64,1280]{1,0:T(8,128)(2,1)S(1)}, bf16[64,1280]{1,0:T(8,128)(2,1)S(1)}, u32[]{:S(2)}, u32[]{:S(2)}) collective-permute-start(bf16[64,1280]{1,0:T(8,128)(2,1)S(1)} %collective-permute-done.7), channel_id=1, source_target_pairs={{0,1},{1,0},{2,3},{3,2},{4,5},{5,4},{6,7},{7,6},{8,15},{9,10},{10,... | collective-permute-start | bytes 491528 | tf_op jit(solution)/shard_map/ppermute | solution.py:144
  75.6 8.5 %collective-permute-start.9 = (bf16[64,1280]{1,0:T(8,128)(2,1)S(1)}, bf16[64,1280]{1,0:T(8,128)(2,1)S(1)}, u32[]{:S(2)}, u32[]{:S(2)}) collective-permute-start(bf16[64,1280]{1,0:T(8,128)(2,1)S(1)} %collective-permute-done.8), channel_id=1, source_target_pairs={{0,7},{1,2},{2,1},{3,4},{4,3},{5,6},{6,5},{7,0},{8,9},{9,8},{10,11... | collective-permute-start | bytes 491528 | tf_op jit(solution)/shard_map/ppermute | solution.py:144
  84.8 25.1 %collective-permute-start.10 = (bf16[256,1280]{1,0:T(8,128)(2,1)}, bf16[256,1280]{1,0:T(8,128)(2,1)S(1)}, u32[]{:S(2)}, u32[]{:S(2)}) collective-permute-start(bf16[256,1280]{1,0:T(8,128)(2,1)} %get-tuple-element.18), channel_id=1, source_target_pairs={{0,16},{16,0},{32,48},{48,32},{8,56},{24,40},{40,24},{56,8},{1,17}... | collective-permute-start | bytes 1966088 | tf_op jit(solution)/shard_map/ppermute | solution.py:144
  84.8 26.3 %collective-permute-start.11 = (bf16[256,1280]{1,0:T(8,128)(2,1)}, bf16[256,1280]{1,0:T(8,128)(2,1)S(1)}, u32[]{:S(2)}, u32[]{:S(2)}) collective-permute-start(bf16[256,1280]{1,0:T(8,128)(2,1)} %get-tuple-element.18), channel_id=1, source_target_pairs={{0,48},{16,32},{32,16},{48,0},{8,24},{24,8},{40,56},{56,40},{1,49}... | collective-permute-start | bytes 1966088 | tf_op jit(solution)/shard_map/ppermute | solution.py:144
  85.6 25.5 %collective-permute-start.19 = (bf16[256,1280]{1,0:T(8,128)(2,1)S(1)}, bf16[256,1280]{1,0:T(8,128)(2,1)S(1)}, u32[]{:S(2)}, u32[]{:S(2)}) collective-permute-start(bf16[256,1280]{1,0:T(8,128)(2,1)S(1)} %get-tuple-element.13), channel_id=1, source_target_pairs={{0,64},{64,0},{128,192},{192,128},{8,200},{72,136},{136,72},{200,8... | collective-permute-start | bytes 1966088 | tf_op jit(solution)/shard_map/ppermute | solution.py:144
  86.0 16.1 %collective-permute-start.22 = (bf16[256,128]{1,0:T(8,128)(2,1)S(1)}, bf16[256,128]{1,0:T(8,128)(2,1)S(1)}, u32[]{:S(2)}, u32[]{:S(2)}) collective-permute-start(bf16[256,128]{1,0:T(8,128)(2,1)S(1)} %copy-done.3), channel_id=1, source_target_pairs={{0,8},{8,0},{1,9},{9,1},{2,10},{10,2},{3,11},{11,3},{4,12},{12,4},... | collective-permute-start | bytes 196616 | tf_op jit(solution)/shard_map/ppermute | solution.py:167
  102.1 8.9 %copy-start.5 = (bf16[1024,1280]{1,0:T(8,128)(2,1)S(1)}, bf16[1024,1280]{1,0:T(8,128)(2,1)}, u32[]{:S(2)}) copy-start(bf16[1024,1280]{1,0:T(8,128)(2,1)} %get-tuple-element.19) | copy-start | bytes 7864324
  102.1 0.6 copy-start.4
  108.8 9.7 %collective-permute-start.20 = (bf16[256,1280]{1,0:T(8,128)(2,1)S(1)}, bf16[256,1280]{1,0:T(8,128)(2,1)S(1)}, u32[]{:S(2)}, u32[]{:S(2)}) collective-permute-start(bf16[256,1280]{1,0:T(8,128)(2,1)S(1)} %get-tuple-element.13), channel_id=1, source_target_pairs={{0,192},{64,128},{128,64},{192,0},{8,72},{72,8},{136,200},{200,136... | collective-permute-start | bytes 1966088 | tf_op jit(solution)/shard_map/ppermute | solution.py:144
  109.9 9.7 %collective-permute-start.12 = (bf16[256,1280]{1,0:T(8,128)(2,1)S(1)}, bf16[256,1280]{1,0:T(8,128)(2,1)S(1)}, u32[]{:S(2)}, u32[]{:S(2)}) collective-permute-start(bf16[256,1280]{1,0:T(8,128)(2,1)S(1)} %collective-permute-done.10), channel_id=1, source_target_pairs={{0,48},{16,32},{32,16},{48,0},{8,24},{24,8},{40,56},{56,40},{1,49}... | collective-permute-start | bytes 1966088 | tf_op jit(solution)/shard_map/ppermute | solution.py:144
  111.1 14.4 %collective-permute-start.21 = (bf16[256,1280]{1,0:T(8,128)(2,1)S(1)}, bf16[256,1280]{1,0:T(8,128)(2,1)S(1)}, u32[]{:S(2)}, u32[]{:S(2)}) collective-permute-start(bf16[256,1280]{1,0:T(8,128)(2,1)S(1)} %collective-permute-done.19), channel_id=1, source_target_pairs={{0,192},{64,128},{128,64},{192,0},{8,72},{72,8},{136,200},{200,136... | collective-permute-start | bytes 1966088 | tf_op jit(solution)/shard_map/ppermute | solution.py:144
  119.7 5.9 %copy-start.6 = (bf16[1024,1280]{1,0:T(8,128)(2,1)}, bf16[1024,1280]{1,0:T(8,128)(2,1)S(1)}, u32[]{:S(2)}) copy-start(bf16[1024,1280]{1,0:T(8,128)(2,1)S(1)} %constant_dynamic-update-slice_fusion.12.rb_ref) | copy-start | bytes 7864324
  143.2 24.5 %collective-permute-start.23 = (bf16[8,16,1,64,128]{4,3,2,1,0:T(8,128)(2,1)}, bf16[8,16,1,64,128]{4,3,2,1,0:T(8,128)(2,1)S(1)}, u32[]{:S(2)}, u32[]{:S(2)}) collective-permute-start(bf16[8,16,1,64,128]{4,3,2,1,0:T(8,128)(2,1)} %pair.3), channel_id=1, source_target_pairs={{0,8},{8,0},{1,9},{9,1},{2,10},{10,2},{3,11},{11,3},{4,12},{12,4},... | collective-permute-start | bytes 6291464 | tf_op jit(solution)/shard_map/ppermute | solution.py:178
Sparse Core Ops, SparseCore 0:
  41.3 52.8 all-gather.1

commit v2 on v0

v2 whole, which is shorter than its diff:
```python
import jax
import jax.numpy as jnp
from jax import lax
from jax.experimental import pallas as pl
from jax.experimental.pallas import tpu as pltpu
from jax.sharding import Mesh, PartitionSpec as P

S, CM, CH, CZ, LOCAL = 128, 256, 32, 128, 8
EH = CH // 2
HALF = EH * S
UNIT = 2 * LOCAL
BLOCK = 4 * 8 * UNIT
MIB = 1024 * 1024
BF16, F32 = jnp.bfloat16, jnp.float32


def project_kernel(core_ref, msa_in, gain_in, shift_in, w1_in, b1_in, w2_in, b2_in, keep_ref, give_ref, lt_ref,
                   msa_ref, gain_ref, shift_ref, w_s, b1_ref, b2_ref, y_s, r_s, sem):
    pairs = ((msa_in, msa_ref), (gain_in, gain_ref), (shift_in, shift_ref), (w1_in, w_s.at[pl.ds(0, CH)]),
             (w2_in, w_s.at[pl.ds(CH, CH)]), (b1_in, b1_ref), (b2_in, b2_ref))
    copies = [pltpu.make_async_copy(src, dst, sem.at[k]) for k, (src, dst) in enumerate(pairs)]
    for copy in copies:
        copy.start()
    for copy in copies:
        copy.wait()
    x = msa_ref[...].astype(F32).reshape(S * LOCAL, CM)
    mean = jnp.mean(x, axis=-1, keepdims=True)
    centered = x - mean
    variance = jnp.mean(centered * centered, axis=-1, keepdims=True)
    normed = (centered * lax.rsqrt(variance + 1e-05) * gain_ref[...] + shift_ref[...]).astype(BF16)
    y = lax.dot_general(normed, w_s[...], (((1,), (1,)), ((), ())), preferred_element_type=F32)
    bias = jnp.concatenate([b1_ref[...], b2_ref[...]], axis=1)
    y_s[:, 0:2 * CH] = (y + bias).astype(BF16).astype(F32)
    for j in range(LOCAL):
        t = y_s[pl.ds(j, S, stride=LOCAL), :].T
        lt_ref[j * CH:(j + 1) * CH, :] = (t[0:CH] * (1.0 / S)).astype(BF16)
        r_s[j * CH:(j + 1) * CH, :] = t[CH:2 * CH]
    core = core_ref[0]
    for e in range(EH):
        keep_ref[:, e * S:(e + 1) * S] = r_s[pl.ds(core * EH + e, LOCAL, stride=CH), :].astype(BF16)
        give_ref[:, e * S:(e + 1) * S] = r_s[pl.ds((1 - core) * EH + e, LOCAL, stride=CH), :].astype(BF16)


def project(core, msa, gain, shift, w1, b1, w2, b2):
    return pl.pallas_call(
        project_kernel,
        grid_spec=pltpu.PrefetchScalarGridSpec(
            num_scalar_prefetch=1,
            grid=(1,),
            in_specs=[pl.BlockSpec(memory_space=pl.ANY)] * 7,
            out_specs=[
                pl.BlockSpec((LOCAL, HALF), lambda n, core: (0, 0)),
                pl.BlockSpec((LOCAL, HALF), lambda n, core: (0, 0)),
                pl.BlockSpec((LOCAL * CH, S), lambda n, core: (0, 0)),
            ],
            scratch_shapes=[
                pltpu.VMEM((S, LOCAL, CM), BF16),
                pltpu.VMEM((1, CM), F32),
                pltpu.VMEM((1, CM), F32),
                pltpu.VMEM((2 * CH, CM), BF16),
                pltpu.VMEM((1, CH), F32),
                pltpu.VMEM((1, CH), F32),
                pltpu.VMEM((S * LOCAL, S), F32),
                pltpu.VMEM((LOCAL * CH, S), F32),
                pltpu.SemaphoreType.DMA((7,)),
            ],
        ),
        out_shape=[
            jax.ShapeDtypeStruct((LOCAL, HALF), BF16),
            jax.ShapeDtypeStruct((LOCAL, HALF), BF16),
            jax.ShapeDtypeStruct((LOCAL * CH, S), BF16),
        ],
        compiler_params=pltpu.CompilerParams(vmem_limit_bytes=60 * MIB),
        name="project",
    )(core, msa, gain.reshape(1, CM), shift.reshape(1, CM), w1.T, b1.reshape(1, CH), w2.T, b2.reshape(1, CH))


def couple_kernel(theirs_ref, mine_ref, w_ref, t_ref):
    lt = jnp.where(pl.program_id(0) < 2, theirs_ref[...], mine_ref[...])
    for n in range(2):
        for i in range(2):
            row = (n * 2 + i) * CH
            t = lax.dot_general(lt[row:row + CH, :], w_ref[...], (((0,), (0,)), ((), ())),
                                preferred_element_type=F32).astype(BF16)
            for e in range(EH):
                t_ref[n, e * S:(e + 1) * S, i * CZ:(i + 1) * CZ] = t[:, e * CZ:(e + 1) * CZ]


def couple(theirs, mine, w):
    return pl.pallas_call(
        couple_kernel,
        grid=(4,),
        in_specs=[
            pl.BlockSpec((4 * CH, S), lambda n: (n % 2, 0)),
            pl.BlockSpec((4 * CH, S), lambda n: (n % 2, 0)),
            pl.BlockSpec((CH, EH * CZ), lambda n: (0, 0)),
        ],
        out_specs=pl.BlockSpec((2, HALF, 2 * CZ), lambda n: (n, 0, 0)),
        out_shape=jax.ShapeDtypeStruct((LOCAL, HALF, 2 * CZ), BF16),
        compiler_params=pltpu.CompilerParams(vmem_limit_bytes=16 * MIB),
        cost_estimate=pl.CostEstimate(flops=2 * 16 * S * CH * EH * CZ, bytes_accessed=9 * MIB, transcendentals=0),
        name="couple",
    )(theirs, mine, w)


def place8(own, core, t):
    rel = jnp.where((own + core) % 2 == 0, t - own, own - t) & 7
    half, low = rel >> 1, rel & 1
    return jnp.where(half == 0, low, jnp.where(half == 1, 4 + low, jnp.where(half == 2, 7 - low, 3 - low)))


def place4(own, core, t):
    rel = jnp.where((own + core) % 2 == 0, t - own, own - t) & 3
    return rel ^ (rel >> 1)


def holder4(own, core, k):
    step = (0, 1, -1, -2)[k]
    return (own + jnp.where((own + core) % 2 == 0, step, -step)) & 3


def block_kernel(count, at_ref, *refs):
    r_refs, t_ref, o_refs, sum_s = refs[:count], refs[count], refs[count + 1:-1], refs[-1]
    core, z = at_ref[0], at_ref[3]
    minor = jnp.where(core == 0, at_ref[1], at_ref[2])
    pm = [place4(minor, core, t) for t in range(4)]
    pz = [place8(z, core, t) for t in range(8)]
    rows = BLOCK // count
    for n in range(2):
        for k in range(count):
            sum_s[n, k * rows:(k + 1) * rows, :] = jnp.dot(r_refs[k][...], t_ref[n], preferred_element_type=F32)

    def store(o_ref):
        for n in range(2):
            for tm in range(4):
                for c in range(2):
                    side = jnp.where(core == c, 0, LOCAL)
                    for tz in range(0, 8, 2):
                        both = [
                            sum_s[n, pl.ds(pl.multiple_of((pm[tm] * 8 + pz[tz + d]) * UNIT + side, LOCAL), LOCAL), :]
                            for d in range(2)
                        ]
                        value = jnp.concatenate(both, axis=0).astype(BF16)
                        for i in range(2):
                            o_ref[n * 2 + i, tm, c, tz * LOCAL:(tz + 2) * LOCAL, :] = value[:, i * CZ:(i + 1) * CZ]

    if len(o_refs) == 1:
        store(o_refs[0])
    else:
        pl.when(pl.program_id(0) < 2)(lambda: store(o_refs[0]))
        pl.when(pl.program_id(0) >= 2)(lambda: store(o_refs[1]))


def block(at, pieces, t, part):
    count = len(pieces)
    rows = BLOCK // count
    first = 2 if part == 1 else 0
    shape = (LOCAL, 4, 2, 64, CZ)
    spec = lambda where: pl.BlockSpec((4,) + shape[1:], lambda n, at: (where(n), 0, 0, 0, 0))
    if part is None:
        out_specs = [spec(lambda n: jnp.minimum(n, 1)), spec(lambda n: jnp.maximum(n - 2, 0))]
    else:
        out_specs = [spec(lambda n: n)]
    return pl.pallas_call(
        lambda *refs: block_kernel(count, *refs),
        grid_spec=pltpu.PrefetchScalarGridSpec(
            num_scalar_prefetch=1,
            grid=(4 if part is None else 2,),
            in_specs=[pl.BlockSpec((rows, HALF), lambda n, at: (0, 0))] * count
            + [pl.BlockSpec((2, HALF, 2 * CZ), lambda n, at: (first + n, 0, 0))],
            out_specs=out_specs,
            scratch_shapes=[pltpu.VMEM((2, BLOCK, 2 * CZ), F32)],
        ),
        out_shape=[jax.ShapeDtypeStruct(shape, BF16)] * len(out_specs),
        compiler_params=pltpu.CompilerParams(vmem_limit_bytes=24 * MIB),
        cost_estimate=pl.CostEstimate(flops=2 * BLOCK * HALF * 1024 * len(out_specs), bytes_accessed=10 * MIB,
                                      transcendentals=0),
        name="block",
    )(at, *pieces, t)


def add_kernel(at_ref, *refs):
    mine, theirs, bias_ref, o_ref = refs[0:4], refs[4:8], refs[8], refs[9]
    core = at_ref[0]
    minor = jnp.where(core == 0, at_ref[1], at_ref[2])
    major = jnp.where(core == 0, at_ref[2], at_ref[1])
    bias = bias_ref[...]
    for k in range(4):
        a = holder4(major, core, k)
        for m in range(4):
            b = holder4(minor, 1 - core, m)
            group = jnp.where(core == 0, b * 4 + a, a * 4 + b)
            for i in range(2):
                v = mine[k][i, b].astype(F32) + theirs[m][i, a].astype(F32)
                o_ref[i, group] = (v.reshape(128, CZ) + bias).astype(BF16).reshape(2, 64, CZ)


def add(at, mine, theirs, bias):
    return pl.pallas_call(
        add_kernel,
        grid_spec=pltpu.PrefetchScalarGridSpec(
            num_scalar_prefetch=1,
            grid=(LOCAL // 2,),
            in_specs=[pl.BlockSpec((2, 4, 2, 64, CZ), lambda n, at: (n, 0, 0, 0, 0))] * 8
            + [pl.BlockSpec((1, CZ), lambda n, at: (0, 0))],
            out_specs=pl.BlockSpec((2, 16, 2, 64, CZ), lambda n, at: (n, 0, 0, 0, 0)),
        ),
        out_shape=jax.ShapeDtypeStruct((LOCAL, 16, 2, 64, CZ), BF16),
        compiler_params=pltpu.CompilerParams(vmem_limit_bytes=24 * MIB),
        cost_estimate=pl.CostEstimate(flops=10**7, bytes_accessed=13 * MIB, transcendentals=0),
        name="add",
    )(at, *mine, *theirs, bias.reshape(1, CZ))


def partner(k, n, core, step):
    return (k + 1 if (k + core + step) % 2 == 0 else k - 1) % n


def along_z(v, step):
    return lax.ppermute(
        v, ("c", "z"), [(c * 8 + k, c * 8 + partner(k, 8, c, step)) for c in range(2) for k in range(8)])


def along_plane(v, last, step):
    pairs = []
    for y in range(4):
        for x in range(4):
            for c in range(2):
                ny, nx = (y, partner(x, 4, c, step)) if (c == 0) == last else (partner(y, 4, c, step), x)
                pairs.append(((y * 4 + x) * 2 + c, (ny * 4 + nx) * 2 + c))
    return lax.ppermute(v, ("y", "x", "c"), pairs)


def swap(v):
    return lax.ppermute(v, "c", [(0, 1), (1, 0)])


def join(*blocks):
    return jnp.concatenate(blocks, axis=0)


def together(*values):
    return lax.optimization_barrier(values)


def per_device(msa, gain, shift, w1, b1, w2, b2, couple_map, couple_offset):
    core = lax.axis_index("c")
    at = jnp.stack([core, lax.axis_index("y"), lax.axis_index("x"), lax.axis_index("z")]).astype(jnp.int32)
    keep, give, lt = project(at, msa, gain, shift, w1, b1, w2, b2)
    r = join(keep, swap(give))
    lt_sibling = swap(lt)
    w = lax.dynamic_slice_in_dim(couple_map.reshape(CH, CH, CZ), core * EH, EH, axis=1).reshape(CH, EH * CZ)

    z1 = join(r, along_z(r, 0))
    z2 = along_z(z1, 1)
    z3 = along_z(z2, 2)
    z4 = along_z(z3, 3)
    r = join(z1, z2, z3, z4)

    m1 = along_plane(r, False, 0)
    m2 = along_plane(r, False, 1)
    m3 = along_plane(m1, False, 1)
    t = couple(lt_sibling, lt, w)
    b0 = join(r, m1, m2, m3)

    b1 = along_plane(b0, True, 0)
    b2 = along_plane(b0, True, 1)
    p0, q0 = block(at, [b0], t, None)
    b1, b2, p0, q0 = together(b1, b2, p0, q0)
    b3 = along_plane(b1[:BLOCK // 2], True, 1), along_plane(b2[BLOCK // 2:], True, 0)
    p1, q1 = block(at, [b1], t, None)
    p2, q2 = block(at, [b2], t, None)
    p3, = block(at, b3, t, 0)
    q3, = block(at, b3, t, 1)
    theirs = [swap(p) for p in (p0, p1, p2, p3)]
    mine = [q0, q1, q2, q3]
    return add(at, mine, theirs, couple_offset).reshape(LOCAL, 16 * 2 * 64, CZ)


def solution(mesh):
    fine = Mesh(mesh.devices.reshape(4, 4, 2, 8), ("y", "x", "c", "z"))
    rows = ("y", "x", "c", "z")
    return jax.shard_map(
        per_device,
        mesh=fine,
        in_specs=(P(None, rows, None), P(), P(), P(), P(), P(), P(), P(), P()),
        out_specs=P(rows, None, None),
        check_vma=False,
    )
```

time: 256 us -> 112 us (0.44)
  waiting for transfers between devices: 129 us -> 30.5 us
  matrix products: 56.1 us -> 0 us
  local copies, waits for them, and re-layouts: 51.9 us -> 8.6 us
  Pallas kernels: 0 us -> 38.2 us
  starting transfers between devices: 0.04 us -> 31.8 us
  between operations: 13.5 us -> 0.17 us
    all_gather x1 -> x0, waiting for transfers between devices: 129 us -> none  [per_device(): lax.all_gather(right, ('row', 'col'), axis=1, tiled=True)]
    dot_general x34 -> x0, matrix products: 56.1 us -> none  [the longest x16 30.7 us: one_part(): jnp.einsum('sic,sje->ijce', left_rows, right_part, preferred_element_type...]
    pallas_call x0 -> x8, Pallas kernels: none -> 38.2 us  [the longest x5 28.3 us: block(): pl.pallas_call(lambda *refs: block_kernel(count, *refs), grid_spec=pltpu....]
    ppermute x0 -> x17, starting transfers between devices: none -> 31.8 us  [the longest x6 17 us: swap(): return lax.ppermute(v, 'c', [(0, 1), (1, 0)])]
    ppermute x0 -> x17, waiting for transfers between devices: none -> 30.5 us  [the longest x7 20 us: along_plane(): return lax.ppermute(v, ('y', 'x', 'c'), pairs)]
    reshape x1 -> x0, local copies, waits for them, and re-layouts: 25 us -> none  [pair_block(): piece.reshape(seqs, count, block, piece.shape[2])]
    convert_element_type x16 -> x0, local copies, waits for them, and re-layouts: 21.7 us -> none  [one_part(): outer = outer.astype(jnp.bfloat16)]
    unnamed x16, local copies, waits for them, and re-layouts: 0.03 us -> 5.7 us
  transfers between devices with their start and end apart: 1 -> 17, of which waited for: 1 -> 10; matrix products, arithmetic and copies ran while one was open for 0% -> 5% of each run, Pallas kernels for 0% -> 28%
where the time goes in v2:
time: 112 us; the launch traced here: 111 us
  Pallas kernels  38.2 us (34%)
  starting transfers between devices  31.8 us (28%)
  waiting for transfers between devices  30.5 us (27%)
  local copies, waits for them, and re-layouts  8.6 us (8%)
  other arithmetic  2.2 us (2%)
    pallas_call x5, Pallas kernels, block(): pl.pallas_call(lambda *refs: block_kernel(count, *refs), grid_spec=pltpu....  28.3 us
    ppermute x7, waiting for transfers between devices, along_plane(): return lax.ppermute(v, ('y', 'x', 'c'), pairs)  20 us
    ppermute x6, starting transfers between devices, swap(): return lax.ppermute(v, 'c', [(0, 1), (1, 0)])  17 us
    ppermute x4, waiting for transfers between devices, along_z(): lax.ppermute(v, ('c', 'z'), [(c * 8 + k, c * 8 + partner(k, 8, c, step))...  9.61 us
    ppermute x7, starting transfers between devices, along_plane(): return lax.ppermute(v, ('y', 'x', 'c'), pairs)  8.51 us
    ppermute x4, starting transfers between devices, along_z(): lax.ppermute(v, ('c', 'z'), [(c * 8 + k, c * 8 + partner(k, 8, c, step))...  6.31 us
    unnamed x16, local copies, waits for them, and re-layouts  5.7 us
    pallas_call x1, Pallas kernels, add(): pl.pallas_call(add_kernel, grid_spec=pltpu.PrefetchScalarGridSpec(num_sca...  3.69 us
  transfers between devices with their start and end apart: 17, of which 10 were waited for; matrix products, arithmetic and copies ran while one was open for 5% of the time, Pallas kernels for 28%

profile of v2, /device:TPU:1, one launch (start us, length us, event | category | flops | bytes accessed | tf_op | source)
XLA Modules:
  0.0 111.4 jit_solution(12587205388381098477)
XLA Ops:
  0.7 3.3 %project.1 = (bf16[8,2048]{1,0:T(8,128)(2,1)}, bf16[8,2048]{1,0:T(8,128)(2,1)}, bf16[256,128]{1,0:T(8,128)(2,1)}) custom-call(s32[4]{0:T(128)} %pad_add_fusion.core_ref.refs_0_.at_ref, bf16[128,8,256]{2,1,0:T(8,128)(2,1)} %msa_in.1, f32[1,256]{1,0:T(1,128)} %bitcast.23, f32[1,256]{1,0:T(1,128)} %bitcast.24, bf16[32,256]{1,0:T(8,128)(2,1)} %bitcast.21, ...), custom_call_target="tpu_custom_call" | custom-call | tf_op jit(solution)/shard_map/project/pallas_call | solution.py:45
  3.9 3.3 %collective-permute-start = (bf16[8,2048]{1,0:T(8,128)(2,1)}, bf16[8,2048]{1,0:T(8,128)(2,1)S(1)}, u32[]{:S(2)}, u32[]{:S(2)}) collective-permute-start(bf16[8,2048]{1,0:T(8,128)(2,1)} %get-tuple-element.19), channel_id=1, source_target_pairs={{0,8},{8,0},{1,9},{9,1},{2,10},{10,2},{3,11},{11,3},{4,12},{12,4},... | collective-permute-start | bytes 98312 | tf_op jit(solution)/shard_map/ppermute | solution.py:235
  7.3 1.4 %constant_dynamic-update-slice_fusion.5 = (bf16[128,2048]{1,0:T(8,128)(2,1)S(1)}, bf16[512,2048]{1,0:T(8,128)(2,1)}) fusion(bf16[8,2048]{1,0:T(8,128)(2,1)} %get-tuple-element.18), kind=kLoop, calls=%fused_computation.8 | loop fusion | bytes 98304
  9.4 3.8 %collective-permute-start.1 = (bf16[16,2048]{1,0:T(8,128)(2,1)S(1)}, bf16[16,2048]{1,0:T(8,128)(2,1)S(1)}, u32[]{:S(2)}, u32[]{:S(2)}) collective-permute-start(bf16[16,2048]{1,0:T(8,128)(2,1)S(1)} %pad_maximum_fusion.1), channel_id=1, source_target_pairs={{0,1},{1,0},{2,3},{3,2},{4,5},{5,4},{6,7},{7,6},{8,15},{9,10},{10,... | collective-permute-start | bytes 196616 | tf_op jit(solution)/shard_map/ppermute | solution.py:220
  13.9 1.0 collective-permute-done.1
  14.9 0.8 pad_maximum_fusion
  16.4 3.5 %collective-permute-done.2 = bf16[32,2048]{1,0:T(8,128)(2,1)S(1)} collective-permute-done((bf16[32,2048]{1,0:T(8,128)(2,1)S(1)}, bf16[32,2048]{1,0:T(8,128)(2,1)S(1)}, u32[]{:S(2)}, u32[]{:S(2)}) %collective-permute-start.2) | collective-permute-done | bytes 131104 | tf_op jit(solution)/shard_map/ppermute | solution.py:220
  19.9 2.4 %collective-permute-start.3 = (bf16[32,2048]{1,0:T(8,128)(2,1)S(1)}, bf16[32,2048]{1,0:T(8,128)(2,1)S(1)}, u32[]{:S(2)}, u32[]{:S(2)}) collective-permute-start(bf16[32,2048]{1,0:T(8,128)(2,1)S(1)} %collective-permute-done.2), channel_id=1, source_target_pairs={{0,1},{1,0},{2,3},{3,2},{4,5},{5,4},{6,7},{7,6},{8,15},{9,10},{10,... | collective-permute-start | bytes 393224 | tf_op jit(solution)/shard_map/ppermute | solution.py:220
  22.9 2.0 %collective-permute-done.3 = bf16[32,2048]{1,0:T(8,128)(2,1)S(1)} collective-permute-done((bf16[32,2048]{1,0:T(8,128)(2,1)S(1)}, bf16[32,2048]{1,0:T(8,128)(2,1)S(1)}, u32[]{:S(2)}, u32[]{:S(2)}) %collective-permute-start.3) | collective-permute-done | bytes 131104 | tf_op jit(solution)/shard_map/ppermute | solution.py:220
  25.6 3.1 %collective-permute-done.4 = bf16[32,2048]{1,0:T(8,128)(2,1)S(1)} collective-permute-done((bf16[32,2048]{1,0:T(8,128)(2,1)S(1)}, bf16[32,2048]{1,0:T(8,128)(2,1)S(1)}, u32[]{:S(2)}, u32[]{:S(2)}) %collective-permute-start.4) | collective-permute-done | bytes 131104 | tf_op jit(solution)/shard_map/ppermute | solution.py:220
  29.4 2.5 %collective-permute-start.5 = (bf16[128,2048]{1,0:T(8,128)(2,1)S(1)}, bf16[128,2048]{1,0:T(8,128)(2,1)S(1)}, u32[]{:S(2)}, u32[]{:S(2)}) collective-permute-start(bf16[128,2048]{1,0:T(8,128)(2,1)S(1)} %get-tuple-element.31), channel_id=1, source_target_pairs={{0,64},{8,56},{16,80},{24,40},{32,96},{40,24},{48,112},{56,8},{64,... | collective-permute-start | bytes 1572872 | tf_op jit(solution)/shard_map/ppermute | solution.py:231
  31.9 6.8 %collective-permute-done.5 = bf16[128,2048]{1,0:T(8,128)(2,1)S(1)} collective-permute-done((bf16[128,2048]{1,0:T(8,128)(2,1)S(1)}, bf16[128,2048]{1,0:T(8,128)(2,1)S(1)}, u32[]{:S(2)}, u32[]{:S(2)}) %collective-permute-start.5) | collective-permute-done | bytes 524320 | tf_op jit(solution)/shard_map/ppermute | solution.py:231
  38.9 0.8 constant_dynamic-update-slice_fusion.8
  40.2 0.8 constant_dynamic-update-slice_fusion.7
  41.0 5.6 %collective-permute-done.7 = bf16[128,2048]{1,0:T(8,128)(2,1)S(1)} collective-permute-done((bf16[128,2048]{1,0:T(8,128)(2,1)S(1)}, bf16[128,2048]{1,0:T(8,128)(2,1)S(1)}, u32[]{:S(2)}, u32[]{:S(2)}) %collective-permute-start.7) | collective-permute-done | bytes 524320 | tf_op jit(solution)/shard_map/ppermute | solution.py:231
  46.7 0.8 constant_dynamic-update-slice_fusion.6.refs_1_
  47.5 1.6 %collective-permute-start.9 = (bf16[512,2048]{1,0:T(8,128)(2,1)}, bf16[512,2048]{1,0:T(8,128)(2,1)}, u32[]{:S(2)}, u32[]{:S(2)}) collective-permute-start(bf16[512,2048]{1,0:T(8,128)(2,1)} %constant_dynamic-update-slice_fusion.6.refs_1_), channel_id=1, source_target_pairs={{0,48},{8,72},{16,32},{24,88},{32,16},{40,104},{48,0},{56,120},{64... | collective-permute-start | bytes 6291464 | tf_op jit(solution)/shard_map/ppermute | solution.py:231
  49.1 1.9 %collective-permute-start.8 = (bf16[512,2048]{1,0:T(8,128)(2,1)}, bf16[512,2048]{1,0:T(8,128)(2,1)S(1)}, u32[]{:S(2)}, u32[]{:S(2)}) collective-permute-start(bf16[512,2048]{1,0:T(8,128)(2,1)} %constant_dynamic-update-slice_fusion.6.refs_1_), channel_id=1, source_target_pairs={{0,16},{8,200},{16,0},{24,216},{32,48},{40,232},{48,32},{56,248},{... | collective-permute-start | bytes 6291464 | tf_op jit(solution)/shard_map/ppermute | solution.py:231
  51.0 5.9 %collective-permute-start.10 = (bf16[256,128]{1,0:T(8,128)(2,1)S(1)}, bf16[256,128]{1,0:T(8,128)(2,1)S(1)}, u32[]{:S(2)}, u32[]{:S(2)}) collective-permute-start(bf16[256,128]{1,0:T(8,128)(2,1)S(1)} %copy-done.1), channel_id=1, source_target_pairs={{0,8},{8,0},{1,9},{9,1},{2,10},{10,2},{3,11},{11,3},{4,12},{12,4},... | collective-permute-start | bytes 196616 | tf_op jit(solution)/shard_map/ppermute | solution.py:235
  57.0 0.8 collective-permute-done.10.theirs_ref
  57.8 3.0 %couple.1.refs_2_.refs_3_ = bf16[8,2048,256]{2,1,0:T(8,128)(2,1)S(1)} custom-call(bf16[256,128]{1,0:T(8,128)(2,1)S(1)} %collective-permute-done.10.theirs_ref, bf16[256,128]{1,0:T(8,128)(2,1)S(1)} %copy-done.1, bf16[32,2048]{1,0:T(8,128)(2,1)S(1)} %bitcast.18), custom_call_target="tpu_custom_call" | custom-call | flops 268435456 | bytes 9437184 | tf_op jit(solution)/shard_map/couple/pallas_call | solution.py:90
  60.8 7.8 %block.5 = (bf16[8,4,2,64,128]{4,3,2,1,0:T(8,128)(2,1)S(1)}, bf16[8,4,2,64,128]{4,3,2,1,0:T(8,128)(2,1)S(1)}) custom-call(s32[4]{0:T(128)S(1)} %copy-done.2, bf16[512,2048]{1,0:T(8,128)(2,1)} %constant_dynamic-update-slice_fusion.6.refs_1_, bf16[8,2048,256]{2,1,0:T(8,128)(2,1)S(1)} %couple.1.refs_2_.refs_3_), custom_call_target="tpu_custom_call" | custom-call | flops 4294967296 | bytes 10485760 | tf_op jit(solution)/shard_map/block/pallas_call | solution.py:164
  68.6 4.5 %collective-permute-done.9.refs_1_ = bf16[512,2048]{1,0:T(8,128)(2,1)} collective-permute-done((bf16[512,2048]{1,0:T(8,128)(2,1)}, bf16[512,2048]{1,0:T(8,128)(2,1)}, u32[]{:S(2)}, u32[]{:S(2)}) %collective-permute-start.9) | collective-permute-done | bytes 2097184 | tf_op jit(solution)/shard_map/ppermute | solution.py:231
  73.1 2.7 %collective-permute-done.8.refs_1_ = bf16[512,2048]{1,0:T(8,128)(2,1)S(1)} collective-permute-done((bf16[512,2048]{1,0:T(8,128)(2,1)}, bf16[512,2048]{1,0:T(8,128)(2,1)S(1)}, u32[]{:S(2)}, u32[]{:S(2)}) %collective-permute-start.8) | collective-permute-done | bytes 2097184 | tf_op jit(solution)/shard_map/ppermute | solution.py:231
  75.9 1.3 %slice.7 = bf16[256,2048]{1,0:T(8,128)(2,1)S(1)} slice(bf16[512,2048]{1,0:T(8,128)(2,1)} %collective-permute-done.9.refs_1_), slice={[256:512], [0:2048]} | slice | bytes 2097152 | tf_op jit(solution)/shard_map/slice | solution.py:270
  77.2 2.2 %collective-permute-start.12 = (bf16[256,2048]{1,0:T(8,128)(2,1)S(1)}, bf16[256,2048]{1,0:T(8,128)(2,1)S(1)}, u32[]{:S(2)}, u32[]{:S(2)}) collective-permute-start(bf16[256,2048]{1,0:T(8,128)(2,1)S(1)} %slice.7), channel_id=1, source_target_pairs={{0,16},{8,200},{16,0},{24,216},{32,48},{40,232},{48,32},{56,248},{... | collective-permute-start | bytes 3145736 | tf_op jit(solution)/shard_map/ppermute | solution.py:231
  79.4 7.8 %block.7 = (bf16[8,4,2,64,128]{4,3,2,1,0:T(8,128)(2,1)S(1)}, bf16[8,4,2,64,128]{4,3,2,1,0:T(8,128)(2,1)S(1)}) custom-call(s32[4]{0:T(128)S(1)} %copy-done.2, bf16[512,2048]{1,0:T(8,128)(2,1)} %collective-permute-done.9.refs_1_, bf16[8,2048,256]{2,1,0:T(8,128)(2,1)S(1)} %couple.1.refs_2_.refs_3_), custom_call_target="tpu_custom_call" | custom-call | flops 4294967296 | bytes 10485760 | tf_op jit(solution)/shard_map/block/pallas_call | solution.py:164
  87.3 7.0 %collective-permute-start.15 = (bf16[8,4,2,64,128]{4,3,2,1,0:T(8,128)(2,1)S(1)}, bf16[8,4,2,64,128]{4,3,2,1,0:T(8,128)(2,1)S(1)}, u32[]{:S(2)}, u32[]{:S(2)}) collective-permute-start(bf16[8,4,2,64,128]{4,3,2,1,0:T(8,128)(2,1)S(1)} %get-tuple-element.30), channel_id=1, source_target_pairs={{0,8},{8,0},{1,9},{9,1},{2,10},{10,2},{3,11},{11,3},{4,12},{12,4},... | collective-permute-start | bytes 3145736 | tf_op jit(solution)/shard_map/ppermute | solution.py:235
  94.2 6.1 %block.6 = (bf16[8,4,2,64,128]{4,3,2,1,0:T(8,128)(2,1)S(1)}, bf16[8,4,2,64,128]{4,3,2,1,0:T(8,128)(2,1)S(1)}) custom-call(s32[4]{0:T(128)S(1)} %copy-done.2, bf16[512,2048]{1,0:T(8,128)(2,1)S(1)} %collective-permute-done.8.refs_1_, bf16[8,2048,256]{2,1,0:T(8,128)(2,1)S(1)} %couple.1.refs_2_.refs_3_), custom_call_target="tpu_custom_call" | custom-call | flops 4294967296 | bytes 10485760 | tf_op jit(solution)/shard_map/block/pallas_call | solution.py:164
  100.9 3.3 %block.9 = bf16[8,4,2,64,128]{4,3,2,1,0:T(8,128)(2,1)S(1)} custom-call(s32[4]{0:T(128)S(1)} %copy-done.2, bf16[256,2048]{1,0:T(8,128)(2,1)S(1)} %collective-permute-done.11.refs_1_, bf16[256,2048]{1,0:T(8,128)(2,1)S(1)} %collective-permute-done.12.refs_2_, bf16[8,2048,256]{2,1,0:T(8,128)(2,1)S(1)} %couple.1.refs_2_.refs_3_), custom_call_target="tpu_custom_call" | custom-call | flops 2147483648 | bytes 10485760 | tf_op jit(solution)/shard_map/block/pallas_call | solution.py:164
  104.4 3.3 %block.8.refs_3_ = bf16[8,4,2,64,128]{4,3,2,1,0:T(8,128)(2,1)S(1)} custom-call(s32[4]{0:T(128)S(1)} %copy-done.2, bf16[256,2048]{1,0:T(8,128)(2,1)S(1)} %collective-permute-done.11.refs_1_, bf16[256,2048]{1,0:T(8,128)(2,1)S(1)} %collective-permute-done.12.refs_2_, bf16[8,2048,256]{2,1,0:T(8,128)(2,1)S(1)} %couple.1.refs_2_.refs_3_), custom_call_target="tpu_custom_call" | custom-call | flops 2147483648 | bytes 10485760 | tf_op jit(solution)/shard_map/block/pallas_call | solution.py:164
  107.8 3.7 %add.11 = bf16[8,16,2,64,128]{4,3,2,1,0:T(8,128)(2,1)} custom-call(s32[4]{0:T(128)S(1)} %copy-done.2, bf16[8,4,2,64,128]{4,3,2,1,0:T(8,128)(2,1)S(1)} %get-tuple-element.23.refs_0_, bf16[8,4,2,64,128]{4,3,2,1,0:T(8,128)(2,1)S(1)} %get-tuple-element.25.refs_1_, bf16[8,4,2,64,128]{4,3,2,1,0:T(8,128)(2,1)S(1)} %get-tuple-element.27.refs_2_, ...), custom_call_target="tpu_custom_call" | custom-call | flops 10000000 | bytes 13631488 | tf_op jit(solution)/shard_map/add/pallas_call | solution.py:199
  (34 shorter events, 6.5 us)
Async XLA Ops:
  0.0 56.9 %copy-start = (bf16[1024,128]{1,0:T(8,128)(2,1)S(1)}, bf16[1024,128]{1,0:T(8,128)(2,1)}, u32[]{:S(2)}) copy-start(bf16[1024,128]{1,0:T(8,128)(2,1)} %param.16) | copy-start | bytes 786436
  3.9 4.7 %collective-permute-start = (bf16[8,2048]{1,0:T(8,128)(2,1)}, bf16[8,2048]{1,0:T(8,128)(2,1)S(1)}, u32[]{:S(2)}, u32[]{:S(2)}) collective-permute-start(bf16[8,2048]{1,0:T(8,128)(2,1)} %get-tuple-element.19), channel_id=1, source_target_pairs={{0,8},{8,0},{1,9},{9,1},{2,10},{10,2},{3,11},{11,3},{4,12},{12,4},... | collective-permute-start | bytes 98312 | tf_op jit(solution)/shard_map/ppermute | solution.py:235
  9.4 5.5 %collective-permute-start.1 = (bf16[16,2048]{1,0:T(8,128)(2,1)S(1)}, bf16[16,2048]{1,0:T(8,128)(2,1)S(1)}, u32[]{:S(2)}, u32[]{:S(2)}) collective-permute-start(bf16[16,2048]{1,0:T(8,128)(2,1)S(1)} %pad_maximum_fusion.1), channel_id=1, source_target_pairs={{0,1},{1,0},{2,3},{3,2},{4,5},{5,4},{6,7},{7,6},{8,15},{9,10},{10,... | collective-permute-start | bytes 196616 | tf_op jit(solution)/shard_map/ppermute | solution.py:220
  15.7 4.2 %collective-permute-start.2 = (bf16[32,2048]{1,0:T(8,128)(2,1)S(1)}, bf16[32,2048]{1,0:T(8,128)(2,1)S(1)}, u32[]{:S(2)}, u32[]{:S(2)}) collective-permute-start(bf16[32,2048]{1,0:T(8,128)(2,1)S(1)} %pad_maximum_fusion), channel_id=1, source_target_pairs={{0,7},{1,2},{2,1},{3,4},{4,3},{5,6},{6,5},{7,0},{8,9},{9,8},{10,11... | collective-permute-start | bytes 393224 | tf_op jit(solution)/shard_map/ppermute | solution.py:220
  19.9 5.0 %collective-permute-start.3 = (bf16[32,2048]{1,0:T(8,128)(2,1)S(1)}, bf16[32,2048]{1,0:T(8,128)(2,1)S(1)}, u32[]{:S(2)}, u32[]{:S(2)}) collective-permute-start(bf16[32,2048]{1,0:T(8,128)(2,1)S(1)} %collective-permute-done.2), channel_id=1, source_target_pairs={{0,1},{1,0},{2,3},{3,2},{4,5},{5,4},{6,7},{7,6},{8,15},{9,10},{10,... | collective-permute-start | bytes 393224 | tf_op jit(solution)/shard_map/ppermute | solution.py:220
  22.2 28.7 %copy-start.1 = (bf16[256,128]{1,0:T(8,128)(2,1)S(1)}, bf16[256,128]{1,0:T(8,128)(2,1)}, u32[]{:S(2)}) copy-start(bf16[256,128]{1,0:T(8,128)(2,1)} %get-tuple-element.20.mine_ref) | copy-start | bytes 196612
  24.9 3.8 %collective-permute-start.4 = (bf16[32,2048]{1,0:T(8,128)(2,1)S(1)}, bf16[32,2048]{1,0:T(8,128)(2,1)S(1)}, u32[]{:S(2)}, u32[]{:S(2)}) collective-permute-start(bf16[32,2048]{1,0:T(8,128)(2,1)S(1)} %collective-permute-done.3), channel_id=1, source_target_pairs={{0,7},{1,2},{2,1},{3,4},{4,3},{5,6},{6,5},{7,0},{8,9},{9,8},{10,11... | collective-permute-start | bytes 393224 | tf_op jit(solution)/shard_map/ppermute | solution.py:220
  29.4 9.2 %collective-permute-start.5 = (bf16[128,2048]{1,0:T(8,128)(2,1)S(1)}, bf16[128,2048]{1,0:T(8,128)(2,1)S(1)}, u32[]{:S(2)}, u32[]{:S(2)}) collective-permute-start(bf16[128,2048]{1,0:T(8,128)(2,1)S(1)} %get-tuple-element.31), channel_id=1, source_target_pairs={{0,64},{8,56},{16,80},{24,40},{32,96},{40,24},{48,112},{56,8},{64,... | collective-permute-start | bytes 1572872 | tf_op jit(solution)/shard_map/ppermute | solution.py:231
  31.9 8.3 %collective-permute-start.6 = (bf16[128,2048]{1,0:T(8,128)(2,1)S(1)}, bf16[128,2048]{1,0:T(8,128)(2,1)S(1)}, u32[]{:S(2)}, u32[]{:S(2)}) collective-permute-start(bf16[128,2048]{1,0:T(8,128)(2,1)S(1)} %get-tuple-element.31), channel_id=1, source_target_pairs={{0,192},{8,24},{16,208},{24,8},{32,224},{40,56},{48,240},{56,40},{... | collective-permute-start | bytes 1572872 | tf_op jit(solution)/shard_map/ppermute | solution.py:231
  38.6 8.0 %collective-permute-start.7 = (bf16[128,2048]{1,0:T(8,128)(2,1)S(1)}, bf16[128,2048]{1,0:T(8,128)(2,1)S(1)}, u32[]{:S(2)}, u32[]{:S(2)}) collective-permute-start(bf16[128,2048]{1,0:T(8,128)(2,1)S(1)} %collective-permute-done.5), channel_id=1, source_target_pairs={{0,192},{8,24},{16,208},{24,8},{32,224},{40,56},{48,240},{56,40},{... | collective-permute-start | bytes 1572872 | tf_op jit(solution)/shard_map/ppermute | solution.py:231
  47.5 25.6 %collective-permute-start.9 = (bf16[512,2048]{1,0:T(8,128)(2,1)}, bf16[512,2048]{1,0:T(8,128)(2,1)}, u32[]{:S(2)}, u32[]{:S(2)}) collective-permute-start(bf16[512,2048]{1,0:T(8,128)(2,1)} %constant_dynamic-update-slice_fusion.6.refs_1_), channel_id=1, source_target_pairs={{0,48},{8,72},{16,32},{24,88},{32,16},{40,104},{48,0},{56,120},{64... | collective-permute-start | bytes 6291464 | tf_op jit(solution)/shard_map/ppermute | solution.py:231
  49.1 26.7 %collective-permute-start.8 = (bf16[512,2048]{1,0:T(8,128)(2,1)}, bf16[512,2048]{1,0:T(8,128)(2,1)S(1)}, u32[]{:S(2)}, u32[]{:S(2)}) collective-permute-start(bf16[512,2048]{1,0:T(8,128)(2,1)} %constant_dynamic-update-slice_fusion.6.refs_1_), channel_id=1, source_target_pairs={{0,16},{8,200},{16,0},{24,216},{32,48},{40,232},{48,32},{56,248},{... | collective-permute-start | bytes 6291464 | tf_op jit(solution)/shard_map/ppermute | solution.py:231
  51.0 6.8 %collective-permute-start.10 = (bf16[256,128]{1,0:T(8,128)(2,1)S(1)}, bf16[256,128]{1,0:T(8,128)(2,1)S(1)}, u32[]{:S(2)}, u32[]{:S(2)}) collective-permute-start(bf16[256,128]{1,0:T(8,128)(2,1)S(1)} %copy-done.1), channel_id=1, source_target_pairs={{0,8},{8,0},{1,9},{9,1},{2,10},{10,2},{3,11},{11,3},{4,12},{12,4},... | collective-permute-start | bytes 196616 | tf_op jit(solution)/shard_map/ppermute | solution.py:235
  57.8 3.0 %copy-start.2 = (s32[4]{0:T(128)S(1)}, s32[4]{0:T(128)}, u32[]{:S(2)}) copy-start(s32[4]{0:T(128)} %pad_add_fusion.core_ref.refs_0_.at_ref) | copy-start | bytes 52
  77.2 23.7 %collective-permute-start.12 = (bf16[256,2048]{1,0:T(8,128)(2,1)S(1)}, bf16[256,2048]{1,0:T(8,128)(2,1)S(1)}, u32[]{:S(2)}, u32[]{:S(2)}) collective-permute-start(bf16[256,2048]{1,0:T(8,128)(2,1)S(1)} %slice.7), channel_id=1, source_target_pairs={{0,16},{8,200},{16,0},{24,216},{32,48},{40,232},{48,32},{56,248},{... | collective-permute-start | bytes 3145736 | tf_op jit(solution)/shard_map/ppermute | solution.py:231
  79.4 21.5 %collective-permute-start.11 = (bf16[256,2048]{1,0:T(8,128)(2,1)S(1)}, bf16[256,2048]{1,0:T(8,128)(2,1)S(1)}, u32[]{:S(2)}, u32[]{:S(2)}) collective-permute-start(bf16[256,2048]{1,0:T(8,128)(2,1)S(1)} %slice.6), channel_id=1, source_target_pairs={{0,48},{8,72},{16,32},{24,88},{32,16},{40,104},{48,0},{56,120},{64... | collective-permute-start | bytes 3145736 | tf_op jit(solution)/shard_map/ppermute | solution.py:231
  87.3 20.4 %collective-permute-start.15 = (bf16[8,4,2,64,128]{4,3,2,1,0:T(8,128)(2,1)S(1)}, bf16[8,4,2,64,128]{4,3,2,1,0:T(8,128)(2,1)S(1)}, u32[]{:S(2)}, u32[]{:S(2)}) collective-permute-start(bf16[8,4,2,64,128]{4,3,2,1,0:T(8,128)(2,1)S(1)} %get-tuple-element.30), channel_id=1, source_target_pairs={{0,8},{8,0},{1,9},{9,1},{2,10},{10,2},{3,11},{11,3},{4,12},{12,4},... | collective-permute-start | bytes 3145736 | tf_op jit(solution)/shard_map/ppermute | solution.py:235
  100.3 7.4 %collective-permute-start.14 = (bf16[8,4,2,64,128]{4,3,2,1,0:T(8,128)(2,1)S(1)}, bf16[8,4,2,64,128]{4,3,2,1,0:T(8,128)(2,1)S(1)}, u32[]{:S(2)}, u32[]{:S(2)}) collective-permute-start(bf16[8,4,2,64,128]{4,3,2,1,0:T(8,128)(2,1)S(1)} %get-tuple-element.29), channel_id=1, source_target_pairs={{0,8},{8,0},{1,9},{9,1},{2,10},{10,2},{3,11},{11,3},{4,12},{12,4},... | collective-permute-start | bytes 3145736 | tf_op jit(solution)/shard_map/ppermute | solution.py:235
  100.4 7.3 %collective-permute-start.13 = (bf16[8,4,2,64,128]{4,3,2,1,0:T(8,128)(2,1)S(1)}, bf16[8,4,2,64,128]{4,3,2,1,0:T(8,128)(2,1)S(1)}, u32[]{:S(2)}, u32[]{:S(2)}) collective-permute-start(bf16[8,4,2,64,128]{4,3,2,1,0:T(8,128)(2,1)S(1)} %get-tuple-element.28), channel_id=1, source_target_pairs={{0,8},{8,0},{1,9},{9,1},{2,10},{10,2},{3,11},{11,3},{4,12},{12,4},... | collective-permute-start | bytes 3145736 | tf_op jit(solution)/shard_map/ppermute | solution.py:235
  104.2 3.5 %copy-start.3 = (f32[128]{0:T(128)S(1)}, f32[128]{0:T(128)}, u32[]{:S(2)}) copy-start(f32[128]{0:T(128)} %param.17) | copy-start | bytes 1540
  104.2 3.5 %collective-permute-start.16 = (bf16[8,4,2,64,128]{4,3,2,1,0:T(8,128)(2,1)S(1)}, bf16[8,4,2,64,128]{4,3,2,1,0:T(8,128)(2,1)S(1)}, u32[]{:S(2)}, u32[]{:S(2)}) collective-permute-start(bf16[8,4,2,64,128]{4,3,2,1,0:T(8,128)(2,1)S(1)} %block.9), channel_id=1, source_target_pairs={{0,8},{8,0},{1,9},{9,1},{2,10},{10,2},{3,11},{11,3},{4,12},{12,4},... | collective-permute-start | bytes 3145736 | tf_op jit(solution)/shard_map/ppermute | solution.py:235

commit v3 on v2

--- a/solution.py
+++ b/solution.py
@@ -119,64 +119,105 @@
     return (own + jnp.where((own + core) % 2 == 0, step, -step)) & 3
 
 
-def block_kernel(count, at_ref, *refs):
-    r_refs, t_ref, o_refs, sum_s = refs[:count], refs[count], refs[count + 1:-1], refs[-1]
+def half_kernel(count, *refs):
+    r_refs, t_ref, o_ref = refs[:count], refs[count], refs[count + 1]
+    for n in range(2):
+        for k in range(count):
+            o_ref[n, k * BLOCK // 2:(k + 1) * BLOCK // 2, :] = jnp.dot(
+                r_refs[k][...], t_ref[n], preferred_element_type=F32)
+
+
+def half(pieces, t):
+    count = len(pieces)
+    rows = count * BLOCK // 2
+    return pl.pallas_call(
+        lambda *refs: half_kernel(count, *refs),
+        grid=(4,),
+        in_specs=[pl.BlockSpec((BLOCK // 2, HALF), lambda n: (0, 0))] * count
+        + [pl.BlockSpec((2, HALF, 2 * CZ), lambda n: (n, 0, 0))],
+        out_specs=pl.BlockSpec((2, rows, 2 * CZ), lambda n: (n, 0, 0)),
+        out_shape=jax.ShapeDtypeStruct((LOCAL, rows, 2 * CZ), F32),
+        compiler_params=pltpu.CompilerParams(vmem_limit_bytes=24 * MIB),
+        cost_estimate=pl.CostEstimate(flops=2 * rows * HALF * 2048, bytes_accessed=10 * MIB, transcendentals=0),
+        name="half",
+    )(*pieces, t)
+
+
+def block_kernel(first, count, ready, at_ref, *refs):
+    given = count if ready else 2 * count
+    r_refs, refs = refs[:given], refs[given:]
+    if ready:
+        done_ref, refs = refs[0], refs[1:]
+    t_ref, o_refs, sum_s, sem = refs[0], refs[1:-2], refs[-2], refs[-1]
+    side_rows = BLOCK // 2
+    copies = []
+    if ready:
+        pair = pl.ds((first + pl.program_id(0)) * 2, 2)
+        for k in range(count):
+            copies.append(pltpu.make_async_copy(
+                done_ref.at[pair, pl.ds(k * side_rows, side_rows)], sum_s.at[:, pl.ds(k * BLOCK, side_rows)], sem.at[k]))
+    for copy in copies:
+        copy.start()
     core, z = at_ref[0], at_ref[3]
     minor = jnp.where(core == 0, at_ref[1], at_ref[2])
     pm = [place4(minor, core, t) for t in range(4)]
     pz = [place8(z, core, t) for t in range(8)]
-    rows = BLOCK // count
+    zrow = [(p >> 2) * side_rows + (p & 3) * UNIT for p in pz]
     for n in range(2):
+        for k in range(given):
+            row = k * BLOCK + side_rows if ready else k * side_rows
+            sum_s[n, row:row + side_rows, :] = jnp.dot(r_refs[k][...], t_ref[n], preferred_element_type=F32)
+    for copy in copies:
+        copy.wait()
+
+    def store(outs):
         for k in range(count):
-            sum_s[n, k * rows:(k + 1) * rows, :] = jnp.dot(r_refs[k][...], t_ref[n], preferred_element_type=F32)
-
-    def store(o_ref):
-        for n in range(2):
-            for tm in range(4):
-                for c in range(2):
-                    side = jnp.where(core == c, 0, LOCAL)
-                    for tz in range(0, 8, 2):
-                        both = [
-                            sum_s[n, pl.ds(pl.multiple_of((pm[tm] * 8 + pz[tz + d]) * UNIT + side, LOCAL), LOCAL), :]
-                            for d in range(2)
-                        ]
-                        value = jnp.concatenate(both, axis=0).astype(BF16)
-                        for i in range(2):
-                            o_ref[n * 2 + i, tm, c, tz * LOCAL:(tz + 2) * LOCAL, :] = value[:, i * CZ:(i + 1) * CZ]
-
-    if len(o_refs) == 1:
-        store(o_refs[0])
+            for n in range(2):
+                for tm in range(4):
+                    for c in range(2):
+                        side = jnp.where(core == c, 0, LOCAL)
+                        for tz in range(0, 8, 2):
+                            both = []
+                            for d in range(2):
+                                row = zrow[tz + d] + pm[tm] * 4 * UNIT + side + k * BLOCK
+                                both.append(sum_s[n, pl.ds(pl.multiple_of(row, LOCAL), LOCAL), :])
+                            value = jnp.concatenate(both, axis=0).astype(BF16)
+                            for i in range(2):
+                                outs[k][n * 2 + i, tm, c, tz * LOCAL:(tz + 2) * LOCAL, :] = value[:, i * CZ:(i + 1) * CZ]
+
+    if len(o_refs) == count:
+        store(o_refs)
     else:
-        pl.when(pl.program_id(0) < 2)(lambda: store(o_refs[0]))
-        pl.when(pl.program_id(0) >= 2)(lambda: store(o_refs[1]))
-
-
-def block(at, pieces, t, part):
-    count = len(pieces)
-    rows = BLOCK // count
+        pl.when(pl.program_id(0) < 2)(lambda: store(o_refs[:count]))
+        pl.when(pl.program_id(0) >= 2)(lambda: store(o_refs[count:]))
+
+
+def block(at, pieces, ready, t, part):
+    count = len(pieces) // (2 if ready is None else 1)
     first = 2 if part == 1 else 0
     shape = (LOCAL, 4, 2, 64, CZ)
     spec = lambda where: pl.BlockSpec((4,) + shape[1:], lambda n, at: (where(n), 0, 0, 0, 0))
     if part is None:
-        out_specs = [spec(lambda n: jnp.minimum(n, 1)), spec(lambda n: jnp.maximum(n - 2, 0))]
+        out_specs = [spec(lambda n: jnp.minimum(n, 1))] * count + [spec(lambda n: jnp.maximum(n - 2, 0))] * count
     else:
-        out_specs = [spec(lambda n: n)]
-    return pl.pallas_call(
-        lambda *refs: block_kernel(count, *refs),
+        out_specs = [spec(lambda n: n)] * count
+    return pl.pallas_call(
+        lambda *refs: block_kernel(first, count, ready is not None, *refs),
         grid_spec=pltpu.PrefetchScalarGridSpec(
             num_scalar_prefetch=1,
             grid=(4 if part is None else 2,),
-            in_specs=[pl.BlockSpec((rows, HALF), lambda n, at: (0, 0))] * count
+            in_specs=[pl.BlockSpec((BLOCK // 2, HALF), lambda n, at: (0, 0))] * len(pieces)
+            + ([] if ready is None else [pl.BlockSpec(memory_space=pl.ANY)])
             + [pl.BlockSpec((2, HALF, 2 * CZ), lambda n, at: (first + n, 0, 0))],
             out_specs=out_specs,
-            scratch_shapes=[pltpu.VMEM((2, BLOCK, 2 * CZ), F32)],
+            scratch_shapes=[pltpu.VMEM((2, count * BLOCK, 2 * CZ), F32), pltpu.SemaphoreType.DMA((2,))],
         ),
         out_shape=[jax.ShapeDtypeStruct(shape, BF16)] * len(out_specs),
         compiler_params=pltpu.CompilerParams(vmem_limit_bytes=24 * MIB),
-        cost_estimate=pl.CostEstimate(flops=2 * BLOCK * HALF * 1024 * len(out_specs), bytes_accessed=10 * MIB,
-                                      transcendentals=0),
+        cost_estimate=pl.CostEstimate(flops=BLOCK * len(pieces) * HALF * (2048 if part is None else 1024),
+                                      bytes_accessed=10 * MIB, transcendentals=0),
         name="block",
-    )(at, *pieces, t)
+    )(at, *pieces, *([] if ready is None else [ready]), t)
 
 
 def add_kernel(at_ref, *refs):
@@ -248,30 +289,40 @@
     at = jnp.stack([core, lax.axis_index("y"), lax.axis_index("x"), lax.axis_index("z")]).astype(jnp.int32)
     keep, give, lt = project(at, msa, gain, shift, w1, b1, w2, b2)
     r = join(keep, swap(give))
-    lt_sibling = swap(lt)
     w = lax.dynamic_slice_in_dim(couple_map.reshape(CH, CH, CZ), core * EH, EH, axis=1).reshape(CH, EH * CZ)
 
     z1 = join(r, along_z(r, 0))
     z2 = along_z(z1, 1)
+    h0 = join(z1, z2)
     z3 = along_z(z2, 2)
-    z4 = along_z(z3, 3)
-    r = join(z1, z2, z3, z4)
-
-    m1 = along_plane(r, False, 0)
-    m2 = along_plane(r, False, 1)
-    m3 = along_plane(m1, False, 1)
+    m1_0 = along_plane(h0, False, 0)
+    m2_0 = along_plane(h0, False, 1)
+    z4, lt = together(along_z(z3, 3), lt)
+    m3_0 = along_plane(m1_0, False, 1)
+    h1, lt_sibling = together(join(z3, z4), swap(lt))
     t = couple(lt_sibling, lt, w)
-    b0 = join(r, m1, m2, m3)
-
-    b1 = along_plane(b0, True, 0)
-    b2 = along_plane(b0, True, 1)
-    p0, q0 = block(at, [b0], t, None)
-    b1, b2, p0, q0 = together(b1, b2, p0, q0)
-    b3 = along_plane(b1[:BLOCK // 2], True, 1), along_plane(b2[BLOCK // 2:], True, 0)
-    p1, q1 = block(at, [b1], t, None)
-    p2, q2 = block(at, [b2], t, None)
-    p3, = block(at, b3, t, 0)
-    q3, = block(at, b3, t, 1)
+    m1_1 = along_plane(h1, False, 0)
+    m2_1 = along_plane(h1, False, 1)
+    m1_1, t = together(m1_1, t)
+    m3_1 = along_plane(m1_1, False, 1)
+    b0_0 = join(h0, m1_0, m2_0, m3_0)
+    b1_0 = along_plane(b0_0, True, 0)
+    b2_0 = along_plane(b0_0, True, 1)
+    b0_1 = join(h1, m1_1, m2_1, m3_1)
+    b1_1 = along_plane(b0_1, True, 0)
+    b2_1 = along_plane(b0_1, True, 1)
+    p0, q0 = block(at, [b0_0, b0_1], None, t, None)
+    b1_0, b2_0, p0, q0 = together(b1_0, b2_0, p0, q0)
+    b3_0 = along_plane(b1_0, True, 1)
+    d12 = half([b1_0, b2_0], t)
+    b2_1, d12 = together(b2_1, d12)
+    b3_1 = along_plane(b2_1, True, 0)
+    p1, p2, q1, q2 = block(at, [b1_1, b2_1], d12, t, None)
+    b3_0, p1 = together(b3_0, p1)
+    d3 = half([b3_0], t)
+    b3_1, d3 = together(b3_1, d3)
+    p3, = block(at, [b3_1], d3, t, 0)
+    q3, = block(at, [b3_1], d3, t, 1)
     theirs = [swap(p) for p in (p0, p1, p2, p3)]
     mine = [q0, q1, q2, q3]
     return add(at, mine, theirs, couple_offset).reshape(LOCAL, 16 * 2 * 64, CZ)

time: 112 us -> 101 us (0.902)
  waiting for transfers between devices: 30.5 us -> 22.4 us
  local copies, waits for them, and re-layouts: 8.6 us -> 1.82 us
  starting transfers between devices: 31.8 us -> 38.2 us
  Pallas kernels: 38.2 us -> 35.6 us
    ppermute x7 -> x12, waiting for transfers between devices: 20 us -> 13.2 us  [along_plane(): return lax.ppermute(v, ('y', 'x', 'c'), pairs)]
    unnamed x16 -> x17, local copies, waits for them, and re-layouts: 5.7 us -> 1.76 us
    ppermute x6, starting transfers between devices: 17 us -> 20.2 us  [swap(): return lax.ppermute(v, 'c', [(0, 1), (1, 0)])]
    ppermute x7 -> x12, starting transfers between devices: 8.51 us -> 11.3 us  [along_plane(): return lax.ppermute(v, ('y', 'x', 'c'), pairs)]
    pallas_call x5 -> x6, Pallas kernels: 28.3 us -> 25.7 us  [the longest x4 17.8 us: block(): pl.pallas_call(lambda *refs: block_kernel(first, count, ready is not None...]
    ppermute x4, waiting for transfers between devices: 9.61 us -> 8.09 us  [along_z(): lax.ppermute(v, ('c', 'z'), [(c * 8 + k, c * 8 + partner(k, 8, c, step))...]
    concatenate x2 -> x3, local copies, waits for them, and re-layouts: 1.5 us -> 0.06 us  [join(): return jnp.concatenate(blocks, axis=0)]
    slice x2 -> x0, local copies, waits for them, and re-layouts: 1.39 us -> none  [the longest x1 1.32 us: per_device(): b2[BLOCK // 2:]]
  transfers between devices with their start and end apart: 17 -> 22, of which waited for: 10 -> 9; matrix products, arithmetic and copies ran while one was open for 5% -> 1% of each run, Pallas kernels for 28% -> 29%
where the time goes in v3:
time: 101 us; the launch traced here: 100 us
  starting transfers between devices  38.2 us (38%)
  Pallas kernels  35.6 us (35%)
  waiting for transfers between devices  22.4 us (22%)
  other arithmetic  2.2 us (2%)
  local copies, waits for them, and re-layouts  1.82 us (2%)
    ppermute x6, starting transfers between devices, swap(): return lax.ppermute(v, 'c', [(0, 1), (1, 0)])  20.2 us
    pallas_call x4, Pallas kernels, block(): pl.pallas_call(lambda *refs: block_kernel(first, count, ready is not None...  17.8 us
    ppermute x12, waiting for transfers between devices, along_plane(): return lax.ppermute(v, ('y', 'x', 'c'), pairs)  13.2 us
    ppermute x12, starting transfers between devices, along_plane(): return lax.ppermute(v, ('y', 'x', 'c'), pairs)  11.3 us
    ppermute x4, waiting for transfers between devices, along_z(): lax.ppermute(v, ('c', 'z'), [(c * 8 + k, c * 8 + partner(k, 8, c, step))...  8.09 us
    pallas_call x2, Pallas kernels, half(): pl.pallas_call(lambda *refs: half_kernel(count, *refs), grid=(4,), in_spe...  7.9 us
    ppermute x4, starting transfers between devices, along_z(): lax.ppermute(v, ('c', 'z'), [(c * 8 + k, c * 8 + partner(k, 8, c, step))...  6.61 us
    pallas_call x1, Pallas kernels, add(): pl.pallas_call(add_kernel, grid_spec=pltpu.PrefetchScalarGridSpec(num_sca...  3.69 us
  transfers between devices with their start and end apart: 22, of which 9 were waited for; matrix products, arithmetic and copies ran while one was open for 1% of the time, Pallas kernels for 29%

profile of v3, /device:TPU:1, one launch (start us, length us, event | category | flops | bytes accessed | tf_op | source)
XLA Modules:
  0.0 100.5 jit_solution(17646133067213377623)
XLA Ops:
  0.7 3.3 %project.1 = (bf16[8,2048]{1,0:T(8,128)(2,1)}, bf16[8,2048]{1,0:T(8,128)(2,1)}, bf16[256,128]{1,0:T(8,128)(2,1)}) custom-call(s32[4]{0:T(128)} %pad_add_fusion.core_ref.refs_0_.at_ref, bf16[128,8,256]{2,1,0:T(8,128)(2,1)} %msa_in.1, f32[1,256]{1,0:T(1,128)} %bitcast.23, f32[1,256]{1,0:T(1,128)} %bitcast.24, bf16[32,256]{1,0:T(8,128)(2,1)} %bitcast.21, ...), custom_call_target="tpu_custom_call" | custom-call | tf_op jit(solution)/shard_map/project/pallas_call | solution.py:45
  3.9 3.3 %collective-permute-start = (bf16[8,2048]{1,0:T(8,128)(2,1)}, bf16[8,2048]{1,0:T(8,128)(2,1)S(1)}, u32[]{:S(2)}, u32[]{:S(2)}) collective-permute-start(bf16[8,2048]{1,0:T(8,128)(2,1)} %get-tuple-element.31), channel_id=1, source_target_pairs={{0,8},{8,0},{1,9},{9,1},{2,10},{10,2},{3,11},{11,3},{4,12},{12,4},... | collective-permute-start | bytes 98312 | tf_op jit(solution)/shard_map/ppermute | solution.py:276
  7.2 1.1 %collective-permute-done = bf16[8,2048]{1,0:T(8,128)(2,1)S(1)} collective-permute-done((bf16[8,2048]{1,0:T(8,128)(2,1)}, bf16[8,2048]{1,0:T(8,128)(2,1)S(1)}, u32[]{:S(2)}, u32[]{:S(2)}) %collective-permute-start) | collective-permute-done | bytes 32800 | tf_op jit(solution)/shard_map/ppermute | solution.py:276
  9.1 3.8 %collective-permute-start.1 = (bf16[16,2048]{1,0:T(8,128)(2,1)S(1)}, bf16[16,2048]{1,0:T(8,128)(2,1)S(1)}, u32[]{:S(2)}, u32[]{:S(2)}) collective-permute-start(bf16[16,2048]{1,0:T(8,128)(2,1)S(1)} %pad_maximum_fusion.2), channel_id=1, source_target_pairs={{0,1},{1,0},{2,3},{3,2},{4,5},{5,4},{6,7},{7,6},{8,15},{9,10},{10,... | collective-permute-start | bytes 196616 | tf_op jit(solution)/shard_map/ppermute | solution.py:261
  13.7 0.9 collective-permute-done.1
  15.5 3.8 %collective-permute-done.2 = bf16[32,2048]{1,0:T(8,128)(2,1)S(1)} collective-permute-done((bf16[32,2048]{1,0:T(8,128)(2,1)S(1)}, bf16[32,2048]{1,0:T(8,128)(2,1)S(1)}, u32[]{:S(2)}, u32[]{:S(2)}) %collective-permute-start.2) | collective-permute-done | bytes 131104 | tf_op jit(solution)/shard_map/ppermute | solution.py:261
  19.2 2.7 %collective-permute-start.8 = (bf16[32,2048]{1,0:T(8,128)(2,1)S(1)}, bf16[32,2048]{1,0:T(8,128)(2,1)S(1)}, u32[]{:S(2)}, u32[]{:S(2)}) collective-permute-start(bf16[32,2048]{1,0:T(8,128)(2,1)S(1)} %collective-permute-done.2), channel_id=1, source_target_pairs={{0,1},{1,0},{2,3},{3,2},{4,5},{5,4},{6,7},{7,6},{8,15},{9,10},{10,... | collective-permute-start | bytes 393224 | tf_op jit(solution)/shard_map/ppermute | solution.py:261
  21.9 2.3 %collective-permute-done.8 = bf16[32,2048]{1,0:T(8,128)(2,1)S(1)} collective-permute-done((bf16[32,2048]{1,0:T(8,128)(2,1)S(1)}, bf16[32,2048]{1,0:T(8,128)(2,1)S(1)}, u32[]{:S(2)}, u32[]{:S(2)}) %collective-permute-start.8) | collective-permute-done | bytes 131104 | tf_op jit(solution)/shard_map/ppermute | solution.py:261
  24.3 2.6 %collective-permute-start.3 = (bf16[64,2048]{1,0:T(8,128)(2,1)S(1)}, bf16[64,2048]{1,0:T(8,128)(2,1)S(1)}, u32[]{:S(2)}, u32[]{:S(2)}) collective-permute-start(bf16[64,2048]{1,0:T(8,128)(2,1)S(1)} %get-tuple-element.55), channel_id=1, source_target_pairs={{0,64},{8,56},{16,80},{24,40},{32,96},{40,24},{48,112},{56,8},{64,... | collective-permute-start | bytes 786440 | tf_op jit(solution)/shard_map/ppermute | solution.py:272
  27.0 1.1 %collective-permute-done.9 = bf16[32,2048]{1,0:T(8,128)(2,1)S(1)} collective-permute-done((bf16[32,2048]{1,0:T(8,128)(2,1)S(1)}, bf16[32,2048]{1,0:T(8,128)(2,1)S(1)}, u32[]{:S(2)}, u32[]{:S(2)}) %collective-permute-start.9) | collective-permute-done | bytes 131104 | tf_op jit(solution)/shard_map/ppermute | solution.py:261
  28.1 5.7 %collective-permute-start.10 = (bf16[256,128]{1,0:T(8,128)(2,1)}, bf16[256,128]{1,0:T(8,128)(2,1)S(1)}, u32[]{:S(2)}, u32[]{:S(2)}) collective-permute-start(bf16[256,128]{1,0:T(8,128)(2,1)} %get-tuple-element.34.mine_ref), channel_id=1, source_target_pairs={{0,8},{8,0},{1,9},{9,1},{2,10},{10,2},{3,11},{11,3},{4,12},{12,4},... | collective-permute-start | bytes 196616 | tf_op jit(solution)/shard_map/ppermute | solution.py:276
  33.9 1.3 %collective-permute-start.5 = (bf16[64,2048]{1,0:T(8,128)(2,1)S(1)}, bf16[64,2048]{1,0:T(8,128)(2,1)S(1)}, u32[]{:S(2)}, u32[]{:S(2)}) collective-permute-start(bf16[64,2048]{1,0:T(8,128)(2,1)S(1)} %collective-permute-done.3), channel_id=1, source_target_pairs={{0,192},{8,24},{16,208},{24,8},{32,224},{40,56},{48,240},{56,40},{... | collective-permute-start | bytes 786440 | tf_op jit(solution)/shard_map/ppermute | solution.py:272
  35.2 0.9 collective-permute-start.12
  36.2 1.9 %collective-permute-start.11 = (bf16[64,2048]{1,0:T(8,128)(2,1)S(1)}, bf16[64,2048]{1,0:T(8,128)(2,1)S(1)}, u32[]{:S(2)}, u32[]{:S(2)}) collective-permute-start(bf16[64,2048]{1,0:T(8,128)(2,1)S(1)} %pad_maximum_fusion), channel_id=1, source_target_pairs={{0,64},{8,56},{16,80},{24,40},{32,96},{40,24},{48,112},{56,8},{64,... | collective-permute-start | bytes 786440 | tf_op jit(solution)/shard_map/ppermute | solution.py:272
  38.9 3.0 %couple.1.refs_3_.refs_2_.refs_4_.refs_1_ = bf16[8,2048,256]{2,1,0:T(8,128)(2,1)S(1)} custom-call(bf16[256,128]{1,0:T(8,128)(2,1)S(1)} %collective-permute-done.10.theirs_ref, bf16[256,128]{1,0:T(8,128)(2,1)S(1)} %copy-done.1, bf16[32,2048]{1,0:T(8,128)(2,1)S(1)} %bitcast.18), custom_call_target="tpu_custom_call" | custom-call | flops 268435456 | bytes 9437184 | tf_op jit(solution)/shard_map/couple/pallas_call | solution.py:90
  42.4 1.7 %collective-permute-start.6 = (bf16[256,2048]{1,0:T(8,128)(2,1)S(1)}, bf16[256,2048]{1,0:T(8,128)(2,1)S(1)}, u32[]{:S(2)}, u32[]{:S(2)}) collective-permute-start(bf16[256,2048]{1,0:T(8,128)(2,1)S(1)} %constant_dynamic-update-slice_fusion.4.refs_1_), channel_id=1, source_target_pairs={{0,16},{8,200},{16,0},{24,216},{32,48},{40,232},{48,32},{56,248},{... | collective-permute-start | bytes 3145736 | tf_op jit(solution)/shard_map/ppermute | solution.py:272
  44.5 5.2 %collective-permute-done.13 = bf16[64,2048]{1,0:T(8,128)(2,1)S(1)} collective-permute-done((bf16[64,2048]{1,0:T(8,128)(2,1)S(1)}, bf16[64,2048]{1,0:T(8,128)(2,1)S(1)}, u32[]{:S(2)}, u32[]{:S(2)}) %collective-permute-start.13) | collective-permute-done | bytes 262176 | tf_op jit(solution)/shard_map/ppermute | solution.py:272
  49.9 1.0 %collective-permute-start.14 = (bf16[256,2048]{1,0:T(8,128)(2,1)S(1)}, bf16[256,2048]{1,0:T(8,128)(2,1)S(1)}, u32[]{:S(2)}, u32[]{:S(2)}) collective-permute-start(bf16[256,2048]{1,0:T(8,128)(2,1)S(1)} %constant_dynamic-update-slice_fusion.11.refs_2_), channel_id=1, source_target_pairs={{0,16},{8,200},{16,0},{24,216},{32,48},{40,232},{48,32},{56,248},{... | collective-permute-start | bytes 3145736 | tf_op jit(solution)/shard_map/ppermute | solution.py:272
  50.9 6.0 %block.4 = (bf16[8,4,2,64,128]{4,3,2,1,0:T(8,128)(2,1)S(1)}, bf16[8,4,2,64,128]{4,3,2,1,0:T(8,128)(2,1)S(1)}) custom-call(s32[4]{0:T(128)S(1)} %copy-done.2, bf16[256,2048]{1,0:T(8,128)(2,1)S(1)} %constant_dynamic-update-slice_fusion.4.refs_1_, bf16[256,2048]{1,0:T(8,128)(2,1)S(1)} %constant_dynamic-update-slice_fusion.11.refs_2_, ...), custom_call_target="tpu_custom_call" | custom-call | flops 4294967296 | bytes 10485760 | tf_op jit(solution)/shard_map/block/pallas_call | solution.py:204
  57.0 1.8 %collective-permute-done.7.refs_1_ = bf16[256,2048]{1,0:T(8,128)(2,1)S(1)} collective-permute-done((bf16[256,2048]{1,0:T(8,128)(2,1)S(1)}, bf16[256,2048]{1,0:T(8,128)(2,1)S(1)}, u32[]{:S(2)}, u32[]{:S(2)}) %collective-permute-start.7) | collective-permute-done | bytes 1048608 | tf_op jit(solution)/shard_map/ppermute | solution.py:272
  58.7 1.9 %collective-permute-done.6.refs_0_ = bf16[256,2048]{1,0:T(8,128)(2,1)S(1)} collective-permute-done((bf16[256,2048]{1,0:T(8,128)(2,1)S(1)}, bf16[256,2048]{1,0:T(8,128)(2,1)S(1)}, u32[]{:S(2)}, u32[]{:S(2)}) %collective-permute-start.6) | collective-permute-done | bytes 1048608 | tf_op jit(solution)/shard_map/ppermute | solution.py:272
  60.7 5.0 %half.2.refs_3_ = f32[8,512,256]{2,1,0:T(8,128)S(1)} custom-call(bf16[256,2048]{1,0:T(8,128)(2,1)S(1)} %collective-permute-done.6.refs_0_, bf16[256,2048]{1,0:T(8,128)(2,1)S(1)} %collective-permute-done.7.refs_1_, bf16[8,2048,256]{2,1,0:T(8,128)(2,1)S(1)} %couple.1.refs_3_.refs_2_.refs_4_.refs_1_), custom_call_target="tpu_custom_call" | custom-call | flops 4294967296 | bytes 10485760 | tf_op jit(solution)/shard_map/half/pallas_call | solution.py:133
  65.7 4.3 %collective-permute-done.15.refs_2_ = bf16[256,2048]{1,0:T(8,128)(2,1)S(1)} collective-permute-done((bf16[256,2048]{1,0:T(8,128)(2,1)S(1)}, bf16[256,2048]{1,0:T(8,128)(2,1)S(1)}, u32[]{:S(2)}, u32[]{:S(2)}) %collective-permute-start.15) | collective-permute-done | bytes 1048608 | tf_op jit(solution)/shard_map/ppermute | solution.py:272
  70.0 0.9 collective-permute-start.16
  70.9 6.8 %collective-permute-start.18 = (bf16[8,4,2,64,128]{4,3,2,1,0:T(8,128)(2,1)S(1)}, bf16[8,4,2,64,128]{4,3,2,1,0:T(8,128)(2,1)S(1)}, u32[]{:S(2)}, u32[]{:S(2)}) collective-permute-start(bf16[8,4,2,64,128]{4,3,2,1,0:T(8,128)(2,1)S(1)} %get-tuple-element.52), channel_id=1, source_target_pairs={{0,8},{8,0},{1,9},{9,1},{2,10},{10,2},{3,11},{11,3},{4,12},{12,4},... | collective-permute-start | bytes 3145736 | tf_op jit(solution)/shard_map/ppermute | solution.py:276
  77.6 7.2 %block.5 = (bf16[8,4,2,64,128]{4,3,2,1,0:T(8,128)(2,1)S(1)}, bf16[8,4,2,64,128]{4,3,2,1,0:T(8,128)(2,1)S(1)}, bf16[8,4,2,64,128]{4,3,2,1,0:T(8,128)(2,1)S(1)}, bf16[8,4,2,64,128]{4,3,2,1,0:T(8,128)(2,1)S(1)}) custom-call(s32[4]{0:T(128)S(1)} %copy-done.2, bf16[256,2048]{1,0:T(8,128)(2,1)S(1)} %collective-permute-done.14.refs_1_, ...), custom_call_target="tpu_custom_call" | custom-call | flops 4294967296 | bytes 10485760 | tf_op jit(solution)/shard_map/block/pallas_call | solution.py:204
  84.8 1.3 %collective-permute-start.20 = (bf16[8,4,2,64,128]{4,3,2,1,0:T(8,128)(2,1)S(1)}, bf16[8,4,2,64,128]{4,3,2,1,0:T(8,128)(2,1)S(1)}, u32[]{:S(2)}, u32[]{:S(2)}) collective-permute-start(bf16[8,4,2,64,128]{4,3,2,1,0:T(8,128)(2,1)S(1)} %get-tuple-element.54), channel_id=1, source_target_pairs={{0,8},{8,0},{1,9},{9,1},{2,10},{10,2},{3,11},{11,3},{4,12},{12,4},... | collective-permute-start | bytes 3145736 | tf_op jit(solution)/shard_map/ppermute | solution.py:276
  86.2 2.3 %collective-permute-start.19 = (bf16[8,4,2,64,128]{4,3,2,1,0:T(8,128)(2,1)S(1)}, bf16[8,4,2,64,128]{4,3,2,1,0:T(8,128)(2,1)S(1)}, u32[]{:S(2)}, u32[]{:S(2)}) collective-permute-start(bf16[8,4,2,64,128]{4,3,2,1,0:T(8,128)(2,1)S(1)} %get-tuple-element.53), channel_id=1, source_target_pairs={{0,8},{8,0},{1,9},{9,1},{2,10},{10,2},{3,11},{11,3},{4,12},{12,4},... | collective-permute-start | bytes 3145736 | tf_op jit(solution)/shard_map/ppermute | solution.py:276
  88.5 2.9 %half.3.refs_2_ = f32[8,256,256]{2,1,0:T(8,128)S(1)} custom-call(bf16[256,2048]{1,0:T(8,128)(2,1)S(1)} %collective-permute-done.17.refs_0_, bf16[8,2048,256]{2,1,0:T(8,128)(2,1)S(1)} %couple.1.refs_3_.refs_2_.refs_4_.refs_1_), custom_call_target="tpu_custom_call" | custom-call | flops 2147483648 | bytes 10485760 | tf_op jit(solution)/shard_map/half/pallas_call | solution.py:133
  91.4 2.3 %block.7 = bf16[8,4,2,64,128]{4,3,2,1,0:T(8,128)(2,1)S(1)} custom-call(s32[4]{0:T(128)S(1)} %copy-done.2, bf16[256,2048]{1,0:T(8,128)(2,1)S(1)} %collective-permute-done.16.refs_1_, f32[8,256,256]{2,1,0:T(8,128)S(1)} %half.3.refs_2_, bf16[8,2048,256]{2,1,0:T(8,128)(2,1)S(1)} %couple.1.refs_3_.refs_2_.refs_4_.refs_1_), custom_call_target="tpu_custom_call" | custom-call | flops 1073741824 | bytes 10485760 | tf_op jit(solution)/shard_map/block/pallas_call | solution.py:204
  94.4 2.3 %block.6.refs_3_ = bf16[8,4,2,64,128]{4,3,2,1,0:T(8,128)(2,1)S(1)} custom-call(s32[4]{0:T(128)S(1)} %copy-done.2, bf16[256,2048]{1,0:T(8,128)(2,1)S(1)} %collective-permute-done.16.refs_1_, f32[8,256,256]{2,1,0:T(8,128)S(1)} %half.3.refs_2_, bf16[8,2048,256]{2,1,0:T(8,128)(2,1)S(1)} %couple.1.refs_3_.refs_2_.refs_4_.refs_1_), custom_call_target="tpu_custom_call" | custom-call | flops 1073741824 | bytes 10485760 | tf_op jit(solution)/shard_map/block/pallas_call | solution.py:204
  96.8 3.7 %add.11 = bf16[8,16,2,64,128]{4,3,2,1,0:T(8,128)(2,1)} custom-call(s32[4]{0:T(128)S(1)} %copy-done.2, bf16[8,4,2,64,128]{4,3,2,1,0:T(8,128)(2,1)S(1)} %get-tuple-element.41.refs_0_, bf16[8,4,2,64,128]{4,3,2,1,0:T(8,128)(2,1)S(1)} %get-tuple-element.46.refs_1_, bf16[8,4,2,64,128]{4,3,2,1,0:T(8,128)(2,1)S(1)} %get-tuple-element.47.refs_2_, ...), custom_call_target="tpu_custom_call" | custom-call | flops 10000000 | bytes 13631488 | tf_op jit(solution)/shard_map/add/pallas_call | solution.py:240
  (46 shorter events, 5.9 us)
Async XLA Ops:
  0.0 26.9 %copy-start = (bf16[1024,128]{1,0:T(8,128)(2,1)S(1)}, bf16[1024,128]{1,0:T(8,128)(2,1)}, u32[]{:S(2)}) copy-start(bf16[1024,128]{1,0:T(8,128)(2,1)} %param.16) | copy-start | bytes 786436
  3.9 4.4 %collective-permute-start = (bf16[8,2048]{1,0:T(8,128)(2,1)}, bf16[8,2048]{1,0:T(8,128)(2,1)S(1)}, u32[]{:S(2)}, u32[]{:S(2)}) collective-permute-start(bf16[8,2048]{1,0:T(8,128)(2,1)} %get-tuple-element.31), channel_id=1, source_target_pairs={{0,8},{8,0},{1,9},{9,1},{2,10},{10,2},{3,11},{11,3},{4,12},{12,4},... | collective-permute-start | bytes 98312 | tf_op jit(solution)/shard_map/ppermute | solution.py:276
  9.1 5.5 %collective-permute-start.1 = (bf16[16,2048]{1,0:T(8,128)(2,1)S(1)}, bf16[16,2048]{1,0:T(8,128)(2,1)S(1)}, u32[]{:S(2)}, u32[]{:S(2)}) collective-permute-start(bf16[16,2048]{1,0:T(8,128)(2,1)S(1)} %pad_maximum_fusion.2), channel_id=1, source_target_pairs={{0,1},{1,0},{2,3},{3,2},{4,5},{5,4},{6,7},{7,6},{8,15},{9,10},{10,... | collective-permute-start | bytes 196616 | tf_op jit(solution)/shard_map/ppermute | solution.py:261
  15.3 3.9 %collective-permute-start.2 = (bf16[32,2048]{1,0:T(8,128)(2,1)S(1)}, bf16[32,2048]{1,0:T(8,128)(2,1)S(1)}, u32[]{:S(2)}, u32[]{:S(2)}) collective-permute-start(bf16[32,2048]{1,0:T(8,128)(2,1)S(1)} %pad_maximum_fusion.1), channel_id=1, source_target_pairs={{0,7},{1,2},{2,1},{3,4},{4,3},{5,6},{6,5},{7,0},{8,9},{9,8},{10,11... | collective-permute-start | bytes 393224 | tf_op jit(solution)/shard_map/ppermute | solution.py:261
  19.2 5.0 %collective-permute-start.8 = (bf16[32,2048]{1,0:T(8,128)(2,1)S(1)}, bf16[32,2048]{1,0:T(8,128)(2,1)S(1)}, u32[]{:S(2)}, u32[]{:S(2)}) collective-permute-start(bf16[32,2048]{1,0:T(8,128)(2,1)S(1)} %collective-permute-done.2), channel_id=1, source_target_pairs={{0,1},{1,0},{2,3},{3,2},{4,5},{5,4},{6,7},{7,6},{8,15},{9,10},{10,... | collective-permute-start | bytes 393224 | tf_op jit(solution)/shard_map/ppermute | solution.py:261
  24.3 3.8 %collective-permute-start.9 = (bf16[32,2048]{1,0:T(8,128)(2,1)S(1)}, bf16[32,2048]{1,0:T(8,128)(2,1)S(1)}, u32[]{:S(2)}, u32[]{:S(2)}) collective-permute-start(bf16[32,2048]{1,0:T(8,128)(2,1)S(1)} %collective-permute-done.8), channel_id=1, source_target_pairs={{0,7},{1,2},{2,1},{3,4},{4,3},{5,6},{6,5},{7,0},{8,9},{9,8},{10,11... | collective-permute-start | bytes 393224 | tf_op jit(solution)/shard_map/ppermute | solution.py:261
  24.3 9.6 %collective-permute-start.3 = (bf16[64,2048]{1,0:T(8,128)(2,1)S(1)}, bf16[64,2048]{1,0:T(8,128)(2,1)S(1)}, u32[]{:S(2)}, u32[]{:S(2)}) collective-permute-start(bf16[64,2048]{1,0:T(8,128)(2,1)S(1)} %get-tuple-element.55), channel_id=1, source_target_pairs={{0,64},{8,56},{16,80},{24,40},{32,96},{40,24},{48,112},{56,8},{64,... | collective-permute-start | bytes 786440 | tf_op jit(solution)/shard_map/ppermute | solution.py:272
  26.9 8.3 %collective-permute-start.4 = (bf16[64,2048]{1,0:T(8,128)(2,1)S(1)}, bf16[64,2048]{1,0:T(8,128)(2,1)S(1)}, u32[]{:S(2)}, u32[]{:S(2)}) collective-permute-start(bf16[64,2048]{1,0:T(8,128)(2,1)S(1)} %get-tuple-element.55), channel_id=1, source_target_pairs={{0,192},{8,24},{16,208},{24,8},{32,224},{40,56},{48,240},{56,40},{... | collective-permute-start | bytes 786440 | tf_op jit(solution)/shard_map/ppermute | solution.py:272
  28.1 7.1 %collective-permute-start.10 = (bf16[256,128]{1,0:T(8,128)(2,1)}, bf16[256,128]{1,0:T(8,128)(2,1)S(1)}, u32[]{:S(2)}, u32[]{:S(2)}) collective-permute-start(bf16[256,128]{1,0:T(8,128)(2,1)} %get-tuple-element.34.mine_ref), channel_id=1, source_target_pairs={{0,8},{8,0},{1,9},{9,1},{2,10},{10,2},{3,11},{11,3},{4,12},{12,4},... | collective-permute-start | bytes 196616 | tf_op jit(solution)/shard_map/ppermute | solution.py:276
  33.9 8.0 %collective-permute-start.5 = (bf16[64,2048]{1,0:T(8,128)(2,1)S(1)}, bf16[64,2048]{1,0:T(8,128)(2,1)S(1)}, u32[]{:S(2)}, u32[]{:S(2)}) collective-permute-start(bf16[64,2048]{1,0:T(8,128)(2,1)S(1)} %collective-permute-done.3), channel_id=1, source_target_pairs={{0,192},{8,24},{16,208},{24,8},{32,224},{40,56},{48,240},{56,40},{... | collective-permute-start | bytes 786440 | tf_op jit(solution)/shard_map/ppermute | solution.py:272
  35.2 9.2 %collective-permute-start.12 = (bf16[64,2048]{1,0:T(8,128)(2,1)S(1)}, bf16[64,2048]{1,0:T(8,128)(2,1)S(1)}, u32[]{:S(2)}, u32[]{:S(2)}) collective-permute-start(bf16[64,2048]{1,0:T(8,128)(2,1)S(1)} %pad_maximum_fusion), channel_id=1, source_target_pairs={{0,192},{8,24},{16,208},{24,8},{32,224},{40,56},{48,240},{56,40},{... | collective-permute-start | bytes 786440 | tf_op jit(solution)/shard_map/ppermute | solution.py:272
  36.2 8.0 %collective-permute-start.11 = (bf16[64,2048]{1,0:T(8,128)(2,1)S(1)}, bf16[64,2048]{1,0:T(8,128)(2,1)S(1)}, u32[]{:S(2)}, u32[]{:S(2)}) collective-permute-start(bf16[64,2048]{1,0:T(8,128)(2,1)S(1)} %pad_maximum_fusion), channel_id=1, source_target_pairs={{0,64},{8,56},{16,80},{24,40},{32,96},{40,24},{48,112},{56,8},{64,... | collective-permute-start | bytes 786440 | tf_op jit(solution)/shard_map/ppermute | solution.py:272
  38.1 0.8 copy-start.1
  38.9 12.0 %copy-start.2 = (s32[4]{0:T(128)S(1)}, s32[4]{0:T(128)}, u32[]{:S(2)}) copy-start(s32[4]{0:T(128)} %pad_add_fusion.core_ref.refs_0_.at_ref) | copy-start | bytes 52
  41.9 16.8 %collective-permute-start.7 = (bf16[256,2048]{1,0:T(8,128)(2,1)S(1)}, bf16[256,2048]{1,0:T(8,128)(2,1)S(1)}, u32[]{:S(2)}, u32[]{:S(2)}) collective-permute-start(bf16[256,2048]{1,0:T(8,128)(2,1)S(1)} %constant_dynamic-update-slice_fusion.4.refs_1_), channel_id=1, source_target_pairs={{0,48},{8,72},{16,32},{24,88},{32,16},{40,104},{48,0},{56,120},{64... | collective-permute-start | bytes 3145736 | tf_op jit(solution)/shard_map/ppermute | solution.py:272
  42.4 18.2 %collective-permute-start.6 = (bf16[256,2048]{1,0:T(8,128)(2,1)S(1)}, bf16[256,2048]{1,0:T(8,128)(2,1)S(1)}, u32[]{:S(2)}, u32[]{:S(2)}) collective-permute-start(bf16[256,2048]{1,0:T(8,128)(2,1)S(1)} %constant_dynamic-update-slice_fusion.4.refs_1_), channel_id=1, source_target_pairs={{0,16},{8,200},{16,0},{24,216},{32,48},{40,232},{48,32},{56,248},{... | collective-permute-start | bytes 3145736 | tf_op jit(solution)/shard_map/ppermute | solution.py:272
  44.2 5.5 %collective-permute-start.13 = (bf16[64,2048]{1,0:T(8,128)(2,1)S(1)}, bf16[64,2048]{1,0:T(8,128)(2,1)S(1)}, u32[]{:S(2)}, u32[]{:S(2)}) collective-permute-start(bf16[64,2048]{1,0:T(8,128)(2,1)S(1)} %collective-permute-done.11), channel_id=1, source_target_pairs={{0,192},{8,24},{16,208},{24,8},{32,224},{40,56},{48,240},{56,40},{... | collective-permute-start | bytes 786440 | tf_op jit(solution)/shard_map/ppermute | solution.py:272
  49.7 20.3 %collective-permute-start.15 = (bf16[256,2048]{1,0:T(8,128)(2,1)S(1)}, bf16[256,2048]{1,0:T(8,128)(2,1)S(1)}, u32[]{:S(2)}, u32[]{:S(2)}) collective-permute-start(bf16[256,2048]{1,0:T(8,128)(2,1)S(1)} %constant_dynamic-update-slice_fusion.11.refs_2_), channel_id=1, source_target_pairs={{0,48},{8,72},{16,32},{24,88},{32,16},{40,104},{48,0},{56,120},{64... | collective-permute-start | bytes 3145736 | tf_op jit(solution)/shard_map/ppermute | solution.py:272
  49.9 27.7 %collective-permute-start.14 = (bf16[256,2048]{1,0:T(8,128)(2,1)S(1)}, bf16[256,2048]{1,0:T(8,128)(2,1)S(1)}, u32[]{:S(2)}, u32[]{:S(2)}) collective-permute-start(bf16[256,2048]{1,0:T(8,128)(2,1)S(1)} %constant_dynamic-update-slice_fusion.11.refs_2_), channel_id=1, source_target_pairs={{0,16},{8,200},{16,0},{24,216},{32,48},{40,232},{48,32},{56,248},{... | collective-permute-start | bytes 3145736 | tf_op jit(solution)/shard_map/ppermute | solution.py:272
  60.7 25.5 %collective-permute-start.17 = (bf16[256,2048]{1,0:T(8,128)(2,1)S(1)}, bf16[256,2048]{1,0:T(8,128)(2,1)S(1)}, u32[]{:S(2)}, u32[]{:S(2)}) collective-permute-start(bf16[256,2048]{1,0:T(8,128)(2,1)S(1)} %collective-permute-done.6.refs_0_), channel_id=1, source_target_pairs={{0,48},{8,72},{16,32},{24,88},{32,16},{40,104},{48,0},{56,120},{64... | collective-permute-start | bytes 3145736 | tf_op jit(solution)/shard_map/ppermute | solution.py:272
  70.0 21.4 %collective-permute-start.16 = (bf16[256,2048]{1,0:T(8,128)(2,1)S(1)}, bf16[256,2048]{1,0:T(8,128)(2,1)S(1)}, u32[]{:S(2)}, u32[]{:S(2)}) collective-permute-start(bf16[256,2048]{1,0:T(8,128)(2,1)S(1)} %collective-permute-done.15.refs_2_), channel_id=1, source_target_pairs={{0,16},{8,200},{16,0},{24,216},{32,48},{40,232},{48,32},{56,248},{... | collective-permute-start | bytes 3145736 | tf_op jit(solution)/shard_map/ppermute | solution.py:272
  70.9 25.8 %collective-permute-start.18 = (bf16[8,4,2,64,128]{4,3,2,1,0:T(8,128)(2,1)S(1)}, bf16[8,4,2,64,128]{4,3,2,1,0:T(8,128)(2,1)S(1)}, u32[]{:S(2)}, u32[]{:S(2)}) collective-permute-start(bf16[8,4,2,64,128]{4,3,2,1,0:T(8,128)(2,1)S(1)} %get-tuple-element.52), channel_id=1, source_target_pairs={{0,8},{8,0},{1,9},{9,1},{2,10},{10,2},{3,11},{11,3},{4,12},{12,4},... | collective-permute-start | bytes 3145736 | tf_op jit(solution)/shard_map/ppermute | solution.py:276
  84.8 11.9 %collective-permute-start.20 = (bf16[8,4,2,64,128]{4,3,2,1,0:T(8,128)(2,1)S(1)}, bf16[8,4,2,64,128]{4,3,2,1,0:T(8,128)(2,1)S(1)}, u32[]{:S(2)}, u32[]{:S(2)}) collective-permute-start(bf16[8,4,2,64,128]{4,3,2,1,0:T(8,128)(2,1)S(1)} %get-tuple-element.54), channel_id=1, source_target_pairs={{0,8},{8,0},{1,9},{9,1},{2,10},{10,2},{3,11},{11,3},{4,12},{12,4},... | collective-permute-start | bytes 3145736 | tf_op jit(solution)/shard_map/ppermute | solution.py:276
  86.2 10.5 %collective-permute-start.19 = (bf16[8,4,2,64,128]{4,3,2,1,0:T(8,128)(2,1)S(1)}, bf16[8,4,2,64,128]{4,3,2,1,0:T(8,128)(2,1)S(1)}, u32[]{:S(2)}, u32[]{:S(2)}) collective-permute-start(bf16[8,4,2,64,128]{4,3,2,1,0:T(8,128)(2,1)S(1)} %get-tuple-element.53), channel_id=1, source_target_pairs={{0,8},{8,0},{1,9},{9,1},{2,10},{10,2},{3,11},{11,3},{4,12},{12,4},... | collective-permute-start | bytes 3145736 | tf_op jit(solution)/shard_map/ppermute | solution.py:276
  93.6 3.1 %copy-start.3 = (f32[128]{0:T(128)S(1)}, f32[128]{0:T(128)}, u32[]{:S(2)}) copy-start(f32[128]{0:T(128)} %param.17) | copy-start | bytes 1540
  93.7 3.1 %collective-permute-start.21 = (bf16[8,4,2,64,128]{4,3,2,1,0:T(8,128)(2,1)S(1)}, bf16[8,4,2,64,128]{4,3,2,1,0:T(8,128)(2,1)S(1)}, u32[]{:S(2)}, u32[]{:S(2)}) collective-permute-start(bf16[8,4,2,64,128]{4,3,2,1,0:T(8,128)(2,1)S(1)} %block.7), channel_id=1, source_target_pairs={{0,8},{8,0},{1,9},{9,1},{2,10},{10,2},{3,11},{11,3},{4,12},{12,4},... | collective-permute-start | bytes 3145736 | tf_op jit(solution)/shard_map/ppermute | solution.py:276

commit v4 on v3

--- a/solution.py
+++ b/solution.py
@@ -254,6 +254,8 @@
 
 
 def partner(k, n, core, step):
+    if step == 2:
+        return (k + 2) % n
     return (k + 1 if (k + core + step) % 2 == 0 else k - 1) % n
 
 
@@ -294,17 +296,16 @@
     z1 = join(r, along_z(r, 0))
     z2 = along_z(z1, 1)
     h0 = join(z1, z2)
-    z3 = along_z(z2, 2)
+    t = couple(swap(lt), lt, w)
+    z3, t = together(along_z(z2, 0), t)
     m1_0 = along_plane(h0, False, 0)
     m2_0 = along_plane(h0, False, 1)
-    z4, lt = together(along_z(z3, 3), lt)
+    z4, offset = together(along_z(z3, 1), couple_offset)
     m3_0 = along_plane(m1_0, False, 1)
-    h1, lt_sibling = together(join(z3, z4), swap(lt))
-    t = couple(lt_sibling, lt, w)
+    h1, offset = together(join(z3, z4), swap(offset))
     m1_1 = along_plane(h1, False, 0)
     m2_1 = along_plane(h1, False, 1)
-    m1_1, t = together(m1_1, t)
-    m3_1 = along_plane(m1_1, False, 1)
+    m3_1 = along_plane(h1, False, 2)
     b0_0 = join(h0, m1_0, m2_0, m3_0)
     b1_0 = along_plane(b0_0, True, 0)
     b2_0 = along_plane(b0_0, True, 1)
@@ -325,7 +326,7 @@
     q3, = block(at, [b3_1], d3, t, 1)
     theirs = [swap(p) for p in (p0, p1, p2, p3)]
     mine = [q0, q1, q2, q3]
-    return add(at, mine, theirs, couple_offset).reshape(LOCAL, 16 * 2 * 64, CZ)
+    return add(at, mine, theirs, offset).reshape(LOCAL, 16 * 2 * 64, CZ)
 
 
 def solution(mesh):

time: 101 us -> 94.8 us (0.939)
  starting transfers between devices: 38.2 us -> 34.5 us
  waiting for transfers between devices: 22.4 us -> 20 us
    ppermute x6 -> x7, starting transfers between devices: 20.2 us -> 11.6 us  [swap(): return lax.ppermute(v, 'c', [(0, 1), (1, 0)])]
    ppermute x12, starting transfers between devices: 11.3 us -> 16 us  [along_plane(): return lax.ppermute(v, ('y', 'x', 'c'), pairs)]
    ppermute x4, waiting for transfers between devices: 8.09 us -> 4.99 us  [along_z(): lax.ppermute(v, ('c', 'z'), [(c * 8 + k, c * 8 + partner(k, 8, c, step))...]
    ppermute x12, waiting for transfers between devices: 13.2 us -> 14.8 us  [along_plane(): return lax.ppermute(v, ('y', 'x', 'c'), pairs)]
  transfers between devices with their start and end apart: 22 -> 23, of which waited for: 9 -> 10; matrix products, arithmetic and copies ran while one was open for 1% -> 3% of each run, Pallas kernels for 29% -> 30%
where the time goes in v4:
time: 94.8 us; the launch traced here: 94.5 us
  Pallas kernels  35.6 us (38%)
  starting transfers between devices  34.5 us (36%)
  waiting for transfers between devices  20 us (21%)
  other arithmetic  2.2 us (2%)
  local copies, waits for them, and re-layouts  1.82 us (2%)
    pallas_call x4, Pallas kernels, block(): pl.pallas_call(lambda *refs: block_kernel(first, count, ready is not None...  17.8 us
    ppermute x12, starting transfers between devices, along_plane(): return lax.ppermute(v, ('y', 'x', 'c'), pairs)  16 us
    ppermute x12, waiting for transfers between devices, along_plane(): return lax.ppermute(v, ('y', 'x', 'c'), pairs)  14.8 us
    ppermute x7, starting transfers between devices, swap(): return lax.ppermute(v, 'c', [(0, 1), (1, 0)])  11.6 us
    pallas_call x2, Pallas kernels, half(): pl.pallas_call(lambda *refs: half_kernel(count, *refs), grid=(4,), in_spe...  7.88 us
    ppermute x4, starting transfers between devices, along_z(): lax.ppermute(v, ('c', 'z'), [(c * 8 + k, c * 8 + partner(k, 8, c, step))...  6.93 us
    ppermute x4, waiting for transfers between devices, along_z(): lax.ppermute(v, ('c', 'z'), [(c * 8 + k, c * 8 + partner(k, 8, c, step))...  4.99 us
    pallas_call x1, Pallas kernels, add(): pl.pallas_call(add_kernel, grid_spec=pltpu.PrefetchScalarGridSpec(num_sca...  3.69 us
  transfers between devices with their start and end apart: 23, of which 10 were waited for; matrix products, arithmetic and copies ran while one was open for 3% of the time, Pallas kernels for 30%

profile of v4, /device:TPU:1, one launch (start us, length us, event | category | flops | bytes accessed | tf_op | source)
XLA Modules:
  0.0 94.5 jit_solution(2690302673190472411)
XLA Ops:
  0.7 3.2 %project.1 = (bf16[8,2048]{1,0:T(8,128)(2,1)}, bf16[8,2048]{1,0:T(8,128)(2,1)}, bf16[256,128]{1,0:T(8,128)(2,1)}) custom-call(s32[4]{0:T(128)} %pad_add_fusion.core_ref.refs_0_.at_ref, bf16[128,8,256]{2,1,0:T(8,128)(2,1)} %msa_in.1, f32[1,256]{1,0:T(1,128)} %bitcast.23, f32[1,256]{1,0:T(1,128)} %bitcast.24, bf16[32,256]{1,0:T(8,128)(2,1)} %bitcast.21, ...), custom_call_target="tpu_custom_call" | custom-call | tf_op jit(solution)/shard_map/project/pallas_call | solution.py:45
  3.9 3.3 %collective-permute-start = (bf16[8,2048]{1,0:T(8,128)(2,1)}, bf16[8,2048]{1,0:T(8,128)(2,1)S(1)}, u32[]{:S(2)}, u32[]{:S(2)}) collective-permute-start(bf16[8,2048]{1,0:T(8,128)(2,1)} %get-tuple-element.31), channel_id=1, source_target_pairs={{0,8},{8,0},{1,9},{9,1},{2,10},{10,2},{3,11},{11,3},{4,12},{12,4},... | collective-permute-start | bytes 98312 | tf_op jit(solution)/shard_map/ppermute | solution.py:278
  9.1 3.8 %collective-permute-start.1 = (bf16[16,2048]{1,0:T(8,128)(2,1)S(1)}, bf16[16,2048]{1,0:T(8,128)(2,1)S(1)}, u32[]{:S(2)}, u32[]{:S(2)}) collective-permute-start(bf16[16,2048]{1,0:T(8,128)(2,1)S(1)} %pad_maximum_fusion.2), channel_id=1, source_target_pairs={{0,1},{1,0},{2,3},{3,2},{4,5},{5,4},{6,7},{7,6},{8,15},{9,10},{10,... | collective-permute-start | bytes 196616 | tf_op jit(solution)/shard_map/ppermute | solution.py:263
  13.0 1.6 %collective-permute-done.1 = bf16[16,2048]{1,0:T(8,128)(2,1)S(1)} collective-permute-done((bf16[16,2048]{1,0:T(8,128)(2,1)S(1)}, bf16[16,2048]{1,0:T(8,128)(2,1)S(1)}, u32[]{:S(2)}, u32[]{:S(2)}) %collective-permute-start.1) | collective-permute-done | bytes 65568 | tf_op jit(solution)/shard_map/ppermute | solution.py:263
  15.5 0.8 copy-done.1
  16.3 3.0 %couple.1.refs_3_.refs_2_.refs_4_.refs_1_ = bf16[8,2048,256]{2,1,0:T(8,128)(2,1)S(1)} custom-call(bf16[256,128]{1,0:T(8,128)(2,1)S(1)} %collective-permute-done.9.theirs_ref, bf16[256,128]{1,0:T(8,128)(2,1)S(1)} %copy-done.1, bf16[32,2048]{1,0:T(8,128)(2,1)S(1)} %bitcast.18), custom_call_target="tpu_custom_call" | custom-call | flops 268435456 | bytes 9437184 | tf_op jit(solution)/shard_map/couple/pallas_call | solution.py:90
  19.3 2.8 %collective-permute-start.8 = (bf16[32,2048]{1,0:T(8,128)(2,1)S(1)}, bf16[32,2048]{1,0:T(8,128)(2,1)S(1)}, u32[]{:S(2)}, u32[]{:S(2)}) collective-permute-start(bf16[32,2048]{1,0:T(8,128)(2,1)S(1)} %collective-permute-done.2), channel_id=1, source_target_pairs={{0,1},{1,0},{2,3},{3,2},{4,5},{5,4},{6,7},{7,6},{8,15},{9,10},{10,... | collective-permute-start | bytes 393224 | tf_op jit(solution)/shard_map/ppermute | solution.py:263
  22.1 2.3 %collective-permute-done.8 = bf16[32,2048]{1,0:T(8,128)(2,1)S(1)} collective-permute-done((bf16[32,2048]{1,0:T(8,128)(2,1)S(1)}, bf16[32,2048]{1,0:T(8,128)(2,1)S(1)}, u32[]{:S(2)}, u32[]{:S(2)}) %collective-permute-start.8) | collective-permute-done | bytes 131104 | tf_op jit(solution)/shard_map/ppermute | solution.py:263
  24.7 2.5 %collective-permute-start.3 = (bf16[64,2048]{1,0:T(8,128)(2,1)S(1)}, bf16[64,2048]{1,0:T(8,128)(2,1)S(1)}, u32[]{:S(2)}, u32[]{:S(2)}) collective-permute-start(bf16[64,2048]{1,0:T(8,128)(2,1)S(1)} %get-tuple-element.55), channel_id=1, source_target_pairs={{0,64},{8,56},{16,80},{24,40},{32,96},{40,24},{48,112},{56,8},{64,... | collective-permute-start | bytes 786440 | tf_op jit(solution)/shard_map/ppermute | solution.py:274
  27.2 1.0 %collective-permute-done.10 = bf16[32,2048]{1,0:T(8,128)(2,1)S(1)} collective-permute-done((bf16[32,2048]{1,0:T(8,128)(2,1)S(1)}, bf16[32,2048]{1,0:T(8,128)(2,1)S(1)}, u32[]{:S(2)}, u32[]{:S(2)}) %collective-permute-start.10) | collective-permute-done | bytes 131104 | tf_op jit(solution)/shard_map/ppermute | solution.py:263
  28.3 5.6 %collective-permute-start.11 = (f32[128]{0:T(128)S(1)}, f32[128]{0:T(128)S(1)}, u32[]{:S(2)}, u32[]{:S(2)}) collective-permute-start(f32[128]{0:T(128)S(1)} %copy-done.3), channel_id=1, source_target_pairs={{0,8},{8,0},{1,9},{9,1},{2,10},{10,2},{3,11},{11,3},{4,12},{12,4},... | collective-permute-start | bytes 1544 | tf_op jit(solution)/shard_map/ppermute | solution.py:278
  33.9 1.2 %collective-permute-start.5 = (bf16[64,2048]{1,0:T(8,128)(2,1)S(1)}, bf16[64,2048]{1,0:T(8,128)(2,1)S(1)}, u32[]{:S(2)}, u32[]{:S(2)}) collective-permute-start(bf16[64,2048]{1,0:T(8,128)(2,1)S(1)} %collective-permute-done.3), channel_id=1, source_target_pairs={{0,192},{8,24},{16,208},{24,8},{32,224},{40,56},{48,240},{56,40},{... | collective-permute-start | bytes 786440 | tf_op jit(solution)/shard_map/ppermute | solution.py:274
  35.2 2.5 %collective-permute-start.14 = (bf16[64,2048]{1,0:T(8,128)(2,1)S(1)}, bf16[64,2048]{1,0:T(8,128)(2,1)S(1)}, u32[]{:S(2)}, u32[]{:S(2)}) collective-permute-start(bf16[64,2048]{1,0:T(8,128)(2,1)S(1)} %pad_maximum_fusion), channel_id=1, source_target_pairs={{0,128},{8,40},{16,144},{24,56},{32,160},{40,8},{48,176},{56,24},{... | collective-permute-start | bytes 786440 | tf_op jit(solution)/shard_map/ppermute | solution.py:274
  39.1 1.4 %collective-permute-start.7 = (bf16[256,2048]{1,0:T(8,128)(2,1)S(1)}, bf16[256,2048]{1,0:T(8,128)(2,1)S(1)}, u32[]{:S(2)}, u32[]{:S(2)}) collective-permute-start(bf16[256,2048]{1,0:T(8,128)(2,1)S(1)} %constant_dynamic-update-slice_fusion.4.refs_1_), channel_id=1, source_target_pairs={{0,48},{8,72},{16,32},{24,88},{32,16},{40,104},{48,0},{56,120},{64... | collective-permute-start | bytes 3145736 | tf_op jit(solution)/shard_map/ppermute | solution.py:274
  40.5 1.9 %collective-permute-start.6 = (bf16[256,2048]{1,0:T(8,128)(2,1)S(1)}, bf16[256,2048]{1,0:T(8,128)(2,1)S(1)}, u32[]{:S(2)}, u32[]{:S(2)}) collective-permute-start(bf16[256,2048]{1,0:T(8,128)(2,1)S(1)} %constant_dynamic-update-slice_fusion.4.refs_1_), channel_id=1, source_target_pairs={{0,16},{8,200},{16,0},{24,216},{32,48},{40,232},{48,32},{56,248},{... | collective-permute-start | bytes 3145736 | tf_op jit(solution)/shard_map/ppermute | solution.py:274
  42.4 4.8 %collective-permute-done.12 = bf16[64,2048]{1,0:T(8,128)(2,1)S(1)} collective-permute-done((bf16[64,2048]{1,0:T(8,128)(2,1)S(1)}, bf16[64,2048]{1,0:T(8,128)(2,1)S(1)}, u32[]{:S(2)}, u32[]{:S(2)}) %collective-permute-start.12) | collective-permute-done | bytes 262176 | tf_op jit(solution)/shard_map/ppermute | solution.py:274
  47.3 1.2 %collective-permute-start.16 = (bf16[256,2048]{1,0:T(8,128)(2,1)S(1)}, bf16[256,2048]{1,0:T(8,128)(2,1)S(1)}, u32[]{:S(2)}, u32[]{:S(2)}) collective-permute-start(bf16[256,2048]{1,0:T(8,128)(2,1)S(1)} %constant_dynamic-update-slice_fusion.11.refs_2_), channel_id=1, source_target_pairs={{0,48},{8,72},{16,32},{24,88},{32,16},{40,104},{48,0},{56,120},{64... | collective-permute-start | bytes 3145736 | tf_op jit(solution)/shard_map/ppermute | solution.py:274
  48.5 1.9 %collective-permute-start.15 = (bf16[256,2048]{1,0:T(8,128)(2,1)S(1)}, bf16[256,2048]{1,0:T(8,128)(2,1)S(1)}, u32[]{:S(2)}, u32[]{:S(2)}) collective-permute-start(bf16[256,2048]{1,0:T(8,128)(2,1)S(1)} %constant_dynamic-update-slice_fusion.11.refs_2_), channel_id=1, source_target_pairs={{0,16},{8,200},{16,0},{24,216},{32,48},{40,232},{48,32},{56,248},{... | collective-permute-start | bytes 3145736 | tf_op jit(solution)/shard_map/ppermute | solution.py:274
  50.4 6.1 %block.4 = (bf16[8,4,2,64,128]{4,3,2,1,0:T(8,128)(2,1)S(1)}, bf16[8,4,2,64,128]{4,3,2,1,0:T(8,128)(2,1)S(1)}) custom-call(s32[4]{0:T(128)S(1)} %copy-done.2, bf16[256,2048]{1,0:T(8,128)(2,1)S(1)} %constant_dynamic-update-slice_fusion.4.refs_1_, bf16[256,2048]{1,0:T(8,128)(2,1)S(1)} %constant_dynamic-update-slice_fusion.11.refs_2_, ...), custom_call_target="tpu_custom_call" | custom-call | flops 4294967296 | bytes 10485760 | tf_op jit(solution)/shard_map/block/pallas_call | solution.py:204
  56.5 2.3 %collective-permute-done.7.refs_1_ = bf16[256,2048]{1,0:T(8,128)(2,1)S(1)} collective-permute-done((bf16[256,2048]{1,0:T(8,128)(2,1)S(1)}, bf16[256,2048]{1,0:T(8,128)(2,1)S(1)}, u32[]{:S(2)}, u32[]{:S(2)}) %collective-permute-start.7) | collective-permute-done | bytes 1048608 | tf_op jit(solution)/shard_map/ppermute | solution.py:274
  58.8 2.2 %collective-permute-done.6.refs_0_ = bf16[256,2048]{1,0:T(8,128)(2,1)S(1)} collective-permute-done((bf16[256,2048]{1,0:T(8,128)(2,1)S(1)}, bf16[256,2048]{1,0:T(8,128)(2,1)S(1)}, u32[]{:S(2)}, u32[]{:S(2)}) %collective-permute-start.6) | collective-permute-done | bytes 1048608 | tf_op jit(solution)/shard_map/ppermute | solution.py:274
  61.0 5.0 %half.2.refs_3_ = f32[8,512,256]{2,1,0:T(8,128)S(1)} custom-call(bf16[256,2048]{1,0:T(8,128)(2,1)S(1)} %collective-permute-done.6.refs_0_, bf16[256,2048]{1,0:T(8,128)(2,1)S(1)} %collective-permute-done.7.refs_1_, bf16[8,2048,256]{2,1,0:T(8,128)(2,1)S(1)} %couple.1.refs_3_.refs_2_.refs_4_.refs_1_), custom_call_target="tpu_custom_call" | custom-call | flops 4294967296 | bytes 10485760 | tf_op jit(solution)/shard_map/half/pallas_call | solution.py:133
  66.1 4.0 %collective-permute-done.16.refs_2_ = bf16[256,2048]{1,0:T(8,128)(2,1)S(1)} collective-permute-done((bf16[256,2048]{1,0:T(8,128)(2,1)S(1)}, bf16[256,2048]{1,0:T(8,128)(2,1)S(1)}, u32[]{:S(2)}, u32[]{:S(2)}) %collective-permute-start.16) | collective-permute-done | bytes 1048608 | tf_op jit(solution)/shard_map/ppermute | solution.py:274
  70.0 2.5 %collective-permute-start.17 = (bf16[256,2048]{1,0:T(8,128)(2,1)S(1)}, bf16[256,2048]{1,0:T(8,128)(2,1)S(1)}, u32[]{:S(2)}, u32[]{:S(2)}) collective-permute-start(bf16[256,2048]{1,0:T(8,128)(2,1)S(1)} %collective-permute-done.16.refs_2_), channel_id=1, source_target_pairs={{0,16},{8,200},{16,0},{24,216},{32,48},{40,232},{48,32},{56,248},{... | collective-permute-start | bytes 3145736 | tf_op jit(solution)/shard_map/ppermute | solution.py:274
  72.5 7.2 %block.5 = (bf16[8,4,2,64,128]{4,3,2,1,0:T(8,128)(2,1)S(1)}, bf16[8,4,2,64,128]{4,3,2,1,0:T(8,128)(2,1)S(1)}, bf16[8,4,2,64,128]{4,3,2,1,0:T(8,128)(2,1)S(1)}, bf16[8,4,2,64,128]{4,3,2,1,0:T(8,128)(2,1)S(1)}) custom-call(s32[4]{0:T(128)S(1)} %copy-done.2, bf16[256,2048]{1,0:T(8,128)(2,1)S(1)} %collective-permute-done.15.refs_1_, ...), custom_call_target="tpu_custom_call" | custom-call | flops 4294967296 | bytes 10485760 | tf_op jit(solution)/shard_map/block/pallas_call | solution.py:204
  80.3 0.9 collective-permute-done.18.refs_0_
  81.2 1.3 %collective-permute-start.20 = (bf16[8,4,2,64,128]{4,3,2,1,0:T(8,128)(2,1)S(1)}, bf16[8,4,2,64,128]{4,3,2,1,0:T(8,128)(2,1)S(1)}, u32[]{:S(2)}, u32[]{:S(2)}) collective-permute-start(bf16[8,4,2,64,128]{4,3,2,1,0:T(8,128)(2,1)S(1)} %get-tuple-element.52), channel_id=1, source_target_pairs={{0,8},{8,0},{1,9},{9,1},{2,10},{10,2},{3,11},{11,3},{4,12},{12,4},... | collective-permute-start | bytes 3145736 | tf_op jit(solution)/shard_map/ppermute | solution.py:278
  82.5 2.9 %half.3.refs_2_ = f32[8,256,256]{2,1,0:T(8,128)S(1)} custom-call(bf16[256,2048]{1,0:T(8,128)(2,1)S(1)} %collective-permute-done.18.refs_0_, bf16[8,2048,256]{2,1,0:T(8,128)(2,1)S(1)} %couple.1.refs_3_.refs_2_.refs_4_.refs_1_), custom_call_target="tpu_custom_call" | custom-call | flops 2147483648 | bytes 10485760 | tf_op jit(solution)/shard_map/half/pallas_call | solution.py:133
  85.4 2.3 %block.7 = bf16[8,4,2,64,128]{4,3,2,1,0:T(8,128)(2,1)S(1)} custom-call(s32[4]{0:T(128)S(1)} %copy-done.2, bf16[256,2048]{1,0:T(8,128)(2,1)S(1)} %collective-permute-done.17.refs_1_, f32[8,256,256]{2,1,0:T(8,128)S(1)} %half.3.refs_2_, bf16[8,2048,256]{2,1,0:T(8,128)(2,1)S(1)} %couple.1.refs_3_.refs_2_.refs_4_.refs_1_), custom_call_target="tpu_custom_call" | custom-call | flops 1073741824 | bytes 10485760 | tf_op jit(solution)/shard_map/block/pallas_call | solution.py:204
  87.7 0.8 collective-permute-start.22
  88.4 2.3 %block.6.refs_3_ = bf16[8,4,2,64,128]{4,3,2,1,0:T(8,128)(2,1)S(1)} custom-call(s32[4]{0:T(128)S(1)} %copy-done.2, bf16[256,2048]{1,0:T(8,128)(2,1)S(1)} %collective-permute-done.17.refs_1_, f32[8,256,256]{2,1,0:T(8,128)S(1)} %half.3.refs_2_, bf16[8,2048,256]{2,1,0:T(8,128)(2,1)S(1)} %couple.1.refs_3_.refs_2_.refs_4_.refs_1_), custom_call_target="tpu_custom_call" | custom-call | flops 1073741824 | bytes 10485760 | tf_op jit(solution)/shard_map/block/pallas_call | solution.py:204
  90.8 3.7 %add.11 = bf16[8,16,2,64,128]{4,3,2,1,0:T(8,128)(2,1)} custom-call(s32[4]{0:T(128)S(1)} %copy-done.2, bf16[8,4,2,64,128]{4,3,2,1,0:T(8,128)(2,1)S(1)} %get-tuple-element.40.refs_0_, bf16[8,4,2,64,128]{4,3,2,1,0:T(8,128)(2,1)S(1)} %get-tuple-element.45.refs_1_, bf16[8,4,2,64,128]{4,3,2,1,0:T(8,128)(2,1)S(1)} %get-tuple-element.46.refs_2_, ...), custom_call_target="tpu_custom_call" | custom-call | flops 10000000 | bytes 13631488 | tf_op jit(solution)/shard_map/add/pallas_call | solution.py:240
  (48 shorter events, 5.8 us)
Async XLA Ops:
  0.0 12.9 %copy-start = (bf16[1024,128]{1,0:T(8,128)(2,1)S(1)}, bf16[1024,128]{1,0:T(8,128)(2,1)}, u32[]{:S(2)}) copy-start(bf16[1024,128]{1,0:T(8,128)(2,1)} %param.16) | copy-start | bytes 786436
  3.9 4.4 %collective-permute-start = (bf16[8,2048]{1,0:T(8,128)(2,1)}, bf16[8,2048]{1,0:T(8,128)(2,1)S(1)}, u32[]{:S(2)}, u32[]{:S(2)}) collective-permute-start(bf16[8,2048]{1,0:T(8,128)(2,1)} %get-tuple-element.31), channel_id=1, source_target_pairs={{0,8},{8,0},{1,9},{9,1},{2,10},{10,2},{3,11},{11,3},{4,12},{12,4},... | collective-permute-start | bytes 98312 | tf_op jit(solution)/shard_map/ppermute | solution.py:278
  7.2 8.2 %collective-permute-start.9 = (bf16[256,128]{1,0:T(8,128)(2,1)}, bf16[256,128]{1,0:T(8,128)(2,1)S(1)}, u32[]{:S(2)}, u32[]{:S(2)}) collective-permute-start(bf16[256,128]{1,0:T(8,128)(2,1)} %get-tuple-element.32.mine_ref), channel_id=1, source_target_pairs={{0,8},{8,0},{1,9},{9,1},{2,10},{10,2},{3,11},{11,3},{4,12},{12,4},... | collective-permute-start | bytes 196616 | tf_op jit(solution)/shard_map/ppermute | solution.py:278
  9.1 5.5 %collective-permute-start.1 = (bf16[16,2048]{1,0:T(8,128)(2,1)S(1)}, bf16[16,2048]{1,0:T(8,128)(2,1)S(1)}, u32[]{:S(2)}, u32[]{:S(2)}) collective-permute-start(bf16[16,2048]{1,0:T(8,128)(2,1)S(1)} %pad_maximum_fusion.2), channel_id=1, source_target_pairs={{0,1},{1,0},{2,3},{3,2},{4,5},{5,4},{6,7},{7,6},{8,15},{9,10},{10,... | collective-permute-start | bytes 196616 | tf_op jit(solution)/shard_map/ppermute | solution.py:263
  15.3 4.0 %collective-permute-start.2 = (bf16[32,2048]{1,0:T(8,128)(2,1)S(1)}, bf16[32,2048]{1,0:T(8,128)(2,1)S(1)}, u32[]{:S(2)}, u32[]{:S(2)}) collective-permute-start(bf16[32,2048]{1,0:T(8,128)(2,1)S(1)} %pad_maximum_fusion.1), channel_id=1, source_target_pairs={{0,7},{1,2},{2,1},{3,4},{4,3},{5,6},{6,5},{7,0},{8,9},{9,8},{10,11... | collective-permute-start | bytes 393224 | tf_op jit(solution)/shard_map/ppermute | solution.py:263
  15.5 0.8 copy-start.1
  16.3 12.0 %copy-start.3 = (f32[128]{0:T(128)S(1)}, f32[128]{0:T(128)}, u32[]{:S(2)}) copy-start(f32[128]{0:T(128)} %param.17) | copy-start | bytes 1540
  19.3 31.1 %copy-start.2 = (s32[4]{0:T(128)S(1)}, s32[4]{0:T(128)}, u32[]{:S(2)}) copy-start(s32[4]{0:T(128)} %pad_add_fusion.core_ref.refs_0_.at_ref) | copy-start | bytes 52
  19.3 5.1 %collective-permute-start.8 = (bf16[32,2048]{1,0:T(8,128)(2,1)S(1)}, bf16[32,2048]{1,0:T(8,128)(2,1)S(1)}, u32[]{:S(2)}, u32[]{:S(2)}) collective-permute-start(bf16[32,2048]{1,0:T(8,128)(2,1)S(1)} %collective-permute-done.2), channel_id=1, source_target_pairs={{0,1},{1,0},{2,3},{3,2},{4,5},{5,4},{6,7},{7,6},{8,15},{9,10},{10,... | collective-permute-start | bytes 393224 | tf_op jit(solution)/shard_map/ppermute | solution.py:263
  24.4 3.9 %collective-permute-start.10 = (bf16[32,2048]{1,0:T(8,128)(2,1)S(1)}, bf16[32,2048]{1,0:T(8,128)(2,1)S(1)}, u32[]{:S(2)}, u32[]{:S(2)}) collective-permute-start(bf16[32,2048]{1,0:T(8,128)(2,1)S(1)} %collective-permute-done.8), channel_id=1, source_target_pairs={{0,7},{1,2},{2,1},{3,4},{4,3},{5,6},{6,5},{7,0},{8,9},{9,8},{10,11... | collective-permute-start | bytes 393224 | tf_op jit(solution)/shard_map/ppermute | solution.py:263
  24.7 9.2 %collective-permute-start.3 = (bf16[64,2048]{1,0:T(8,128)(2,1)S(1)}, bf16[64,2048]{1,0:T(8,128)(2,1)S(1)}, u32[]{:S(2)}, u32[]{:S(2)}) collective-permute-start(bf16[64,2048]{1,0:T(8,128)(2,1)S(1)} %get-tuple-element.55), channel_id=1, source_target_pairs={{0,64},{8,56},{16,80},{24,40},{32,96},{40,24},{48,112},{56,8},{64,... | collective-permute-start | bytes 786440 | tf_op jit(solution)/shard_map/ppermute | solution.py:274
  27.2 7.9 %collective-permute-start.4 = (bf16[64,2048]{1,0:T(8,128)(2,1)S(1)}, bf16[64,2048]{1,0:T(8,128)(2,1)S(1)}, u32[]{:S(2)}, u32[]{:S(2)}) collective-permute-start(bf16[64,2048]{1,0:T(8,128)(2,1)S(1)} %get-tuple-element.55), channel_id=1, source_target_pairs={{0,192},{8,24},{16,208},{24,8},{32,224},{40,56},{48,240},{56,40},{... | collective-permute-start | bytes 786440 | tf_op jit(solution)/shard_map/ppermute | solution.py:274
  28.3 6.8 %collective-permute-start.11 = (f32[128]{0:T(128)S(1)}, f32[128]{0:T(128)S(1)}, u32[]{:S(2)}, u32[]{:S(2)}) collective-permute-start(f32[128]{0:T(128)S(1)} %copy-done.3), channel_id=1, source_target_pairs={{0,8},{8,0},{1,9},{9,1},{2,10},{10,2},{3,11},{11,3},{4,12},{12,4},... | collective-permute-start | bytes 1544 | tf_op jit(solution)/shard_map/ppermute | solution.py:278
  33.9 5.2 %collective-permute-start.5 = (bf16[64,2048]{1,0:T(8,128)(2,1)S(1)}, bf16[64,2048]{1,0:T(8,128)(2,1)S(1)}, u32[]{:S(2)}, u32[]{:S(2)}) collective-permute-start(bf16[64,2048]{1,0:T(8,128)(2,1)S(1)} %collective-permute-done.3), channel_id=1, source_target_pairs={{0,192},{8,24},{16,208},{24,8},{32,224},{40,56},{48,240},{56,40},{... | collective-permute-start | bytes 786440 | tf_op jit(solution)/shard_map/ppermute | solution.py:274
  35.2 12.1 %collective-permute-start.14 = (bf16[64,2048]{1,0:T(8,128)(2,1)S(1)}, bf16[64,2048]{1,0:T(8,128)(2,1)S(1)}, u32[]{:S(2)}, u32[]{:S(2)}) collective-permute-start(bf16[64,2048]{1,0:T(8,128)(2,1)S(1)} %pad_maximum_fusion), channel_id=1, source_target_pairs={{0,128},{8,40},{16,144},{24,56},{32,160},{40,8},{48,176},{56,24},{... | collective-permute-start | bytes 786440 | tf_op jit(solution)/shard_map/ppermute | solution.py:274
  37.7 9.5 %collective-permute-start.13 = (bf16[64,2048]{1,0:T(8,128)(2,1)S(1)}, bf16[64,2048]{1,0:T(8,128)(2,1)S(1)}, u32[]{:S(2)}, u32[]{:S(2)}) collective-permute-start(bf16[64,2048]{1,0:T(8,128)(2,1)S(1)} %pad_maximum_fusion), channel_id=1, source_target_pairs={{0,192},{8,24},{16,208},{24,8},{32,224},{40,56},{48,240},{56,40},{... | collective-permute-start | bytes 786440 | tf_op jit(solution)/shard_map/ppermute | solution.py:274
  37.8 9.5 %collective-permute-start.12 = (bf16[64,2048]{1,0:T(8,128)(2,1)S(1)}, bf16[64,2048]{1,0:T(8,128)(2,1)S(1)}, u32[]{:S(2)}, u32[]{:S(2)}) collective-permute-start(bf16[64,2048]{1,0:T(8,128)(2,1)S(1)} %pad_maximum_fusion), channel_id=1, source_target_pairs={{0,64},{8,56},{16,80},{24,40},{32,96},{40,24},{48,112},{56,8},{64,... | collective-permute-start | bytes 786440 | tf_op jit(solution)/shard_map/ppermute | solution.py:274
  39.1 19.6 %collective-permute-start.7 = (bf16[256,2048]{1,0:T(8,128)(2,1)S(1)}, bf16[256,2048]{1,0:T(8,128)(2,1)S(1)}, u32[]{:S(2)}, u32[]{:S(2)}) collective-permute-start(bf16[256,2048]{1,0:T(8,128)(2,1)S(1)} %constant_dynamic-update-slice_fusion.4.refs_1_), channel_id=1, source_target_pairs={{0,48},{8,72},{16,32},{24,88},{32,16},{40,104},{48,0},{56,120},{64... | collective-permute-start | bytes 3145736 | tf_op jit(solution)/shard_map/ppermute | solution.py:274
  40.5 20.5 %collective-permute-start.6 = (bf16[256,2048]{1,0:T(8,128)(2,1)S(1)}, bf16[256,2048]{1,0:T(8,128)(2,1)S(1)}, u32[]{:S(2)}, u32[]{:S(2)}) collective-permute-start(bf16[256,2048]{1,0:T(8,128)(2,1)S(1)} %constant_dynamic-update-slice_fusion.4.refs_1_), channel_id=1, source_target_pairs={{0,16},{8,200},{16,0},{24,216},{32,48},{40,232},{48,32},{56,248},{... | collective-permute-start | bytes 3145736 | tf_op jit(solution)/shard_map/ppermute | solution.py:274
  47.3 22.7 %collective-permute-start.16 = (bf16[256,2048]{1,0:T(8,128)(2,1)S(1)}, bf16[256,2048]{1,0:T(8,128)(2,1)S(1)}, u32[]{:S(2)}, u32[]{:S(2)}) collective-permute-start(bf16[256,2048]{1,0:T(8,128)(2,1)S(1)} %constant_dynamic-update-slice_fusion.11.refs_2_), channel_id=1, source_target_pairs={{0,48},{8,72},{16,32},{24,88},{32,16},{40,104},{48,0},{56,120},{64... | collective-permute-start | bytes 3145736 | tf_op jit(solution)/shard_map/ppermute | solution.py:274
  48.5 24.0 %collective-permute-start.15 = (bf16[256,2048]{1,0:T(8,128)(2,1)S(1)}, bf16[256,2048]{1,0:T(8,128)(2,1)S(1)}, u32[]{:S(2)}, u32[]{:S(2)}) collective-permute-start(bf16[256,2048]{1,0:T(8,128)(2,1)S(1)} %constant_dynamic-update-slice_fusion.11.refs_2_), channel_id=1, source_target_pairs={{0,16},{8,200},{16,0},{24,216},{32,48},{40,232},{48,32},{56,248},{... | collective-permute-start | bytes 3145736 | tf_op jit(solution)/shard_map/ppermute | solution.py:274
  61.0 20.2 %collective-permute-start.18 = (bf16[256,2048]{1,0:T(8,128)(2,1)S(1)}, bf16[256,2048]{1,0:T(8,128)(2,1)S(1)}, u32[]{:S(2)}, u32[]{:S(2)}) collective-permute-start(bf16[256,2048]{1,0:T(8,128)(2,1)S(1)} %collective-permute-done.6.refs_0_), channel_id=1, source_target_pairs={{0,48},{8,72},{16,32},{24,88},{32,16},{40,104},{48,0},{56,120},{64... | collective-permute-start | bytes 3145736 | tf_op jit(solution)/shard_map/ppermute | solution.py:274
  70.0 15.4 %collective-permute-start.17 = (bf16[256,2048]{1,0:T(8,128)(2,1)S(1)}, bf16[256,2048]{1,0:T(8,128)(2,1)S(1)}, u32[]{:S(2)}, u32[]{:S(2)}) collective-permute-start(bf16[256,2048]{1,0:T(8,128)(2,1)S(1)} %collective-permute-done.16.refs_2_), channel_id=1, source_target_pairs={{0,16},{8,200},{16,0},{24,216},{32,48},{40,232},{48,32},{56,248},{... | collective-permute-start | bytes 3145736 | tf_op jit(solution)/shard_map/ppermute | solution.py:274
  72.5 18.2 %collective-permute-start.19 = (bf16[8,4,2,64,128]{4,3,2,1,0:T(8,128)(2,1)S(1)}, bf16[8,4,2,64,128]{4,3,2,1,0:T(8,128)(2,1)S(1)}, u32[]{:S(2)}, u32[]{:S(2)}) collective-permute-start(bf16[8,4,2,64,128]{4,3,2,1,0:T(8,128)(2,1)S(1)} %get-tuple-element.51), channel_id=1, source_target_pairs={{0,8},{8,0},{1,9},{9,1},{2,10},{10,2},{3,11},{11,3},{4,12},{12,4},... | collective-permute-start | bytes 3145736 | tf_op jit(solution)/shard_map/ppermute | solution.py:278
  79.7 11.0 %collective-permute-start.21 = (bf16[8,4,2,64,128]{4,3,2,1,0:T(8,128)(2,1)S(1)}, bf16[8,4,2,64,128]{4,3,2,1,0:T(8,128)(2,1)S(1)}, u32[]{:S(2)}, u32[]{:S(2)}) collective-permute-start(bf16[8,4,2,64,128]{4,3,2,1,0:T(8,128)(2,1)S(1)} %get-tuple-element.53), channel_id=1, source_target_pairs={{0,8},{8,0},{1,9},{9,1},{2,10},{10,2},{3,11},{11,3},{4,12},{12,4},... | collective-permute-start | bytes 3145736 | tf_op jit(solution)/shard_map/ppermute | solution.py:278
  81.2 9.5 %collective-permute-start.20 = (bf16[8,4,2,64,128]{4,3,2,1,0:T(8,128)(2,1)S(1)}, bf16[8,4,2,64,128]{4,3,2,1,0:T(8,128)(2,1)S(1)}, u32[]{:S(2)}, u32[]{:S(2)}) collective-permute-start(bf16[8,4,2,64,128]{4,3,2,1,0:T(8,128)(2,1)S(1)} %get-tuple-element.52), channel_id=1, source_target_pairs={{0,8},{8,0},{1,9},{9,1},{2,10},{10,2},{3,11},{11,3},{4,12},{12,4},... | collective-permute-start | bytes 3145736 | tf_op jit(solution)/shard_map/ppermute | solution.py:278
  87.7 3.1 %collective-permute-start.22 = (bf16[8,4,2,64,128]{4,3,2,1,0:T(8,128)(2,1)S(1)}, bf16[8,4,2,64,128]{4,3,2,1,0:T(8,128)(2,1)S(1)}, u32[]{:S(2)}, u32[]{:S(2)}) collective-permute-start(bf16[8,4,2,64,128]{4,3,2,1,0:T(8,128)(2,1)S(1)} %block.7), channel_id=1, source_target_pairs={{0,8},{8,0},{1,9},{9,1},{2,10},{10,2},{3,11},{11,3},{4,12},{12,4},... | collective-permute-start | bytes 3145736 | tf_op jit(solution)/shard_map/ppermute | solution.py:278

commit v5 on v4

--- a/solution.py
+++ b/solution.py
@@ -106,7 +106,7 @@
 def place8(own, core, t):
     rel = jnp.where((own + core) % 2 == 0, t - own, own - t) & 7
     half, low = rel >> 1, rel & 1
-    return jnp.where(half == 0, low, jnp.where(half == 1, 4 + low, jnp.where(half == 2, 7 - low, 3 - low)))
+    return jnp.where(half == 0, low, jnp.where(half == 1, 4 + low, jnp.where(half == 2, 6 + low, 3 - low)))
 
 
 def place4(own, core, t):
@@ -260,8 +260,13 @@
 
 
 def along_z(v, step):
-    return lax.ppermute(
-        v, ("c", "z"), [(c * 8 + k, c * 8 + partner(k, 8, c, step)) for c in range(2) for k in range(8)])
+    pairs = []
+    for c in range(2):
+        for k in range(8):
+            ahead = 1 if (k + c) % 2 == 0 else -1
+            source = (k + (ahead, -ahead, 2 * ahead, 4)[step]) % 8
+            pairs.append((c * 8 + source, c * 8 + k))
+    return lax.ppermute(v, ("c", "z"), pairs)
 
 
 def along_plane(v, last, step):
@@ -296,12 +301,14 @@
     z1 = join(r, along_z(r, 0))
     z2 = along_z(z1, 1)
     h0 = join(z1, z2)
-    t = couple(swap(lt), lt, w)
-    z3, t = together(along_z(z2, 0), t)
+    h0, lt, lt_sibling = together(h0, lt, swap(lt))
+    t = couple(lt_sibling, lt, w)
+    z3 = along_z(z1, 2)
     m1_0 = along_plane(h0, False, 0)
     m2_0 = along_plane(h0, False, 1)
-    z4, offset = together(along_z(z3, 1), couple_offset)
-    m3_0 = along_plane(m1_0, False, 1)
+    m3_0 = along_plane(h0, False, 2)
+    z3, t = together(z3, t)
+    z4, offset, t = together(along_z(z1, 3), couple_offset, t)
     h1, offset = together(join(z3, z4), swap(offset))
     m1_1 = along_plane(h1, False, 0)
     m2_1 = along_plane(h1, False, 1)

time: 94.8 us -> 89.3 us (0.942)
  waiting for transfers between devices: 20 us -> 16.5 us
  starting transfers between devices: 34.5 us -> 32.5 us
    ppermute x7, starting transfers between devices: 11.6 us -> 8.45 us  [swap(): return lax.ppermute(v, 'c', [(0, 1), (1, 0)])]
    ppermute x4, waiting for transfers between devices: 4.99 us -> 1.97 us  [along_z(): return lax.ppermute(v, ('c', 'z'), pairs)]
    ppermute x12, waiting for transfers between devices: 14.8 us -> 13.1 us  [along_plane(): return lax.ppermute(v, ('y', 'x', 'c'), pairs)]
    ppermute x7, waiting for transfers between devices: 0.22 us -> 1.45 us  [swap(): return lax.ppermute(v, 'c', [(0, 1), (1, 0)])]
  transfers between devices with their start and end apart: 23 -> 23, of which waited for: 10 -> 10; matrix products, arithmetic and copies ran while one was open for 3% -> 2% of each run, Pallas kernels for 30% -> 32%
where the time goes in v5:
time: 89.3 us; the launch traced here: 88.9 us
  Pallas kernels  35.6 us (40%)
  starting transfers between devices  32.5 us (36%)
  waiting for transfers between devices  16.5 us (18%)
  other arithmetic  2.21 us (2%)
  local copies, waits for them, and re-layouts  1.82 us (2%)
    pallas_call x4, Pallas kernels, block(): pl.pallas_call(lambda *refs: block_kernel(first, count, ready is not None...  17.7 us
    ppermute x12, starting transfers between devices, along_plane(): return lax.ppermute(v, ('y', 'x', 'c'), pairs)  16.9 us
    ppermute x12, waiting for transfers between devices, along_plane(): return lax.ppermute(v, ('y', 'x', 'c'), pairs)  13.1 us
    ppermute x7, starting transfers between devices, swap(): return lax.ppermute(v, 'c', [(0, 1), (1, 0)])  8.45 us
    pallas_call x2, Pallas kernels, half(): pl.pallas_call(lambda *refs: half_kernel(count, *refs), grid=(4,), in_spe...  7.91 us
    ppermute x4, starting transfers between devices, along_z(): return lax.ppermute(v, ('c', 'z'), pairs)  7.18 us
    pallas_call x1, Pallas kernels, add(): pl.pallas_call(add_kernel, grid_spec=pltpu.PrefetchScalarGridSpec(num_sca...  3.69 us
    pallas_call x1, Pallas kernels, project(): pl.pallas_call(project_kernel, grid_spec=pltpu.PrefetchScalarGridSpec(num...  3.25 us
  transfers between devices with their start and end apart: 23, of which 10 were waited for; matrix products, arithmetic and copies ran while one was open for 2% of the time, Pallas kernels for 32%

profile of v5, /device:TPU:1, one launch (start us, length us, event | category | flops | bytes accessed | tf_op | source)
XLA Modules:
  0.0 88.9 jit_solution(17437944446705795303)
XLA Ops:
  0.7 3.2 %project.1 = (bf16[8,2048]{1,0:T(8,128)(2,1)}, bf16[8,2048]{1,0:T(8,128)(2,1)}, bf16[256,128]{1,0:T(8,128)(2,1)}) custom-call(s32[4]{0:T(128)} %pad_add_fusion.core_ref.refs_0_.at_ref, bf16[128,8,256]{2,1,0:T(8,128)(2,1)} %msa_in.1, f32[1,256]{1,0:T(1,128)} %bitcast.23, f32[1,256]{1,0:T(1,128)} %bitcast.24, bf16[32,256]{1,0:T(8,128)(2,1)} %bitcast.21, ...), custom_call_target="tpu_custom_call" | custom-call | tf_op jit(solution)/shard_map/project/pallas_call | solution.py:45
  3.9 3.3 %collective-permute-start = (bf16[8,2048]{1,0:T(8,128)(2,1)}, bf16[8,2048]{1,0:T(8,128)(2,1)S(1)}, u32[]{:S(2)}, u32[]{:S(2)}) collective-permute-start(bf16[8,2048]{1,0:T(8,128)(2,1)} %get-tuple-element.35), channel_id=1, source_target_pairs={{0,8},{8,0},{1,9},{9,1},{2,10},{10,2},{3,11},{11,3},{4,12},{12,4},... | collective-permute-start | bytes 98312 | tf_op jit(solution)/shard_map/ppermute | solution.py:283
  8.3 0.8 pad_maximum_fusion.2
  9.1 3.8 %collective-permute-start.1 = (bf16[16,2048]{1,0:T(8,128)(2,1)S(1)}, bf16[16,2048]{1,0:T(8,128)(2,1)S(1)}, u32[]{:S(2)}, u32[]{:S(2)}) collective-permute-start(bf16[16,2048]{1,0:T(8,128)(2,1)S(1)} %pad_maximum_fusion.2), channel_id=1, source_target_pairs={{1,0},{0,1},{3,2},{2,3},{5,4},{4,5},{7,6},{6,7},{15,8},{10,9},{9,1... | collective-permute-start | bytes 196616 | tf_op jit(solution)/shard_map/ppermute | solution.py:269
  12.9 1.6 %collective-permute-done.1 = bf16[16,2048]{1,0:T(8,128)(2,1)S(1)} collective-permute-done((bf16[16,2048]{1,0:T(8,128)(2,1)S(1)}, bf16[16,2048]{1,0:T(8,128)(2,1)S(1)}, u32[]{:S(2)}, u32[]{:S(2)}) %collective-permute-start.1) | collective-permute-done | bytes 65568 | tf_op jit(solution)/shard_map/ppermute | solution.py:269
  14.6 3.2 %collective-permute-start.3 = (bf16[256,128]{1,0:T(8,128)(2,1)}, bf16[256,128]{1,0:T(8,128)(2,1)S(1)}, u32[]{:S(2)}, u32[]{:S(2)}) collective-permute-start(bf16[256,128]{1,0:T(8,128)(2,1)} %get-tuple-element.39.mine_ref), channel_id=1, source_target_pairs={{0,8},{8,0},{1,9},{9,1},{2,10},{10,2},{3,11},{11,3},{4,12},{12,4},... | collective-permute-start | bytes 196616 | tf_op jit(solution)/shard_map/ppermute | solution.py:283
  17.9 1.2 %collective-permute-start.10 = (bf16[32,2048]{1,0:T(8,128)(2,1)S(1)}, bf16[32,2048]{1,0:T(8,128)(2,1)S(1)}, u32[]{:S(2)}, u32[]{:S(2)}) collective-permute-start(bf16[32,2048]{1,0:T(8,128)(2,1)S(1)} %constant_dynamic-update-slice_fusion), channel_id=1, source_target_pairs={{4,0},{5,1},{6,2},{7,3},{0,4},{1,5},{2,6},{3,7},{12,8},{13,9},{14,... | collective-permute-start | bytes 393224 | tf_op jit(solution)/shard_map/ppermute | solution.py:269
  19.1 2.1 %collective-permute-start.9 = (bf16[32,2048]{1,0:T(8,128)(2,1)S(1)}, bf16[32,2048]{1,0:T(8,128)(2,1)S(1)}, u32[]{:S(2)}, u32[]{:S(2)}) collective-permute-start(bf16[32,2048]{1,0:T(8,128)(2,1)S(1)} %constant_dynamic-update-slice_fusion), channel_id=1, source_target_pairs={{2,0},{7,1},{4,2},{1,3},{6,4},{3,5},{0,6},{5,7},{14,8},{11,9},{8,1... | collective-permute-start | bytes 393224 | tf_op jit(solution)/shard_map/ppermute | solution.py:269
  21.2 0.8 pad_maximum_fusion
  22.0 2.8 %collective-permute-start.6 = (bf16[64,2048]{1,0:T(8,128)(2,1)S(1)}, bf16[64,2048]{1,0:T(8,128)(2,1)S(1)}, u32[]{:S(2)}, u32[]{:S(2)}) collective-permute-start(bf16[64,2048]{1,0:T(8,128)(2,1)S(1)} %pad_maximum_fusion), channel_id=1, source_target_pairs={{0,128},{8,40},{16,144},{24,56},{32,160},{40,8},{48,176},{56,24},{... | collective-permute-start | bytes 786440 | tf_op jit(solution)/shard_map/ppermute | solution.py:279
  25.7 0.8 copy-done.1
  26.5 3.0 %couple.1.refs_3_.refs_2_.refs_4_.refs_1_ = bf16[8,2048,256]{2,1,0:T(8,128)(2,1)S(1)} custom-call(bf16[256,128]{1,0:T(8,128)(2,1)S(1)} %collective-permute-done.3.theirs_ref, bf16[256,128]{1,0:T(8,128)(2,1)S(1)} %copy-done.1, bf16[32,2048]{1,0:T(8,128)(2,1)S(1)} %bitcast.18), custom_call_target="tpu_custom_call" | custom-call | flops 268435456 | bytes 9437184 | tf_op jit(solution)/shard_map/couple/pallas_call | solution.py:90
  29.9 1.2 %collective-permute-start.11 = (f32[128]{0:T(128)S(1)}, f32[128]{0:T(128)S(1)}, u32[]{:S(2)}, u32[]{:S(2)}) collective-permute-start(f32[128]{0:T(128)S(1)} %copy-done.3), channel_id=1, source_target_pairs={{0,8},{8,0},{1,9},{9,1},{2,10},{10,2},{3,11},{11,3},{4,12},{12,4},... | collective-permute-start | bytes 1544 | tf_op jit(solution)/shard_map/ppermute | solution.py:283
  31.1 0.8 collective-permute-done.11
  31.9 2.7 %collective-permute-start.14 = (bf16[64,2048]{1,0:T(8,128)(2,1)S(1)}, bf16[64,2048]{1,0:T(8,128)(2,1)S(1)}, u32[]{:S(2)}, u32[]{:S(2)}) collective-permute-start(bf16[64,2048]{1,0:T(8,128)(2,1)S(1)} %pad_maximum_fusion.1), channel_id=1, source_target_pairs={{0,128},{8,40},{16,144},{24,56},{32,160},{40,8},{48,176},{56,24},{... | collective-permute-start | bytes 786440 | tf_op jit(solution)/shard_map/ppermute | solution.py:279
  35.8 1.4 %collective-permute-start.8 = (bf16[256,2048]{1,0:T(8,128)(2,1)S(1)}, bf16[256,2048]{1,0:T(8,128)(2,1)S(1)}, u32[]{:S(2)}, u32[]{:S(2)}) collective-permute-start(bf16[256,2048]{1,0:T(8,128)(2,1)S(1)} %constant_dynamic-update-slice_fusion.3.refs_1_), channel_id=1, source_target_pairs={{0,48},{8,72},{16,32},{24,88},{32,16},{40,104},{48,0},{56,120},{64... | collective-permute-start | bytes 3145736 | tf_op jit(solution)/shard_map/ppermute | solution.py:279
  37.1 1.9 %collective-permute-start.7 = (bf16[256,2048]{1,0:T(8,128)(2,1)S(1)}, bf16[256,2048]{1,0:T(8,128)(2,1)S(1)}, u32[]{:S(2)}, u32[]{:S(2)}) collective-permute-start(bf16[256,2048]{1,0:T(8,128)(2,1)S(1)} %constant_dynamic-update-slice_fusion.3.refs_1_), channel_id=1, source_target_pairs={{0,16},{8,200},{16,0},{24,216},{32,48},{40,232},{48,32},{56,248},{... | collective-permute-start | bytes 3145736 | tf_op jit(solution)/shard_map/ppermute | solution.py:279
  39.0 3.4 %collective-permute-done.12 = bf16[64,2048]{1,0:T(8,128)(2,1)S(1)} collective-permute-done((bf16[64,2048]{1,0:T(8,128)(2,1)S(1)}, bf16[64,2048]{1,0:T(8,128)(2,1)S(1)}, u32[]{:S(2)}, u32[]{:S(2)}) %collective-permute-start.12) | collective-permute-done | bytes 262176 | tf_op jit(solution)/shard_map/ppermute | solution.py:279
  42.5 0.9 %collective-permute-start.16 = (bf16[256,2048]{1,0:T(8,128)(2,1)S(1)}, bf16[256,2048]{1,0:T(8,128)(2,1)S(1)}, u32[]{:S(2)}, u32[]{:S(2)}) collective-permute-start(bf16[256,2048]{1,0:T(8,128)(2,1)S(1)} %constant_dynamic-update-slice_fusion.7.refs_2_), channel_id=1, source_target_pairs={{0,48},{8,72},{16,32},{24,88},{32,16},{40,104},{48,0},{56,120},{64... | collective-permute-start | bytes 3145736 | tf_op jit(solution)/shard_map/ppermute | solution.py:279
  43.5 2.9 %collective-permute-start.15 = (bf16[256,2048]{1,0:T(8,128)(2,1)S(1)}, bf16[256,2048]{1,0:T(8,128)(2,1)S(1)}, u32[]{:S(2)}, u32[]{:S(2)}) collective-permute-start(bf16[256,2048]{1,0:T(8,128)(2,1)S(1)} %constant_dynamic-update-slice_fusion.7.refs_2_), channel_id=1, source_target_pairs={{0,16},{8,200},{16,0},{24,216},{32,48},{40,232},{48,32},{56,248},{... | collective-permute-start | bytes 3145736 | tf_op jit(solution)/shard_map/ppermute | solution.py:279
  46.4 6.0 %block.4 = (bf16[8,4,2,64,128]{4,3,2,1,0:T(8,128)(2,1)S(1)}, bf16[8,4,2,64,128]{4,3,2,1,0:T(8,128)(2,1)S(1)}) custom-call(s32[4]{0:T(128)S(1)} %copy-done.2, bf16[256,2048]{1,0:T(8,128)(2,1)S(1)} %constant_dynamic-update-slice_fusion.3.refs_1_, bf16[256,2048]{1,0:T(8,128)(2,1)S(1)} %constant_dynamic-update-slice_fusion.7.refs_2_, ...), custom_call_target="tpu_custom_call" | custom-call | flops 4294967296 | bytes 10485760 | tf_op jit(solution)/shard_map/block/pallas_call | solution.py:204
  52.4 1.7 %collective-permute-done.8.refs_1_ = bf16[256,2048]{1,0:T(8,128)(2,1)S(1)} collective-permute-done((bf16[256,2048]{1,0:T(8,128)(2,1)S(1)}, bf16[256,2048]{1,0:T(8,128)(2,1)S(1)}, u32[]{:S(2)}, u32[]{:S(2)}) %collective-permute-start.8) | collective-permute-done | bytes 1048608 | tf_op jit(solution)/shard_map/ppermute | solution.py:279
  54.1 1.1 %collective-permute-start.18 = (bf16[256,2048]{1,0:T(8,128)(2,1)S(1)}, bf16[256,2048]{1,0:T(8,128)(2,1)S(1)}, u32[]{:S(2)}, u32[]{:S(2)}) collective-permute-start(bf16[256,2048]{1,0:T(8,128)(2,1)S(1)} %collective-permute-done.7.refs_0_), channel_id=1, source_target_pairs={{0,48},{8,72},{16,32},{24,88},{32,16},{40,104},{48,0},{56,120},{64... | collective-permute-start | bytes 3145736 | tf_op jit(solution)/shard_map/ppermute | solution.py:279
  55.2 5.0 %half.2.refs_3_ = f32[8,512,256]{2,1,0:T(8,128)S(1)} custom-call(bf16[256,2048]{1,0:T(8,128)(2,1)S(1)} %collective-permute-done.7.refs_0_, bf16[256,2048]{1,0:T(8,128)(2,1)S(1)} %collective-permute-done.8.refs_1_, bf16[8,2048,256]{2,1,0:T(8,128)(2,1)S(1)} %couple.1.refs_3_.refs_2_.refs_4_.refs_1_), custom_call_target="tpu_custom_call" | custom-call | flops 4294967296 | bytes 10485760 | tf_op jit(solution)/shard_map/half/pallas_call | solution.py:133
  60.3 5.1 %collective-permute-done.16.refs_2_ = bf16[256,2048]{1,0:T(8,128)(2,1)S(1)} collective-permute-done((bf16[256,2048]{1,0:T(8,128)(2,1)S(1)}, bf16[256,2048]{1,0:T(8,128)(2,1)S(1)}, u32[]{:S(2)}, u32[]{:S(2)}) %collective-permute-start.16) | collective-permute-done | bytes 1048608 | tf_op jit(solution)/shard_map/ppermute | solution.py:279
  65.3 1.2 %collective-permute-start.17 = (bf16[256,2048]{1,0:T(8,128)(2,1)S(1)}, bf16[256,2048]{1,0:T(8,128)(2,1)S(1)}, u32[]{:S(2)}, u32[]{:S(2)}) collective-permute-start(bf16[256,2048]{1,0:T(8,128)(2,1)S(1)} %collective-permute-done.16.refs_2_), channel_id=1, source_target_pairs={{0,16},{8,200},{16,0},{24,216},{32,48},{40,232},{48,32},{56,248},{... | collective-permute-start | bytes 3145736 | tf_op jit(solution)/shard_map/ppermute | solution.py:279
  66.6 7.2 %block.5 = (bf16[8,4,2,64,128]{4,3,2,1,0:T(8,128)(2,1)S(1)}, bf16[8,4,2,64,128]{4,3,2,1,0:T(8,128)(2,1)S(1)}, bf16[8,4,2,64,128]{4,3,2,1,0:T(8,128)(2,1)S(1)}, bf16[8,4,2,64,128]{4,3,2,1,0:T(8,128)(2,1)S(1)}) custom-call(s32[4]{0:T(128)S(1)} %copy-done.2, bf16[256,2048]{1,0:T(8,128)(2,1)S(1)} %collective-permute-done.15.refs_1_, ...), custom_call_target="tpu_custom_call" | custom-call | flops 4294967296 | bytes 10485760 | tf_op jit(solution)/shard_map/block/pallas_call | solution.py:204
  74.4 2.2 %collective-permute-done.18.refs_0_ = bf16[256,2048]{1,0:T(8,128)(2,1)S(1)} collective-permute-done((bf16[256,2048]{1,0:T(8,128)(2,1)S(1)}, bf16[256,2048]{1,0:T(8,128)(2,1)S(1)}, u32[]{:S(2)}, u32[]{:S(2)}) %collective-permute-start.18) | collective-permute-done | bytes 1048608 | tf_op jit(solution)/shard_map/ppermute | solution.py:279
  76.6 2.9 %half.3.refs_2_ = f32[8,256,256]{2,1,0:T(8,128)S(1)} custom-call(bf16[256,2048]{1,0:T(8,128)(2,1)S(1)} %collective-permute-done.18.refs_0_, bf16[8,2048,256]{2,1,0:T(8,128)(2,1)S(1)} %couple.1.refs_3_.refs_2_.refs_4_.refs_1_), custom_call_target="tpu_custom_call" | custom-call | flops 2147483648 | bytes 10485760 | tf_op jit(solution)/shard_map/half/pallas_call | solution.py:133
  80.2 2.3 %block.7 = bf16[8,4,2,64,128]{4,3,2,1,0:T(8,128)(2,1)S(1)} custom-call(s32[4]{0:T(128)S(1)} %copy-done.2, bf16[256,2048]{1,0:T(8,128)(2,1)S(1)} %collective-permute-done.17.refs_1_, f32[8,256,256]{2,1,0:T(8,128)S(1)} %half.3.refs_2_, bf16[8,2048,256]{2,1,0:T(8,128)(2,1)S(1)} %couple.1.refs_3_.refs_2_.refs_4_.refs_1_), custom_call_target="tpu_custom_call" | custom-call | flops 1073741824 | bytes 10485760 | tf_op jit(solution)/shard_map/block/pallas_call | solution.py:204
  82.6 2.3 %block.6.refs_3_ = bf16[8,4,2,64,128]{4,3,2,1,0:T(8,128)(2,1)S(1)} custom-call(s32[4]{0:T(128)S(1)} %copy-done.2, bf16[256,2048]{1,0:T(8,128)(2,1)S(1)} %collective-permute-done.17.refs_1_, f32[8,256,256]{2,1,0:T(8,128)S(1)} %half.3.refs_2_, bf16[8,2048,256]{2,1,0:T(8,128)(2,1)S(1)} %couple.1.refs_3_.refs_2_.refs_4_.refs_1_), custom_call_target="tpu_custom_call" | custom-call | flops 1073741824 | bytes 10485760 | tf_op jit(solution)/shard_map/block/pallas_call | solution.py:204
  85.2 3.7 %add.11 = bf16[8,16,2,64,128]{4,3,2,1,0:T(8,128)(2,1)} custom-call(s32[4]{0:T(128)S(1)} %copy-done.2, bf16[8,4,2,64,128]{4,3,2,1,0:T(8,128)(2,1)S(1)} %get-tuple-element.48.refs_0_, bf16[8,4,2,64,128]{4,3,2,1,0:T(8,128)(2,1)S(1)} %get-tuple-element.53.refs_1_, bf16[8,4,2,64,128]{4,3,2,1,0:T(8,128)(2,1)S(1)} %get-tuple-element.54.refs_2_, ...), custom_call_target="tpu_custom_call" | custom-call | flops 10000000 | bytes 13631488 | tf_op jit(solution)/shard_map/add/pallas_call | solution.py:240
  (48 shorter events, 5.9 us)
Async XLA Ops:
  0.0 17.8 %copy-start = (bf16[1024,128]{1,0:T(8,128)(2,1)S(1)}, bf16[1024,128]{1,0:T(8,128)(2,1)}, u32[]{:S(2)}) copy-start(bf16[1024,128]{1,0:T(8,128)(2,1)} %param.16) | copy-start | bytes 786436
  3.9 4.4 %collective-permute-start = (bf16[8,2048]{1,0:T(8,128)(2,1)}, bf16[8,2048]{1,0:T(8,128)(2,1)S(1)}, u32[]{:S(2)}, u32[]{:S(2)}) collective-permute-start(bf16[8,2048]{1,0:T(8,128)(2,1)} %get-tuple-element.35), channel_id=1, source_target_pairs={{0,8},{8,0},{1,9},{9,1},{2,10},{10,2},{3,11},{11,3},{4,12},{12,4},... | collective-permute-start | bytes 98312 | tf_op jit(solution)/shard_map/ppermute | solution.py:283
  9.1 5.5 %collective-permute-start.1 = (bf16[16,2048]{1,0:T(8,128)(2,1)S(1)}, bf16[16,2048]{1,0:T(8,128)(2,1)S(1)}, u32[]{:S(2)}, u32[]{:S(2)}) collective-permute-start(bf16[16,2048]{1,0:T(8,128)(2,1)S(1)} %pad_maximum_fusion.2), channel_id=1, source_target_pairs={{1,0},{0,1},{3,2},{2,3},{5,4},{4,5},{7,6},{6,7},{15,8},{10,9},{9,1... | collective-permute-start | bytes 196616 | tf_op jit(solution)/shard_map/ppermute | solution.py:269
  14.6 6.6 %collective-permute-start.2 = (bf16[32,2048]{1,0:T(8,128)(2,1)S(1)}, bf16[32,2048]{1,0:T(8,128)(2,1)S(1)}, u32[]{:S(2)}, u32[]{:S(2)}) collective-permute-start(bf16[32,2048]{1,0:T(8,128)(2,1)S(1)} %constant_dynamic-update-slice_fusion), channel_id=1, source_target_pairs={{7,0},{2,1},{1,2},{4,3},{3,4},{6,5},{5,6},{0,7},{9,8},{8,9},{11,10... | collective-permute-start | bytes 393224 | tf_op jit(solution)/shard_map/ppermute | solution.py:269
  14.6 7.4 %collective-permute-start.3 = (bf16[256,128]{1,0:T(8,128)(2,1)}, bf16[256,128]{1,0:T(8,128)(2,1)S(1)}, u32[]{:S(2)}, u32[]{:S(2)}) collective-permute-start(bf16[256,128]{1,0:T(8,128)(2,1)} %get-tuple-element.39.mine_ref), channel_id=1, source_target_pairs={{0,8},{8,0},{1,9},{9,1},{2,10},{10,2},{3,11},{11,3},{4,12},{12,4},... | collective-permute-start | bytes 196616 | tf_op jit(solution)/shard_map/ppermute | solution.py:283
  17.9 12.0 %collective-permute-start.10 = (bf16[32,2048]{1,0:T(8,128)(2,1)S(1)}, bf16[32,2048]{1,0:T(8,128)(2,1)S(1)}, u32[]{:S(2)}, u32[]{:S(2)}) collective-permute-start(bf16[32,2048]{1,0:T(8,128)(2,1)S(1)} %constant_dynamic-update-slice_fusion), channel_id=1, source_target_pairs={{4,0},{5,1},{6,2},{7,3},{0,4},{1,5},{2,6},{3,7},{12,8},{13,9},{14,... | collective-permute-start | bytes 393224 | tf_op jit(solution)/shard_map/ppermute | solution.py:269
  19.1 10.4 %collective-permute-start.9 = (bf16[32,2048]{1,0:T(8,128)(2,1)S(1)}, bf16[32,2048]{1,0:T(8,128)(2,1)S(1)}, u32[]{:S(2)}, u32[]{:S(2)}) collective-permute-start(bf16[32,2048]{1,0:T(8,128)(2,1)S(1)} %constant_dynamic-update-slice_fusion), channel_id=1, source_target_pairs={{2,0},{7,1},{4,2},{1,3},{6,4},{3,5},{0,6},{5,7},{14,8},{11,9},{8,1... | collective-permute-start | bytes 393224 | tf_op jit(solution)/shard_map/ppermute | solution.py:269
  22.0 13.7 %collective-permute-start.6 = (bf16[64,2048]{1,0:T(8,128)(2,1)S(1)}, bf16[64,2048]{1,0:T(8,128)(2,1)S(1)}, u32[]{:S(2)}, u32[]{:S(2)}) collective-permute-start(bf16[64,2048]{1,0:T(8,128)(2,1)S(1)} %pad_maximum_fusion), channel_id=1, source_target_pairs={{0,128},{8,40},{16,144},{24,56},{32,160},{40,8},{48,176},{56,24},{... | collective-permute-start | bytes 786440 | tf_op jit(solution)/shard_map/ppermute | solution.py:279
  24.8 10.8 %collective-permute-start.5 = (bf16[64,2048]{1,0:T(8,128)(2,1)S(1)}, bf16[64,2048]{1,0:T(8,128)(2,1)S(1)}, u32[]{:S(2)}, u32[]{:S(2)}) collective-permute-start(bf16[64,2048]{1,0:T(8,128)(2,1)S(1)} %pad_maximum_fusion), channel_id=1, source_target_pairs={{0,192},{8,24},{16,208},{24,8},{32,224},{40,56},{48,240},{56,40},{... | collective-permute-start | bytes 786440 | tf_op jit(solution)/shard_map/ppermute | solution.py:279
  25.2 9.9 %collective-permute-start.4 = (bf16[64,2048]{1,0:T(8,128)(2,1)S(1)}, bf16[64,2048]{1,0:T(8,128)(2,1)S(1)}, u32[]{:S(2)}, u32[]{:S(2)}) collective-permute-start(bf16[64,2048]{1,0:T(8,128)(2,1)S(1)} %pad_maximum_fusion), channel_id=1, source_target_pairs={{0,64},{8,56},{16,80},{24,40},{32,96},{40,24},{48,112},{56,8},{64,... | collective-permute-start | bytes 786440 | tf_op jit(solution)/shard_map/ppermute | solution.py:279
  25.7 0.8 copy-start.1
  26.5 3.4 %copy-start.3 = (f32[128]{0:T(128)S(1)}, f32[128]{0:T(128)}, u32[]{:S(2)}) copy-start(f32[128]{0:T(128)} %param.17) | copy-start | bytes 1540
  29.5 16.9 %copy-start.2 = (s32[4]{0:T(128)S(1)}, s32[4]{0:T(128)}, u32[]{:S(2)}) copy-start(s32[4]{0:T(128)} %pad_add_fusion.core_ref.refs_0_.at_ref) | copy-start | bytes 52
  29.9 2.0 %collective-permute-start.11 = (f32[128]{0:T(128)S(1)}, f32[128]{0:T(128)S(1)}, u32[]{:S(2)}, u32[]{:S(2)}) collective-permute-start(f32[128]{0:T(128)S(1)} %copy-done.3), channel_id=1, source_target_pairs={{0,8},{8,0},{1,9},{9,1},{2,10},{10,2},{3,11},{11,3},{4,12},{12,4},... | collective-permute-start | bytes 1544 | tf_op jit(solution)/shard_map/ppermute | solution.py:283
  31.9 10.5 %collective-permute-start.14 = (bf16[64,2048]{1,0:T(8,128)(2,1)S(1)}, bf16[64,2048]{1,0:T(8,128)(2,1)S(1)}, u32[]{:S(2)}, u32[]{:S(2)}) collective-permute-start(bf16[64,2048]{1,0:T(8,128)(2,1)S(1)} %pad_maximum_fusion.1), channel_id=1, source_target_pairs={{0,128},{8,40},{16,144},{24,56},{32,160},{40,8},{48,176},{56,24},{... | collective-permute-start | bytes 786440 | tf_op jit(solution)/shard_map/ppermute | solution.py:279
  34.7 7.8 %collective-permute-start.13 = (bf16[64,2048]{1,0:T(8,128)(2,1)S(1)}, bf16[64,2048]{1,0:T(8,128)(2,1)S(1)}, u32[]{:S(2)}, u32[]{:S(2)}) collective-permute-start(bf16[64,2048]{1,0:T(8,128)(2,1)S(1)} %pad_maximum_fusion.1), channel_id=1, source_target_pairs={{0,192},{8,24},{16,208},{24,8},{32,224},{40,56},{48,240},{56,40},{... | collective-permute-start | bytes 786440 | tf_op jit(solution)/shard_map/ppermute | solution.py:279
  35.0 7.4 %collective-permute-start.12 = (bf16[64,2048]{1,0:T(8,128)(2,1)S(1)}, bf16[64,2048]{1,0:T(8,128)(2,1)S(1)}, u32[]{:S(2)}, u32[]{:S(2)}) collective-permute-start(bf16[64,2048]{1,0:T(8,128)(2,1)S(1)} %pad_maximum_fusion.1), channel_id=1, source_target_pairs={{0,64},{8,56},{16,80},{24,40},{32,96},{40,24},{48,112},{56,8},{64,... | collective-permute-start | bytes 786440 | tf_op jit(solution)/shard_map/ppermute | solution.py:279
  35.8 18.3 %collective-permute-start.8 = (bf16[256,2048]{1,0:T(8,128)(2,1)S(1)}, bf16[256,2048]{1,0:T(8,128)(2,1)S(1)}, u32[]{:S(2)}, u32[]{:S(2)}) collective-permute-start(bf16[256,2048]{1,0:T(8,128)(2,1)S(1)} %constant_dynamic-update-slice_fusion.3.refs_1_), channel_id=1, source_target_pairs={{0,48},{8,72},{16,32},{24,88},{32,16},{40,104},{48,0},{56,120},{64... | collective-permute-start | bytes 3145736 | tf_op jit(solution)/shard_map/ppermute | solution.py:279
  37.1 17.0 %collective-permute-start.7 = (bf16[256,2048]{1,0:T(8,128)(2,1)S(1)}, bf16[256,2048]{1,0:T(8,128)(2,1)S(1)}, u32[]{:S(2)}, u32[]{:S(2)}) collective-permute-start(bf16[256,2048]{1,0:T(8,128)(2,1)S(1)} %constant_dynamic-update-slice_fusion.3.refs_1_), channel_id=1, source_target_pairs={{0,16},{8,200},{16,0},{24,216},{32,48},{40,232},{48,32},{56,248},{... | collective-permute-start | bytes 3145736 | tf_op jit(solution)/shard_map/ppermute | solution.py:279
  42.5 22.8 %collective-permute-start.16 = (bf16[256,2048]{1,0:T(8,128)(2,1)S(1)}, bf16[256,2048]{1,0:T(8,128)(2,1)S(1)}, u32[]{:S(2)}, u32[]{:S(2)}) collective-permute-start(bf16[256,2048]{1,0:T(8,128)(2,1)S(1)} %constant_dynamic-update-slice_fusion.7.refs_2_), channel_id=1, source_target_pairs={{0,48},{8,72},{16,32},{24,88},{32,16},{40,104},{48,0},{56,120},{64... | collective-permute-start | bytes 3145736 | tf_op jit(solution)/shard_map/ppermute | solution.py:279
  43.5 23.1 %collective-permute-start.15 = (bf16[256,2048]{1,0:T(8,128)(2,1)S(1)}, bf16[256,2048]{1,0:T(8,128)(2,1)S(1)}, u32[]{:S(2)}, u32[]{:S(2)}) collective-permute-start(bf16[256,2048]{1,0:T(8,128)(2,1)S(1)} %constant_dynamic-update-slice_fusion.7.refs_2_), channel_id=1, source_target_pairs={{0,16},{8,200},{16,0},{24,216},{32,48},{40,232},{48,32},{56,248},{... | collective-permute-start | bytes 3145736 | tf_op jit(solution)/shard_map/ppermute | solution.py:279
  54.1 22.5 %collective-permute-start.18 = (bf16[256,2048]{1,0:T(8,128)(2,1)S(1)}, bf16[256,2048]{1,0:T(8,128)(2,1)S(1)}, u32[]{:S(2)}, u32[]{:S(2)}) collective-permute-start(bf16[256,2048]{1,0:T(8,128)(2,1)S(1)} %collective-permute-done.7.refs_0_), channel_id=1, source_target_pairs={{0,48},{8,72},{16,32},{24,88},{32,16},{40,104},{48,0},{56,120},{64... | collective-permute-start | bytes 3145736 | tf_op jit(solution)/shard_map/ppermute | solution.py:279
  65.3 14.9 %collective-permute-start.17 = (bf16[256,2048]{1,0:T(8,128)(2,1)S(1)}, bf16[256,2048]{1,0:T(8,128)(2,1)S(1)}, u32[]{:S(2)}, u32[]{:S(2)}) collective-permute-start(bf16[256,2048]{1,0:T(8,128)(2,1)S(1)} %collective-permute-done.16.refs_2_), channel_id=1, source_target_pairs={{0,16},{8,200},{16,0},{24,216},{32,48},{40,232},{48,32},{56,248},{... | collective-permute-start | bytes 3145736 | tf_op jit(solution)/shard_map/ppermute | solution.py:279
  66.6 18.3 %collective-permute-start.19 = (bf16[8,4,2,64,128]{4,3,2,1,0:T(8,128)(2,1)S(1)}, bf16[8,4,2,64,128]{4,3,2,1,0:T(8,128)(2,1)S(1)}, u32[]{:S(2)}, u32[]{:S(2)}) collective-permute-start(bf16[8,4,2,64,128]{4,3,2,1,0:T(8,128)(2,1)S(1)} %get-tuple-element.59), channel_id=1, source_target_pairs={{0,8},{8,0},{1,9},{9,1},{2,10},{10,2},{3,11},{11,3},{4,12},{12,4},... | collective-permute-start | bytes 3145736 | tf_op jit(solution)/shard_map/ppermute | solution.py:283
  73.8 11.1 %collective-permute-start.21 = (bf16[8,4,2,64,128]{4,3,2,1,0:T(8,128)(2,1)S(1)}, bf16[8,4,2,64,128]{4,3,2,1,0:T(8,128)(2,1)S(1)}, u32[]{:S(2)}, u32[]{:S(2)}) collective-permute-start(bf16[8,4,2,64,128]{4,3,2,1,0:T(8,128)(2,1)S(1)} %get-tuple-element.61), channel_id=1, source_target_pairs={{0,8},{8,0},{1,9},{9,1},{2,10},{10,2},{3,11},{11,3},{4,12},{12,4},... | collective-permute-start | bytes 3145736 | tf_op jit(solution)/shard_map/ppermute | solution.py:283
  76.6 8.3 %collective-permute-start.20 = (bf16[8,4,2,64,128]{4,3,2,1,0:T(8,128)(2,1)S(1)}, bf16[8,4,2,64,128]{4,3,2,1,0:T(8,128)(2,1)S(1)}, u32[]{:S(2)}, u32[]{:S(2)}) collective-permute-start(bf16[8,4,2,64,128]{4,3,2,1,0:T(8,128)(2,1)S(1)} %get-tuple-element.60), channel_id=1, source_target_pairs={{0,8},{8,0},{1,9},{9,1},{2,10},{10,2},{3,11},{11,3},{4,12},{12,4},... | collective-permute-start | bytes 3145736 | tf_op jit(solution)/shard_map/ppermute | solution.py:283
  82.5 2.7 %collective-permute-start.22 = (bf16[8,4,2,64,128]{4,3,2,1,0:T(8,128)(2,1)S(1)}, bf16[8,4,2,64,128]{4,3,2,1,0:T(8,128)(2,1)S(1)}, u32[]{:S(2)}, u32[]{:S(2)}) collective-permute-start(bf16[8,4,2,64,128]{4,3,2,1,0:T(8,128)(2,1)S(1)} %block.7), channel_id=1, source_target_pairs={{0,8},{8,0},{1,9},{9,1},{2,10},{10,2},{3,11},{11,3},{4,12},{12,4},... | collective-permute-start | bytes 3145736 | tf_op jit(solution)/shard_map/ppermute | solution.py:283

commit v6 on v5

--- a/solution.py
+++ b/solution.py
@@ -231,7 +231,7 @@
         for m in range(4):
             b = holder4(minor, 1 - core, m)
             group = jnp.where(core == 0, b * 4 + a, a * 4 + b)
-            for i in range(2):
+            for i in range(4):
                 v = mine[k][i, b].astype(F32) + theirs[m][i, a].astype(F32)
                 o_ref[i, group] = (v.reshape(128, CZ) + bias).astype(BF16).reshape(2, 64, CZ)
 
@@ -241,10 +241,10 @@
         add_kernel,
         grid_spec=pltpu.PrefetchScalarGridSpec(
             num_scalar_prefetch=1,
-            grid=(LOCAL // 2,),
-            in_specs=[pl.BlockSpec((2, 4, 2, 64, CZ), lambda n, at: (n, 0, 0, 0, 0))] * 8
+            grid=(2,),
+            in_specs=[pl.BlockSpec((4, 4, 2, 64, CZ), lambda n, at: (n, 0, 0, 0, 0))] * 8
             + [pl.BlockSpec((1, CZ), lambda n, at: (0, 0))],
-            out_specs=pl.BlockSpec((2, 16, 2, 64, CZ), lambda n, at: (n, 0, 0, 0, 0)),
+            out_specs=pl.BlockSpec((4, 16, 2, 64, CZ), lambda n, at: (n, 0, 0, 0, 0)),
         ),
         out_shape=jax.ShapeDtypeStruct((LOCAL, 16, 2, 64, CZ), BF16),
         compiler_params=pltpu.CompilerParams(vmem_limit_bytes=24 * MIB),

time: 89.3 us -> 88.8 us (level)
  no operation moved by 1% of the time
where the time goes in v6:
time: 88.8 us; the launch traced here: 88.4 us
  Pallas kernels  35.1 us (40%)
  starting transfers between devices  32.5 us (37%)
  waiting for transfers between devices  16.5 us (19%)
  other arithmetic  2.21 us (2%)
  local copies, waits for them, and re-layouts  1.82 us (2%)
    pallas_call x4, Pallas kernels, block(): pl.pallas_call(lambda *refs: block_kernel(first, count, ready is not None...  17.7 us
    ppermute x12, starting transfers between devices, along_plane(): return lax.ppermute(v, ('y', 'x', 'c'), pairs)  16.9 us
    ppermute x12, waiting for transfers between devices, along_plane(): return lax.ppermute(v, ('y', 'x', 'c'), pairs)  13.1 us
    ppermute x7, starting transfers between devices, swap(): return lax.ppermute(v, 'c', [(0, 1), (1, 0)])  8.45 us
    pallas_call x2, Pallas kernels, half(): pl.pallas_call(lambda *refs: half_kernel(count, *refs), grid=(4,), in_spe...  7.91 us
    ppermute x4, starting transfers between devices, along_z(): return lax.ppermute(v, ('c', 'z'), pairs)  7.18 us
    pallas_call x1, Pallas kernels, project(): pl.pallas_call(project_kernel, grid_spec=pltpu.PrefetchScalarGridSpec(num...  3.25 us
    pallas_call x1, Pallas kernels, add(): pl.pallas_call(add_kernel, grid_spec=pltpu.PrefetchScalarGridSpec(num_sca...  3.2 us
  transfers between devices with their start and end apart: 23, of which 10 were waited for; matrix products, arithmetic and copies ran while one was open for 2% of the time, Pallas kernels for 32%

profile of v6, /device:TPU:1, one launch (start us, length us, event | category | flops | bytes accessed | tf_op | source)
XLA Modules:
  0.0 88.4 jit_solution(3384254091840744260)
XLA Ops:
  0.7 3.2 %project.1 = (bf16[8,2048]{1,0:T(8,128)(2,1)}, bf16[8,2048]{1,0:T(8,128)(2,1)}, bf16[256,128]{1,0:T(8,128)(2,1)}) custom-call(s32[4]{0:T(128)} %pad_add_fusion.core_ref.refs_0_.at_ref, bf16[128,8,256]{2,1,0:T(8,128)(2,1)} %msa_in.1, f32[1,256]{1,0:T(1,128)} %bitcast.23, f32[1,256]{1,0:T(1,128)} %bitcast.24, bf16[32,256]{1,0:T(8,128)(2,1)} %bitcast.21, ...), custom_call_target="tpu_custom_call" | custom-call | tf_op jit(solution)/shard_map/project/pallas_call | solution.py:45
  3.9 3.3 %collective-permute-start = (bf16[8,2048]{1,0:T(8,128)(2,1)}, bf16[8,2048]{1,0:T(8,128)(2,1)S(1)}, u32[]{:S(2)}, u32[]{:S(2)}) collective-permute-start(bf16[8,2048]{1,0:T(8,128)(2,1)} %get-tuple-element.35), channel_id=1, source_target_pairs={{0,8},{8,0},{1,9},{9,1},{2,10},{10,2},{3,11},{11,3},{4,12},{12,4},... | collective-permute-start | bytes 98312 | tf_op jit(solution)/shard_map/ppermute | solution.py:283
  8.3 0.8 pad_maximum_fusion.2
  9.1 3.8 %collective-permute-start.1 = (bf16[16,2048]{1,0:T(8,128)(2,1)S(1)}, bf16[16,2048]{1,0:T(8,128)(2,1)S(1)}, u32[]{:S(2)}, u32[]{:S(2)}) collective-permute-start(bf16[16,2048]{1,0:T(8,128)(2,1)S(1)} %pad_maximum_fusion.2), channel_id=1, source_target_pairs={{1,0},{0,1},{3,2},{2,3},{5,4},{4,5},{7,6},{6,7},{15,8},{10,9},{9,1... | collective-permute-start | bytes 196616 | tf_op jit(solution)/shard_map/ppermute | solution.py:269
  12.9 1.6 %collective-permute-done.1 = bf16[16,2048]{1,0:T(8,128)(2,1)S(1)} collective-permute-done((bf16[16,2048]{1,0:T(8,128)(2,1)S(1)}, bf16[16,2048]{1,0:T(8,128)(2,1)S(1)}, u32[]{:S(2)}, u32[]{:S(2)}) %collective-permute-start.1) | collective-permute-done | bytes 65568 | tf_op jit(solution)/shard_map/ppermute | solution.py:269
  14.6 3.2 %collective-permute-start.3 = (bf16[256,128]{1,0:T(8,128)(2,1)}, bf16[256,128]{1,0:T(8,128)(2,1)S(1)}, u32[]{:S(2)}, u32[]{:S(2)}) collective-permute-start(bf16[256,128]{1,0:T(8,128)(2,1)} %get-tuple-element.39.mine_ref), channel_id=1, source_target_pairs={{0,8},{8,0},{1,9},{9,1},{2,10},{10,2},{3,11},{11,3},{4,12},{12,4},... | collective-permute-start | bytes 196616 | tf_op jit(solution)/shard_map/ppermute | solution.py:283
  17.9 1.2 %collective-permute-start.10 = (bf16[32,2048]{1,0:T(8,128)(2,1)S(1)}, bf16[32,2048]{1,0:T(8,128)(2,1)S(1)}, u32[]{:S(2)}, u32[]{:S(2)}) collective-permute-start(bf16[32,2048]{1,0:T(8,128)(2,1)S(1)} %constant_dynamic-update-slice_fusion), channel_id=1, source_target_pairs={{4,0},{5,1},{6,2},{7,3},{0,4},{1,5},{2,6},{3,7},{12,8},{13,9},{14,... | collective-permute-start | bytes 393224 | tf_op jit(solution)/shard_map/ppermute | solution.py:269
  19.1 2.1 %collective-permute-start.9 = (bf16[32,2048]{1,0:T(8,128)(2,1)S(1)}, bf16[32,2048]{1,0:T(8,128)(2,1)S(1)}, u32[]{:S(2)}, u32[]{:S(2)}) collective-permute-start(bf16[32,2048]{1,0:T(8,128)(2,1)S(1)} %constant_dynamic-update-slice_fusion), channel_id=1, source_target_pairs={{2,0},{7,1},{4,2},{1,3},{6,4},{3,5},{0,6},{5,7},{14,8},{11,9},{8,1... | collective-permute-start | bytes 393224 | tf_op jit(solution)/shard_map/ppermute | solution.py:269
  21.2 0.8 pad_maximum_fusion
  22.0 2.8 %collective-permute-start.6 = (bf16[64,2048]{1,0:T(8,128)(2,1)S(1)}, bf16[64,2048]{1,0:T(8,128)(2,1)S(1)}, u32[]{:S(2)}, u32[]{:S(2)}) collective-permute-start(bf16[64,2048]{1,0:T(8,128)(2,1)S(1)} %pad_maximum_fusion), channel_id=1, source_target_pairs={{0,128},{8,40},{16,144},{24,56},{32,160},{40,8},{48,176},{56,24},{... | collective-permute-start | bytes 786440 | tf_op jit(solution)/shard_map/ppermute | solution.py:279
  25.7 0.8 copy-done.1
  26.5 3.0 %couple.1.refs_3_.refs_2_.refs_4_.refs_1_ = bf16[8,2048,256]{2,1,0:T(8,128)(2,1)S(1)} custom-call(bf16[256,128]{1,0:T(8,128)(2,1)S(1)} %collective-permute-done.3.theirs_ref, bf16[256,128]{1,0:T(8,128)(2,1)S(1)} %copy-done.1, bf16[32,2048]{1,0:T(8,128)(2,1)S(1)} %bitcast.18), custom_call_target="tpu_custom_call" | custom-call | flops 268435456 | bytes 9437184 | tf_op jit(solution)/shard_map/couple/pallas_call | solution.py:90
  29.9 1.2 %collective-permute-start.11 = (f32[128]{0:T(128)S(1)}, f32[128]{0:T(128)S(1)}, u32[]{:S(2)}, u32[]{:S(2)}) collective-permute-start(f32[128]{0:T(128)S(1)} %copy-done.3), channel_id=1, source_target_pairs={{0,8},{8,0},{1,9},{9,1},{2,10},{10,2},{3,11},{11,3},{4,12},{12,4},... | collective-permute-start | bytes 1544 | tf_op jit(solution)/shard_map/ppermute | solution.py:283
  31.1 0.8 collective-permute-done.11
  31.9 2.7 %collective-permute-start.14 = (bf16[64,2048]{1,0:T(8,128)(2,1)S(1)}, bf16[64,2048]{1,0:T(8,128)(2,1)S(1)}, u32[]{:S(2)}, u32[]{:S(2)}) collective-permute-start(bf16[64,2048]{1,0:T(8,128)(2,1)S(1)} %pad_maximum_fusion.1), channel_id=1, source_target_pairs={{0,128},{8,40},{16,144},{24,56},{32,160},{40,8},{48,176},{56,24},{... | collective-permute-start | bytes 786440 | tf_op jit(solution)/shard_map/ppermute | solution.py:279
  35.8 1.4 %collective-permute-start.8 = (bf16[256,2048]{1,0:T(8,128)(2,1)S(1)}, bf16[256,2048]{1,0:T(8,128)(2,1)S(1)}, u32[]{:S(2)}, u32[]{:S(2)}) collective-permute-start(bf16[256,2048]{1,0:T(8,128)(2,1)S(1)} %constant_dynamic-update-slice_fusion.3.refs_1_), channel_id=1, source_target_pairs={{0,48},{8,72},{16,32},{24,88},{32,16},{40,104},{48,0},{56,120},{64... | collective-permute-start | bytes 3145736 | tf_op jit(solution)/shard_map/ppermute | solution.py:279
  37.1 1.9 %collective-permute-start.7 = (bf16[256,2048]{1,0:T(8,128)(2,1)S(1)}, bf16[256,2048]{1,0:T(8,128)(2,1)S(1)}, u32[]{:S(2)}, u32[]{:S(2)}) collective-permute-start(bf16[256,2048]{1,0:T(8,128)(2,1)S(1)} %constant_dynamic-update-slice_fusion.3.refs_1_), channel_id=1, source_target_pairs={{0,16},{8,200},{16,0},{24,216},{32,48},{40,232},{48,32},{56,248},{... | collective-permute-start | bytes 3145736 | tf_op jit(solution)/shard_map/ppermute | solution.py:279
  39.0 3.4 %collective-permute-done.12 = bf16[64,2048]{1,0:T(8,128)(2,1)S(1)} collective-permute-done((bf16[64,2048]{1,0:T(8,128)(2,1)S(1)}, bf16[64,2048]{1,0:T(8,128)(2,1)S(1)}, u32[]{:S(2)}, u32[]{:S(2)}) %collective-permute-start.12) | collective-permute-done | bytes 262176 | tf_op jit(solution)/shard_map/ppermute | solution.py:279
  42.5 0.9 %collective-permute-start.16 = (bf16[256,2048]{1,0:T(8,128)(2,1)S(1)}, bf16[256,2048]{1,0:T(8,128)(2,1)S(1)}, u32[]{:S(2)}, u32[]{:S(2)}) collective-permute-start(bf16[256,2048]{1,0:T(8,128)(2,1)S(1)} %constant_dynamic-update-slice_fusion.7.refs_2_), channel_id=1, source_target_pairs={{0,48},{8,72},{16,32},{24,88},{32,16},{40,104},{48,0},{56,120},{64... | collective-permute-start | bytes 3145736 | tf_op jit(solution)/shard_map/ppermute | solution.py:279
  43.5 2.9 %collective-permute-start.15 = (bf16[256,2048]{1,0:T(8,128)(2,1)S(1)}, bf16[256,2048]{1,0:T(8,128)(2,1)S(1)}, u32[]{:S(2)}, u32[]{:S(2)}) collective-permute-start(bf16[256,2048]{1,0:T(8,128)(2,1)S(1)} %constant_dynamic-update-slice_fusion.7.refs_2_), channel_id=1, source_target_pairs={{0,16},{8,200},{16,0},{24,216},{32,48},{40,232},{48,32},{56,248},{... | collective-permute-start | bytes 3145736 | tf_op jit(solution)/shard_map/ppermute | solution.py:279
  46.4 6.0 %block.4 = (bf16[8,4,2,64,128]{4,3,2,1,0:T(8,128)(2,1)S(1)}, bf16[8,4,2,64,128]{4,3,2,1,0:T(8,128)(2,1)S(1)}) custom-call(s32[4]{0:T(128)S(1)} %copy-done.2, bf16[256,2048]{1,0:T(8,128)(2,1)S(1)} %constant_dynamic-update-slice_fusion.3.refs_1_, bf16[256,2048]{1,0:T(8,128)(2,1)S(1)} %constant_dynamic-update-slice_fusion.7.refs_2_, ...), custom_call_target="tpu_custom_call" | custom-call | flops 4294967296 | bytes 10485760 | tf_op jit(solution)/shard_map/block/pallas_call | solution.py:204
  52.4 1.7 %collective-permute-done.8.refs_1_ = bf16[256,2048]{1,0:T(8,128)(2,1)S(1)} collective-permute-done((bf16[256,2048]{1,0:T(8,128)(2,1)S(1)}, bf16[256,2048]{1,0:T(8,128)(2,1)S(1)}, u32[]{:S(2)}, u32[]{:S(2)}) %collective-permute-start.8) | collective-permute-done | bytes 1048608 | tf_op jit(solution)/shard_map/ppermute | solution.py:279
  54.1 1.1 %collective-permute-start.18 = (bf16[256,2048]{1,0:T(8,128)(2,1)S(1)}, bf16[256,2048]{1,0:T(8,128)(2,1)S(1)}, u32[]{:S(2)}, u32[]{:S(2)}) collective-permute-start(bf16[256,2048]{1,0:T(8,128)(2,1)S(1)} %collective-permute-done.7.refs_0_), channel_id=1, source_target_pairs={{0,48},{8,72},{16,32},{24,88},{32,16},{40,104},{48,0},{56,120},{64... | collective-permute-start | bytes 3145736 | tf_op jit(solution)/shard_map/ppermute | solution.py:279
  55.2 5.0 %half.2.refs_3_ = f32[8,512,256]{2,1,0:T(8,128)S(1)} custom-call(bf16[256,2048]{1,0:T(8,128)(2,1)S(1)} %collective-permute-done.7.refs_0_, bf16[256,2048]{1,0:T(8,128)(2,1)S(1)} %collective-permute-done.8.refs_1_, bf16[8,2048,256]{2,1,0:T(8,128)(2,1)S(1)} %couple.1.refs_3_.refs_2_.refs_4_.refs_1_), custom_call_target="tpu_custom_call" | custom-call | flops 4294967296 | bytes 10485760 | tf_op jit(solution)/shard_map/half/pallas_call | solution.py:133
  60.3 5.1 %collective-permute-done.16.refs_2_ = bf16[256,2048]{1,0:T(8,128)(2,1)S(1)} collective-permute-done((bf16[256,2048]{1,0:T(8,128)(2,1)S(1)}, bf16[256,2048]{1,0:T(8,128)(2,1)S(1)}, u32[]{:S(2)}, u32[]{:S(2)}) %collective-permute-start.16) | collective-permute-done | bytes 1048608 | tf_op jit(solution)/shard_map/ppermute | solution.py:279
  65.3 1.2 %collective-permute-start.17 = (bf16[256,2048]{1,0:T(8,128)(2,1)S(1)}, bf16[256,2048]{1,0:T(8,128)(2,1)S(1)}, u32[]{:S(2)}, u32[]{:S(2)}) collective-permute-start(bf16[256,2048]{1,0:T(8,128)(2,1)S(1)} %collective-permute-done.16.refs_2_), channel_id=1, source_target_pairs={{0,16},{8,200},{16,0},{24,216},{32,48},{40,232},{48,32},{56,248},{... | collective-permute-start | bytes 3145736 | tf_op jit(solution)/shard_map/ppermute | solution.py:279
  66.6 7.2 %block.5 = (bf16[8,4,2,64,128]{4,3,2,1,0:T(8,128)(2,1)S(1)}, bf16[8,4,2,64,128]{4,3,2,1,0:T(8,128)(2,1)S(1)}, bf16[8,4,2,64,128]{4,3,2,1,0:T(8,128)(2,1)S(1)}, bf16[8,4,2,64,128]{4,3,2,1,0:T(8,128)(2,1)S(1)}) custom-call(s32[4]{0:T(128)S(1)} %copy-done.2, bf16[256,2048]{1,0:T(8,128)(2,1)S(1)} %collective-permute-done.15.refs_1_, ...), custom_call_target="tpu_custom_call" | custom-call | flops 4294967296 | bytes 10485760 | tf_op jit(solution)/shard_map/block/pallas_call | solution.py:204
  74.4 2.2 %collective-permute-done.18.refs_0_ = bf16[256,2048]{1,0:T(8,128)(2,1)S(1)} collective-permute-done((bf16[256,2048]{1,0:T(8,128)(2,1)S(1)}, bf16[256,2048]{1,0:T(8,128)(2,1)S(1)}, u32[]{:S(2)}, u32[]{:S(2)}) %collective-permute-start.18) | collective-permute-done | bytes 1048608 | tf_op jit(solution)/shard_map/ppermute | solution.py:279
  76.6 2.9 %half.3.refs_2_ = f32[8,256,256]{2,1,0:T(8,128)S(1)} custom-call(bf16[256,2048]{1,0:T(8,128)(2,1)S(1)} %collective-permute-done.18.refs_0_, bf16[8,2048,256]{2,1,0:T(8,128)(2,1)S(1)} %couple.1.refs_3_.refs_2_.refs_4_.refs_1_), custom_call_target="tpu_custom_call" | custom-call | flops 2147483648 | bytes 10485760 | tf_op jit(solution)/shard_map/half/pallas_call | solution.py:133
  80.2 2.3 %block.7 = bf16[8,4,2,64,128]{4,3,2,1,0:T(8,128)(2,1)S(1)} custom-call(s32[4]{0:T(128)S(1)} %copy-done.2, bf16[256,2048]{1,0:T(8,128)(2,1)S(1)} %collective-permute-done.17.refs_1_, f32[8,256,256]{2,1,0:T(8,128)S(1)} %half.3.refs_2_, bf16[8,2048,256]{2,1,0:T(8,128)(2,1)S(1)} %couple.1.refs_3_.refs_2_.refs_4_.refs_1_), custom_call_target="tpu_custom_call" | custom-call | flops 1073741824 | bytes 10485760 | tf_op jit(solution)/shard_map/block/pallas_call | solution.py:204
  82.6 2.3 %block.6.refs_3_ = bf16[8,4,2,64,128]{4,3,2,1,0:T(8,128)(2,1)S(1)} custom-call(s32[4]{0:T(128)S(1)} %copy-done.2, bf16[256,2048]{1,0:T(8,128)(2,1)S(1)} %collective-permute-done.17.refs_1_, f32[8,256,256]{2,1,0:T(8,128)S(1)} %half.3.refs_2_, bf16[8,2048,256]{2,1,0:T(8,128)(2,1)S(1)} %couple.1.refs_3_.refs_2_.refs_4_.refs_1_), custom_call_target="tpu_custom_call" | custom-call | flops 1073741824 | bytes 10485760 | tf_op jit(solution)/shard_map/block/pallas_call | solution.py:204
  85.2 3.2 %add.11 = bf16[8,16,2,64,128]{4,3,2,1,0:T(8,128)(2,1)} custom-call(s32[4]{0:T(128)S(1)} %copy-done.2, bf16[8,4,2,64,128]{4,3,2,1,0:T(8,128)(2,1)S(1)} %get-tuple-element.48.refs_0_, bf16[8,4,2,64,128]{4,3,2,1,0:T(8,128)(2,1)S(1)} %get-tuple-element.53.refs_1_, bf16[8,4,2,64,128]{4,3,2,1,0:T(8,128)(2,1)S(1)} %get-tuple-element.54.refs_2_, ...), custom_call_target="tpu_custom_call" | custom-call | flops 10000000 | bytes 13631488 | tf_op jit(solution)/shard_map/add/pallas_call | solution.py:240
  (48 shorter events, 5.9 us)
Async XLA Ops:
  0.0 17.8 %copy-start = (bf16[1024,128]{1,0:T(8,128)(2,1)S(1)}, bf16[1024,128]{1,0:T(8,128)(2,1)}, u32[]{:S(2)}) copy-start(bf16[1024,128]{1,0:T(8,128)(2,1)} %param.16) | copy-start | bytes 786436
  3.9 4.4 %collective-permute-start = (bf16[8,2048]{1,0:T(8,128)(2,1)}, bf16[8,2048]{1,0:T(8,128)(2,1)S(1)}, u32[]{:S(2)}, u32[]{:S(2)}) collective-permute-start(bf16[8,2048]{1,0:T(8,128)(2,1)} %get-tuple-element.35), channel_id=1, source_target_pairs={{0,8},{8,0},{1,9},{9,1},{2,10},{10,2},{3,11},{11,3},{4,12},{12,4},... | collective-permute-start | bytes 98312 | tf_op jit(solution)/shard_map/ppermute | solution.py:283
  9.1 5.5 %collective-permute-start.1 = (bf16[16,2048]{1,0:T(8,128)(2,1)S(1)}, bf16[16,2048]{1,0:T(8,128)(2,1)S(1)}, u32[]{:S(2)}, u32[]{:S(2)}) collective-permute-start(bf16[16,2048]{1,0:T(8,128)(2,1)S(1)} %pad_maximum_fusion.2), channel_id=1, source_target_pairs={{1,0},{0,1},{3,2},{2,3},{5,4},{4,5},{7,6},{6,7},{15,8},{10,9},{9,1... | collective-permute-start | bytes 196616 | tf_op jit(solution)/shard_map/ppermute | solution.py:269
  14.6 6.6 %collective-permute-start.2 = (bf16[32,2048]{1,0:T(8,128)(2,1)S(1)}, bf16[32,2048]{1,0:T(8,128)(2,1)S(1)}, u32[]{:S(2)}, u32[]{:S(2)}) collective-permute-start(bf16[32,2048]{1,0:T(8,128)(2,1)S(1)} %constant_dynamic-update-slice_fusion), channel_id=1, source_target_pairs={{7,0},{2,1},{1,2},{4,3},{3,4},{6,5},{5,6},{0,7},{9,8},{8,9},{11,10... | collective-permute-start | bytes 393224 | tf_op jit(solution)/shard_map/ppermute | solution.py:269
  14.6 7.4 %collective-permute-start.3 = (bf16[256,128]{1,0:T(8,128)(2,1)}, bf16[256,128]{1,0:T(8,128)(2,1)S(1)}, u32[]{:S(2)}, u32[]{:S(2)}) collective-permute-start(bf16[256,128]{1,0:T(8,128)(2,1)} %get-tuple-element.39.mine_ref), channel_id=1, source_target_pairs={{0,8},{8,0},{1,9},{9,1},{2,10},{10,2},{3,11},{11,3},{4,12},{12,4},... | collective-permute-start | bytes 196616 | tf_op jit(solution)/shard_map/ppermute | solution.py:283
  17.9 12.0 %collective-permute-start.10 = (bf16[32,2048]{1,0:T(8,128)(2,1)S(1)}, bf16[32,2048]{1,0:T(8,128)(2,1)S(1)}, u32[]{:S(2)}, u32[]{:S(2)}) collective-permute-start(bf16[32,2048]{1,0:T(8,128)(2,1)S(1)} %constant_dynamic-update-slice_fusion), channel_id=1, source_target_pairs={{4,0},{5,1},{6,2},{7,3},{0,4},{1,5},{2,6},{3,7},{12,8},{13,9},{14,... | collective-permute-start | bytes 393224 | tf_op jit(solution)/shard_map/ppermute | solution.py:269
  19.1 10.4 %collective-permute-start.9 = (bf16[32,2048]{1,0:T(8,128)(2,1)S(1)}, bf16[32,2048]{1,0:T(8,128)(2,1)S(1)}, u32[]{:S(2)}, u32[]{:S(2)}) collective-permute-start(bf16[32,2048]{1,0:T(8,128)(2,1)S(1)} %constant_dynamic-update-slice_fusion), channel_id=1, source_target_pairs={{2,0},{7,1},{4,2},{1,3},{6,4},{3,5},{0,6},{5,7},{14,8},{11,9},{8,1... | collective-permute-start | bytes 393224 | tf_op jit(solution)/shard_map/ppermute | solution.py:269
  22.0 13.7 %collective-permute-start.6 = (bf16[64,2048]{1,0:T(8,128)(2,1)S(1)}, bf16[64,2048]{1,0:T(8,128)(2,1)S(1)}, u32[]{:S(2)}, u32[]{:S(2)}) collective-permute-start(bf16[64,2048]{1,0:T(8,128)(2,1)S(1)} %pad_maximum_fusion), channel_id=1, source_target_pairs={{0,128},{8,40},{16,144},{24,56},{32,160},{40,8},{48,176},{56,24},{... | collective-permute-start | bytes 786440 | tf_op jit(solution)/shard_map/ppermute | solution.py:279
  24.8 10.8 %collective-permute-start.5 = (bf16[64,2048]{1,0:T(8,128)(2,1)S(1)}, bf16[64,2048]{1,0:T(8,128)(2,1)S(1)}, u32[]{:S(2)}, u32[]{:S(2)}) collective-permute-start(bf16[64,2048]{1,0:T(8,128)(2,1)S(1)} %pad_maximum_fusion), channel_id=1, source_target_pairs={{0,192},{8,24},{16,208},{24,8},{32,224},{40,56},{48,240},{56,40},{... | collective-permute-start | bytes 786440 | tf_op jit(solution)/shard_map/ppermute | solution.py:279
  25.2 9.9 %collective-permute-start.4 = (bf16[64,2048]{1,0:T(8,128)(2,1)S(1)}, bf16[64,2048]{1,0:T(8,128)(2,1)S(1)}, u32[]{:S(2)}, u32[]{:S(2)}) collective-permute-start(bf16[64,2048]{1,0:T(8,128)(2,1)S(1)} %pad_maximum_fusion), channel_id=1, source_target_pairs={{0,64},{8,56},{16,80},{24,40},{32,96},{40,24},{48,112},{56,8},{64,... | collective-permute-start | bytes 786440 | tf_op jit(solution)/shard_map/ppermute | solution.py:279
  25.7 0.8 copy-start.1
  26.5 3.4 %copy-start.3 = (f32[128]{0:T(128)S(1)}, f32[128]{0:T(128)}, u32[]{:S(2)}) copy-start(f32[128]{0:T(128)} %param.17) | copy-start | bytes 1540
  29.5 16.9 %copy-start.2 = (s32[4]{0:T(128)S(1)}, s32[4]{0:T(128)}, u32[]{:S(2)}) copy-start(s32[4]{0:T(128)} %pad_add_fusion.core_ref.refs_0_.at_ref) | copy-start | bytes 52
  29.9 2.0 %collective-permute-start.11 = (f32[128]{0:T(128)S(1)}, f32[128]{0:T(128)S(1)}, u32[]{:S(2)}, u32[]{:S(2)}) collective-permute-start(f32[128]{0:T(128)S(1)} %copy-done.3), channel_id=1, source_target_pairs={{0,8},{8,0},{1,9},{9,1},{2,10},{10,2},{3,11},{11,3},{4,12},{12,4},... | collective-permute-start | bytes 1544 | tf_op jit(solution)/shard_map/ppermute | solution.py:283
  31.9 10.5 %collective-permute-start.14 = (bf16[64,2048]{1,0:T(8,128)(2,1)S(1)}, bf16[64,2048]{1,0:T(8,128)(2,1)S(1)}, u32[]{:S(2)}, u32[]{:S(2)}) collective-permute-start(bf16[64,2048]{1,0:T(8,128)(2,1)S(1)} %pad_maximum_fusion.1), channel_id=1, source_target_pairs={{0,128},{8,40},{16,144},{24,56},{32,160},{40,8},{48,176},{56,24},{... | collective-permute-start | bytes 786440 | tf_op jit(solution)/shard_map/ppermute | solution.py:279
  34.7 7.8 %collective-permute-start.13 = (bf16[64,2048]{1,0:T(8,128)(2,1)S(1)}, bf16[64,2048]{1,0:T(8,128)(2,1)S(1)}, u32[]{:S(2)}, u32[]{:S(2)}) collective-permute-start(bf16[64,2048]{1,0:T(8,128)(2,1)S(1)} %pad_maximum_fusion.1), channel_id=1, source_target_pairs={{0,192},{8,24},{16,208},{24,8},{32,224},{40,56},{48,240},{56,40},{... | collective-permute-start | bytes 786440 | tf_op jit(solution)/shard_map/ppermute | solution.py:279
  35.0 7.4 %collective-permute-start.12 = (bf16[64,2048]{1,0:T(8,128)(2,1)S(1)}, bf16[64,2048]{1,0:T(8,128)(2,1)S(1)}, u32[]{:S(2)}, u32[]{:S(2)}) collective-permute-start(bf16[64,2048]{1,0:T(8,128)(2,1)S(1)} %pad_maximum_fusion.1), channel_id=1, source_target_pairs={{0,64},{8,56},{16,80},{24,40},{32,96},{40,24},{48,112},{56,8},{64,... | collective-permute-start | bytes 786440 | tf_op jit(solution)/shard_map/ppermute | solution.py:279
  35.8 18.3 %collective-permute-start.8 = (bf16[256,2048]{1,0:T(8,128)(2,1)S(1)}, bf16[256,2048]{1,0:T(8,128)(2,1)S(1)}, u32[]{:S(2)}, u32[]{:S(2)}) collective-permute-start(bf16[256,2048]{1,0:T(8,128)(2,1)S(1)} %constant_dynamic-update-slice_fusion.3.refs_1_), channel_id=1, source_target_pairs={{0,48},{8,72},{16,32},{24,88},{32,16},{40,104},{48,0},{56,120},{64... | collective-permute-start | bytes 3145736 | tf_op jit(solution)/shard_map/ppermute | solution.py:279
  37.1 17.0 %collective-permute-start.7 = (bf16[256,2048]{1,0:T(8,128)(2,1)S(1)}, bf16[256,2048]{1,0:T(8,128)(2,1)S(1)}, u32[]{:S(2)}, u32[]{:S(2)}) collective-permute-start(bf16[256,2048]{1,0:T(8,128)(2,1)S(1)} %constant_dynamic-update-slice_fusion.3.refs_1_), channel_id=1, source_target_pairs={{0,16},{8,200},{16,0},{24,216},{32,48},{40,232},{48,32},{56,248},{... | collective-permute-start | bytes 3145736 | tf_op jit(solution)/shard_map/ppermute | solution.py:279
  42.5 22.8 %collective-permute-start.16 = (bf16[256,2048]{1,0:T(8,128)(2,1)S(1)}, bf16[256,2048]{1,0:T(8,128)(2,1)S(1)}, u32[]{:S(2)}, u32[]{:S(2)}) collective-permute-start(bf16[256,2048]{1,0:T(8,128)(2,1)S(1)} %constant_dynamic-update-slice_fusion.7.refs_2_), channel_id=1, source_target_pairs={{0,48},{8,72},{16,32},{24,88},{32,16},{40,104},{48,0},{56,120},{64... | collective-permute-start | bytes 3145736 | tf_op jit(solution)/shard_map/ppermute | solution.py:279
  43.5 23.1 %collective-permute-start.15 = (bf16[256,2048]{1,0:T(8,128)(2,1)S(1)}, bf16[256,2048]{1,0:T(8,128)(2,1)S(1)}, u32[]{:S(2)}, u32[]{:S(2)}) collective-permute-start(bf16[256,2048]{1,0:T(8,128)(2,1)S(1)} %constant_dynamic-update-slice_fusion.7.refs_2_), channel_id=1, source_target_pairs={{0,16},{8,200},{16,0},{24,216},{32,48},{40,232},{48,32},{56,248},{... | collective-permute-start | bytes 3145736 | tf_op jit(solution)/shard_map/ppermute | solution.py:279
  54.1 22.5 %collective-permute-start.18 = (bf16[256,2048]{1,0:T(8,128)(2,1)S(1)}, bf16[256,2048]{1,0:T(8,128)(2,1)S(1)}, u32[]{:S(2)}, u32[]{:S(2)}) collective-permute-start(bf16[256,2048]{1,0:T(8,128)(2,1)S(1)} %collective-permute-done.7.refs_0_), channel_id=1, source_target_pairs={{0,48},{8,72},{16,32},{24,88},{32,16},{40,104},{48,0},{56,120},{64... | collective-permute-start | bytes 3145736 | tf_op jit(solution)/shard_map/ppermute | solution.py:279
  65.3 14.9 %collective-permute-start.17 = (bf16[256,2048]{1,0:T(8,128)(2,1)S(1)}, bf16[256,2048]{1,0:T(8,128)(2,1)S(1)}, u32[]{:S(2)}, u32[]{:S(2)}) collective-permute-start(bf16[256,2048]{1,0:T(8,128)(2,1)S(1)} %collective-permute-done.16.refs_2_), channel_id=1, source_target_pairs={{0,16},{8,200},{16,0},{24,216},{32,48},{40,232},{48,32},{56,248},{... | collective-permute-start | bytes 3145736 | tf_op jit(solution)/shard_map/ppermute | solution.py:279
  66.6 18.3 %collective-permute-start.19 = (bf16[8,4,2,64,128]{4,3,2,1,0:T(8,128)(2,1)S(1)}, bf16[8,4,2,64,128]{4,3,2,1,0:T(8,128)(2,1)S(1)}, u32[]{:S(2)}, u32[]{:S(2)}) collective-permute-start(bf16[8,4,2,64,128]{4,3,2,1,0:T(8,128)(2,1)S(1)} %get-tuple-element.59), channel_id=1, source_target_pairs={{0,8},{8,0},{1,9},{9,1},{2,10},{10,2},{3,11},{11,3},{4,12},{12,4},... | collective-permute-start | bytes 3145736 | tf_op jit(solution)/shard_map/ppermute | solution.py:283
  73.8 11.1 %collective-permute-start.21 = (bf16[8,4,2,64,128]{4,3,2,1,0:T(8,128)(2,1)S(1)}, bf16[8,4,2,64,128]{4,3,2,1,0:T(8,128)(2,1)S(1)}, u32[]{:S(2)}, u32[]{:S(2)}) collective-permute-start(bf16[8,4,2,64,128]{4,3,2,1,0:T(8,128)(2,1)S(1)} %get-tuple-element.61), channel_id=1, source_target_pairs={{0,8},{8,0},{1,9},{9,1},{2,10},{10,2},{3,11},{11,3},{4,12},{12,4},... | collective-permute-start | bytes 3145736 | tf_op jit(solution)/shard_map/ppermute | solution.py:283
  76.6 8.3 %collective-permute-start.20 = (bf16[8,4,2,64,128]{4,3,2,1,0:T(8,128)(2,1)S(1)}, bf16[8,4,2,64,128]{4,3,2,1,0:T(8,128)(2,1)S(1)}, u32[]{:S(2)}, u32[]{:S(2)}) collective-permute-start(bf16[8,4,2,64,128]{4,3,2,1,0:T(8,128)(2,1)S(1)} %get-tuple-element.60), channel_id=1, source_target_pairs={{0,8},{8,0},{1,9},{9,1},{2,10},{10,2},{3,11},{11,3},{4,12},{12,4},... | collective-permute-start | bytes 3145736 | tf_op jit(solution)/shard_map/ppermute | solution.py:283
  82.5 2.7 %collective-permute-start.22 = (bf16[8,4,2,64,128]{4,3,2,1,0:T(8,128)(2,1)S(1)}, bf16[8,4,2,64,128]{4,3,2,1,0:T(8,128)(2,1)S(1)}, u32[]{:S(2)}, u32[]{:S(2)}) collective-permute-start(bf16[8,4,2,64,128]{4,3,2,1,0:T(8,128)(2,1)S(1)} %block.7), channel_id=1, source_target_pairs={{0,8},{8,0},{1,9},{9,1},{2,10},{10,2},{3,11},{11,3},{4,12},{12,4},... | collective-permute-start | bytes 3145736 | tf_op jit(solution)/shard_map/ppermute | solution.py:283
